TPU v7x, 32 devices: a whole 2x2x4 slice. The times are simulated.
32 devices in a mesh: gz: 4 (over x, core), ty: 2 (over y), tx: 4 (over z).
Axes of the slice: x: 2, y: 2, z: 4, core: 2. Of those that a mesh axis runs over, the one named last changes fastest.
Arguments:
- images: bfloat16 [4, 1024, 2048], P('gz', 'ty', 'tx'), may hold values from -40 to 40, as said below
- boundary: bfloat16 [1024, 2048], P('ty', 'tx'), may hold values from -40 to 40, as said below
- anchor: float32 [4, 256, 512], P('gz', 'ty', 'tx'), may hold values from 0.02 to 0.5
Outputs:
- mesh_shift: float32 [4, 2, 256, 512], P('gz', None, 'ty', 'tx')
- drift: float32 [4, 2, 4, 2, 128], P('gz', 'ty', 'tx')
Inputs may be any that keep to these rules, and one draw needn't show every extreme that they name: `images`: pixel intensities. `boundary`: pixel intensities.
All inputs are finite; a program needn't handle non-finite values.
Results may differ from a plain program's by a relative error of at most 0.0003.
Values may be sent and summed in bfloat16 or wider, within the bound.
No kernel may reach another device: no remote copies, remote signals or barrier semaphores. Data moves between devices by JAX's collectives and lax.ppermute only.
A program may use at most 64 MiB of HBM per device.

v0:
```python
import math

import jax
import jax.numpy as jnp
import numpy as np
from jax import lax
from jax.experimental import pallas as pl
from jax.experimental.pallas import tpu as pltpu
from jax.sharding import PartitionSpec as P

PATCH = 128
STRIDE = 4
SWEEPS = 32
HALF = PATCH // 2
BF16 = jnp.bfloat16
F32 = jnp.float32


def split_table(table):
    high = table.astype(BF16)
    low = (table - high.astype(np.float64)).astype(BF16)
    return (high, low)


def transform_tables():
    counter = np.arange(PATCH)
    phase = (counter[:, None] * counter[None, :] % PATCH) * (2.0 * math.pi / PATCH)
    basis = np.concatenate([np.cos(phase[:HALF]), np.sin(phase[:HALF])])
    basis[HALF] = np.cos(phase[HALF])
    gains = np.full(PATCH, 2.0)
    gains[0] = gains[HALF] = 1.0
    inverse = basis.T * gains / PATCH
    forward_pair = np.zeros((2, PATCH, 2, 2, HALF))
    inverse_pair = np.zeros((2, 2, HALF, 2, PATCH))
    for side in range(2):
        forward_pair[side, :, :, side] = basis.T.reshape(PATCH, 2, HALF)
        inverse_pair[:, side, :, side] = inverse.T.reshape(2, HALF, PATCH)
    forward_pair = forward_pair.reshape(2 * PATCH, 2 * PATCH)
    inverse_pair = inverse_pair.reshape(2 * PATCH, 2 * PATCH)
    right_high, right_low = split_table(forward_pair)
    back_high, back_low = split_table(inverse_pair)
    left_high, left_low = split_table(basis)
    undo_high, undo_low = split_table(inverse / PATCH)
    rights = np.stack([right_high, right_low, back_high, back_low])
    lefts = np.stack(
        [
            np.concatenate([left_high, left_high, left_low], axis=1),
            np.concatenate([undo_high, undo_high, undo_low], axis=1),
        ]
    )
    return (rights, lefts)


def halves(value):
    high = value.astype(BF16)
    return (high, (value - high.astype(F32)).astype(BF16))


def dot(left, right):
    return jnp.dot(left, right, preferred_element_type=F32)


def left_transform(table, value):
    high, low = halves(value)
    return dot(table, jnp.concatenate([high, low, high], axis=0))


def quarters(spec):
    return (
        (spec[:HALF, :PATCH], spec[:HALF, PATCH:]),
        (spec[HALF:, :PATCH], spec[HALF:, PATCH:]),
    )


def cross_operand(spec):
    (cc, cs), (sc, ss) = quarters(spec)
    first_row = lax.broadcasted_iota(jnp.int32, (HALF, PATCH), 0) == 0
    first_lane = lax.broadcasted_iota(jnp.int32, (HALF, PATCH), 1) % HALF == 0

    def lanes(cosine, sine):
        return (cosine, jnp.where(first_lane, sine, cosine), jnp.where(first_lane, 0.0, sine))

    return (
        lanes(cc, cs),
        lanes(jnp.where(first_row, sc, cc), jnp.where(first_row, ss, cs)),
        lanes(jnp.where(first_row, 0.0, sc), jnp.where(first_row, 0.0, ss)),
    )


def cross(operand, spec):
    (row_c, row_d, row_s) = operand
    (bc, bs) = quarters(spec)

    def cosine(a, b):
        return a[0] * b[0] + a[2] * b[1]

    def sine(a, b):
        return a[1] * b[1] - a[2] * b[0]

    cc = cosine(row_c, bc) + cosine(row_s, bs)
    cs = sine(row_c, bc) + sine(row_s, bs)
    sc = cosine(row_d, bs) - cosine(row_s, bc)
    ss = sine(row_d, bs) - sine(row_s, bc)
    return jnp.concatenate(
        [jnp.concatenate([cc, cs], axis=1), jnp.concatenate([sc, ss], axis=1)], axis=0
    )


def flows_kernel(prior_ref, own_ref, later_ref, rights_ref, lefts_ref, out_ref, stats_ref):
    rows, cols = own_ref.shape
    per_row = cols // (2 * PATCH)
    blocks = rows // PATCH * per_row
    patches = 2 * blocks

    def block_step(block, carry):
        row = pl.multiple_of(block // per_row * PATCH, PATCH)
        col = pl.multiple_of(block % per_row * (2 * PATCH), 2 * PATCH)
        window = (pl.ds(row, PATCH), pl.ds(col, 2 * PATCH))
        pixels = jnp.concatenate([ref[window] for ref in (prior_ref, own_ref, later_ref)], axis=0)
        right = dot(pixels, rights_ref[0]) + dot(pixels, rights_ref[1])
        wide = jnp.concatenate([right[:PATCH], right[PATCH : 2 * PATCH], right[2 * PATCH :]], axis=1)
        spec = left_transform(lefts_ref[0], wide)
        prior, own, later = (spec[:, i * 2 * PATCH : (i + 1) * 2 * PATCH] for i in range(3))
        operand = cross_operand(prior)
        products = jnp.concatenate([cross(operand, own), cross(operand, later)], axis=0)
        high, low = halves(products)
        back = dot(high, rights_ref[2]) + dot(low, rights_ref[2]) + dot(high, rights_ref[3])
        back = jnp.concatenate([back[:PATCH], back[PATCH:]], axis=1)
        scores = left_transform(lefts_ref[1], back)
        groups = scores.reshape(PATCH // 8, 8, 4 * PATCH)
        peak = jnp.max(groups, axis=0)
        total = jnp.zeros_like(peak)
        moment = jnp.zeros_like(peak)
        for group in range(PATCH // 8):
            weight = jnp.exp(groups[group] - peak)
            shift = 8 * group - (PATCH if group >= PATCH // 16 else 0)
            total = total + weight
            moment = moment + float(shift) * weight
        for pair in range(2):
            for side in range(2):
                lanes = slice((2 * pair + side) * PATCH, (2 * pair + side + 1) * PATCH)
                slot = pair * patches + 2 * block + side
                stats_ref[0, slot] = peak[:, lanes]
                stats_ref[1, slot] = total[:, lanes]
                stats_ref[2, slot] = moment[:, lanes]
        return carry

    lax.fori_loop(0, blocks, block_step, 0)
    peak = stats_ref[0]
    best = jnp.max(jnp.max(peak, axis=1, keepdims=True), axis=2, keepdims=True)
    scale = jnp.exp(peak - best)
    total = scale * stats_ref[1]
    within = lax.broadcasted_iota(jnp.int32, peak.shape, 1).astype(F32)
    moment = scale * stats_ref[2] + within * total
    total = jnp.sum(total, axis=1)
    lane = lax.broadcasted_iota(jnp.int32, total.shape, 1)
    signed = jnp.where(lane < HALF, lane, lane - PATCH).astype(F32)
    mass = jnp.sum(total, axis=1, keepdims=True) * STRIDE
    along_rows = jnp.sum(jnp.sum(moment, axis=1), axis=1, keepdims=True) / mass
    along_cols = jnp.sum(total * signed, axis=1, keepdims=True) / mass
    lane = lax.broadcasted_iota(jnp.int32, out_ref.shape, 1)
    near_rows, near_cols = along_rows[:patches], along_cols[:patches]
    out = jnp.where(lane == 0, near_rows, near_cols)
    out = jnp.where(lane == 2, along_rows[patches:] - near_rows, out)
    out_ref[...] = jnp.where(lane == 3, along_cols[patches:] - near_cols, out)


def flows(prior, own, later):
    rights, lefts = transform_tables()
    patches = own.shape[0] // PATCH * (own.shape[1] // PATCH)
    return pl.pallas_call(
        flows_kernel,
        out_shape=jax.ShapeDtypeStruct((patches, PATCH), F32),
        scratch_shapes=[pltpu.VMEM((3, 2 * patches, 8, PATCH), F32)],
        compiler_params=pltpu.CompilerParams(vmem_limit_bytes=32 * 2**20),
        name="flows",
    )(prior, own, later, jnp.asarray(rights), jnp.asarray(lefts))


def spread_weights(nodes, patches):
    node_pos = (np.arange(nodes) + 0.5) * STRIDE / PATCH - 0.5
    weights = np.maximum(0.0, 1.0 - np.abs(node_pos[:, None] - np.arange(patches)[None, :]))
    return weights / weights.sum(axis=1, keepdims=True)


def ring_tables(nodes, patches):
    span = np.arange(nodes + 2 * SWEEPS) - SWEEPS
    lane_node = np.concatenate([span[SWEEPS:], span, span[:SWEEPS]])
    spread = spread_weights(nodes, patches)

    def wide(positions):
        table = np.zeros((len(positions), 3, patches))
        for tile in range(3):
            at = positions - (tile - 1) * nodes
            hit = (at >= 0) & (at < nodes)
            table[hit, tile] = spread[at[hit]]
        return table

    shape = (3, 3, patches, patches)
    rows = wide(span)[:, None, :, :, None]
    cols = wide(lane_node).transpose(1, 2, 0)[:, None, None]
    left = np.broadcast_to(rows, (len(span),) + shape).reshape(len(span), -1)
    right = np.broadcast_to(cols, shape + (len(lane_node),)).reshape(-1, len(lane_node))
    return (left.astype(BF16), right.astype(np.float32), lane_node.astype(np.int32)[None])


def relax_kernel(
    place_ref, own_ref, even_ref, odd_ref, anchor_ref, even_anchor_ref, odd_anchor_ref,
    left_ref, right_ref, lane_node_ref, mesh_ref, profile_ref, work_ref, gain_ref, base_ref,
):
    rows, lanes = work_ref.shape
    nodes = mesh_ref.shape[1]
    turn = nodes // 2
    at_even = place_ref[2] == 1

    def beside(even, odd):
        return (jnp.where(at_even, odd, even), jnp.where(at_even, even, odd))

    before, after = beside(even_ref[...], odd_ref[...])
    sources = jnp.concatenate([before, own_ref[...], after], axis=0)
    first = lax.broadcasted_iota(jnp.int32, (1, lanes), 1)
    second = (first >= nodes + SWEEPS) & (first < lanes - SWEEPS)
    spread = jnp.where(second, sources[:, 1:2], sources[:, 0:1]) * right_ref[...]
    target = jnp.zeros((rows, lanes), F32)
    for piece in range(3):
        part = spread.astype(BF16)
        target = target + dot(left_ref[...], part)
        spread = spread - part.astype(F32)
    own = anchor_ref[...]
    before, after = beside(even_anchor_ref[...], odd_anchor_ref[...])
    lane = lax.broadcasted_iota(jnp.int32, own.shape, 1)
    turned = pltpu.roll(own, turn, 1)
    middle = jnp.where(lane < turn, jnp.where(lane < SWEEPS, after, pltpu.roll(before, turn, 1)), turned)
    last = jnp.where(lane < turn, turned, jnp.where(lane < turn + SWEEPS, pltpu.roll(after, turn, 1), before))
    weight = jnp.concatenate([own, middle, last], axis=1)
    row_node = lax.broadcasted_iota(jnp.int32, (rows, lanes), 0) - SWEEPS + place_ref[0]
    col_node = lane_node_ref[...] + place_ref[1]
    inside = (row_node >= 0) & (row_node < place_ref[3]) & (col_node >= 0) & (col_node < place_ref[4])
    gain = jnp.where(inside, 1.0 / (4.0 + weight), 0.0)
    gain_ref[...] = gain
    base_ref[...] = gain * weight * target
    work_ref[...] = jnp.where(inside, target, 0.0)
    group = 8
    for step in range(SWEEPS // group):
        window = slice(step * group, rows - step * group)
        count = rows - 2 * step * group

        def sweep(counter, carry):
            mesh = work_ref[window]
            around = pltpu.roll(mesh, 1, 0) + pltpu.roll(mesh, count - 1, 0)
            around = around + pltpu.roll(mesh, 1, 1) + pltpu.roll(mesh, lanes - 1, 1)
            work_ref[window] = gain_ref[window] * around + base_ref[window]
            return carry

        lax.fori_loop(0, group, sweep, 0)
    final = work_ref[SWEEPS : SWEEPS + nodes]
    down = final[:, :nodes]
    tail = pltpu.roll(final[:, nodes:], turn, 1)
    across = tail[:, nodes:]
    mesh_ref[0] = down
    mesh_ref[1] = across
    share = 1.0 / nodes
    down_mean = jnp.sum(jnp.transpose(down), axis=0, keepdims=True) * share
    across_mean = jnp.sum(across, axis=0, keepdims=True) * share
    row = lax.broadcasted_iota(jnp.int32, profile_ref.shape, 0)
    ramp = lax.broadcasted_iota(jnp.int32, profile_ref.shape, 1).astype(F32)
    profile = jnp.where(row == 0, down_mean, across_mean)
    profile_ref[...] = jnp.clip(ramp + profile, 0.0, nodes - 1.0)


def relax(place, targets, anchors, nodes, patches):
    left, right, lane_node = ring_tables(nodes, patches)
    rows, lanes = left.shape[0], right.shape[1]
    vmem = pl.BlockSpec(memory_space=pltpu.VMEM)
    return pl.pallas_call(
        relax_kernel,
        out_shape=(
            jax.ShapeDtypeStruct((2, nodes, nodes), F32),
            jax.ShapeDtypeStruct((8, nodes), F32),
        ),
        in_specs=[pl.BlockSpec(memory_space=pltpu.SMEM)] + [vmem] * 9,
        out_specs=(vmem, vmem),
        scratch_shapes=[pltpu.VMEM((rows, lanes), F32)] * 3,
        compiler_params=pltpu.CompilerParams(vmem_limit_bytes=32 * 2**20),
        name="relax",
    )(place, *targets, *anchors, jnp.asarray(left), jnp.asarray(right), jnp.asarray(lane_node))


def compose_kernel(place_ref, landings_ref, out_ref):
    count = landings_ref.shape[0]
    nodes = landings_ref.shape[2]
    ramp = lax.broadcasted_iota(jnp.int32, out_ref.shape, 1).astype(F32)
    value = landings_ref[count - 1]
    for section in range(count - 2, -1, -1):
        landing = landings_ref[section]
        floor = jnp.minimum(jnp.floor(landing), nodes - 2.0)
        index = floor.astype(jnp.int32)
        share = landing - floor
        below = jnp.take_along_axis(value, index, axis=1)
        above = jnp.take_along_axis(value, index + 1, axis=1)
        joined = (1.0 - share) * below + share * above
        value = jnp.where(place_ref[5] > section, joined, landing)
    out_ref[...] = value - ramp


def compose(place, landings):
    vmem = pl.BlockSpec(memory_space=pltpu.VMEM)
    return pl.pallas_call(
        compose_kernel,
        out_shape=jax.ShapeDtypeStruct(landings.shape[1:], F32),
        in_specs=[pl.BlockSpec(memory_space=pltpu.SMEM), vmem],
        out_specs=vmem,
        name="compose",
    )(place, landings)


def swap_pairs(value, axis, first, spare):
    count, other = lax.axis_size(axis), lax.axis_size(spare)
    axes = ("gz", "ty", "tx")
    flip = axes.index(axis) > axes.index(spare)

    def place(here, beside):
        return beside * count + here if flip else here * other + beside

    moves = []
    for here in range(count):
        there = ((here + first) ^ 1) - first
        for beside in range(other):
            target = place(there, beside) if 0 <= there < count else place(here, beside ^ 1)
            moves.append((place(here, beside), target))
    return lax.ppermute(value, (spare, axis) if flip else (axis, spare), moves)


def local(images, boundary, anchor):
    nodes = anchor.shape[1]
    own = images[0]
    patches = own.shape[0] // PATCH
    section, ty, tx = (lax.axis_index(axis) for axis in ("gz", "ty", "tx"))
    sections = lax.axis_size("gz")
    n_ty, n_tx = lax.axis_size("ty"), lax.axis_size("tx")
    place = jnp.stack(
        [ty * nodes, tx * nodes, 1 - tx % 2, n_ty * nodes, n_tx * nodes, section]
    ).astype(jnp.int32)
    even = section % 2 == 0
    chip = swap_pairs(own, "gz", 0, "ty")
    far = swap_pairs(own, "gz", 1, "ty")
    prior = jnp.where(even, jnp.where(section == 0, boundary, far), chip)
    later = jnp.where(even, chip, far)
    up, down = rows_beside(anchor[0])
    rows = jnp.concatenate([up[nodes - SWEEPS :], anchor[0], down[:SWEEPS]], axis=0)
    anchors = (rows, swap_pairs(rows, "tx", 0, "gz"), swap_pairs(rows, "tx", 1, "gz"))
    flow = flows(prior, own, later)
    turn = [(i, (i + 1) % sections) for i in range(sections)]
    up, down = rows_beside(flow)
    before = lax.ppermute(flow, "gz", turn)
    flow = jnp.concatenate([up, flow, down], axis=0)
    up, down = rows_beside(before)
    before = jnp.concatenate([up, before, down], axis=0)
    column = jnp.where(section <= 1, flow[:, 0:2], 0.5 * (flow[:, 0:2] + before[:, 2:4]))
    column = jnp.pad(column, ((0, 0), (0, PATCH - 2)))
    targets = (column, swap_pairs(column, "tx", 0, "gz"), swap_pairs(column, "tx", 1, "gz"))
    mesh, landing = relax(place, targets, anchors, nodes, patches)
    landings = lax.all_gather(landing, "gz", axis=0)
    drift = compose(place, landings)
    return (mesh[None], drift[:2].reshape(1, 1, 1, 2, nodes))


def rows_beside(value):
    count = lax.axis_size("ty")
    if count == 2:
        other = swap_pairs(value, "ty", 0, "gz")
        return (other, other)
    even = swap_pairs(value, "ty", 0, "gz")
    odd = swap_pairs(value, "ty", 1, "gz")
    at_even = lax.axis_index("ty") % 2 == 0
    return (jnp.where(at_even, odd, even), jnp.where(at_even, even, odd))


def solution(mesh):
    return jax.shard_map(
        local,
        mesh=mesh,
        in_specs=(P("gz", "ty", "tx"), P("ty", "tx"), P("gz", "ty", "tx")),
        out_specs=(P("gz", None, "ty", "tx"), P("gz", "ty", "tx", None, None)),
        check_vma=False,
    )
```

profile of v0, /device:TPU:0, one launch (start us, length us, event | category | flops | bytes accessed | tf_op | source)
XLA Modules:
  0.0 51.4 jit_solution(8537935114301469624)
XLA Ops:
  0.6 3.0 %collective-permute-start = (bf16[512,512]{1,0:T(8,128)(2,1)}, bf16[512,512]{1,0:T(8,128)(2,1)S(1)}, u32[]{:S(2)}, u32[]{:S(2)}) collective-permute-start(bf16[512,512]{1,0:T(8,128)(2,1)} %bitcast.10), channel_id=1, source_target_pairs={{0,4},{4,0},{8,16},{12,20},{16,8},{20,12},{24,28},{28,24},{1,5},{5... | collective-permute-start | bytes 1572872 | tf_op jit(solution)/shard_map/ppermute | solution.py:331
  3.7 0.1 collective-permute-start.1
  3.7 1.5 %collective-permute-start.7 = (f32[128,128]{1,0:T(8,128)}, f32[128,128]{1,0:T(8,128)S(1)}, u32[]{:S(2)}, u32[]{:S(2)}) collective-permute-start(f32[128,128]{1,0:T(8,128)} %bitcast.13), channel_id=1, source_target_pairs={{0,4},{8,12},{16,20},{24,28},{4,0},{12,8},{20,16},{28,24},{1,5},{9... | collective-permute-start | bytes 196616 | tf_op jit(solution)/shard_map/ppermute | solution.py:331
  5.3 6.5 %collective-permute-done = bf16[512,512]{1,0:T(8,128)(2,1)S(1)} collective-permute-done((bf16[512,512]{1,0:T(8,128)(2,1)}, bf16[512,512]{1,0:T(8,128)(2,1)S(1)}, u32[]{:S(2)}, u32[]{:S(2)}) %collective-permute-start) | collective-permute-done | bytes 524320 | tf_op jit(solution)/shard_map/ppermute | solution.py:331
  11.7 0.0 collective-permute-done.1
  11.7 1.2 %broadcast_select_fusion = (bf16[512,512]{1,0:T(8,128)(2,1)S(1)}, bf16[512,512]{1,0:T(8,128)(2,1)S(1)}) fusion(bf16[512,512]{1,0:T(8,128)(2,1)S(1)} %collective-permute-done.1, bf16[512,512]{1,0:T(8,128)(2,1)S(1)} %collective-permute-done, pred[]{:T(512)S(6)} %eq.9, bf16[512,512]{1,0:T(8,128)(2,1)} %param.9, pred[]{:T(512)S(6)} %eq.10), kind=kLoop, calls=%fused_computation.1 | loop fusion | flops 786432 | bytes 2621442 | tf_op jit(solution)/shard_map/jit(_where)/select_n | solution.py:348
  12.9 0.0 copy-start.7
  12.9 9.4 %flows.1 = f32[16,128]{1,0:T(8,128)S(1)} custom-call(bf16[512,512]{1,0:T(8,128)(2,1)S(1)} %get-tuple-element.7.prior_ref, bf16[512,512]{1,0:T(8,128)(2,1)S(1)} %bitcast.12, bf16[512,512]{1,0:T(8,128)(2,1)S(1)} %get-tuple-element.6.later_ref, bf16[4,256,256]{2,1,0:T(8,128)(2,1)S(1)} %copy-done.1, bf16[2,128,384]{2,1,0:T(8,128)(2,1)S(1)} %copy-done.3), custom_call_target="tpu_custom_call" | custom-call | tf_op jit(solution)/shard_map/flows/pallas_call | solution.py:171
  22.4 0.0 copy-start.2
  22.4 0.1 collective-permute-start.3
  22.5 0.0 collective-permute-done.7
  22.5 2.1 %collective-permute-start.2 = (f32[16,128]{1,0:T(8,128)S(1)}, f32[16,128]{1,0:T(8,128)S(1)}, u32[]{:S(2)}, u32[]{:S(2)}) collective-permute-start(f32[16,128]{1,0:T(8,128)S(1)} %flows.1), channel_id=1, source_target_pairs={{0,4},{8,12},{16,20},{24,28},{4,0},{12,8},{20,16},{28,24},{1,5},{9... | collective-permute-start | bytes 24584 | tf_op jit(solution)/shard_map/ppermute | solution.py:331
  24.6 1.0 %collective-permute-done.3 = f32[16,128]{1,0:T(8,128)S(1)} collective-permute-done((f32[16,128]{1,0:T(8,128)S(1)}, f32[16,128]{1,0:T(8,128)S(1)}, u32[]{:S(2)}, u32[]{:S(2)}) %collective-permute-start.3) | collective-permute-done | bytes 8224 | tf_op jit(solution)/shard_map/ppermute | solution.py:355
  25.5 2.0 %collective-permute-start.4 = (f32[16,128]{1,0:T(8,128)S(1)}, f32[16,128]{1,0:T(8,128)S(1)}, u32[]{:S(2)}, u32[]{:S(2)}) collective-permute-start(f32[16,128]{1,0:T(8,128)S(1)} %collective-permute-done.3), channel_id=1, source_target_pairs={{0,4},{8,12},{16,20},{24,28},{4,0},{12,8},{20,16},{28,24},{1,5},{9... | collective-permute-start | bytes 24584 | tf_op jit(solution)/shard_map/ppermute | solution.py:331
  27.6 0.0 copy-start.4
  27.6 1.6 %collective-permute-start.8 = (f32[192,128]{1,0:T(8,128)S(1)}, f32[192,128]{1,0:T(8,128)S(1)}, u32[]{:S(2)}, u32[]{:S(2)}) collective-permute-start(f32[192,128]{1,0:T(8,128)S(1)} %pad_maximum_fusion.anchor_ref), channel_id=1, source_target_pairs={{0,1},{8,9},{16,17},{24,25},{1,0},{9,8},{17,16},{25,24},{2,3},{10,... | collective-permute-start | bytes 294920 | tf_op jit(solution)/shard_map/ppermute | solution.py:331
  29.2 0.1 fusion.2
  29.3 3.2 %collective-permute-start.5 = (f32[48,128]{1,0:T(8,128)S(1)}, f32[48,128]{1,0:T(8,128)S(1)}, u32[]{:S(2)}, u32[]{:S(2)}) collective-permute-start(f32[48,128]{1,0:T(8,128)S(1)} %pad.4.own_ref), channel_id=1, source_target_pairs={{0,1},{8,9},{16,17},{24,25},{1,0},{9,8},{17,16},{25,24},{2,3},{10,... | collective-permute-start | bytes 73736 | tf_op jit(solution)/shard_map/ppermute | solution.py:331
  32.5 0.1 stack.19.place_ref
  32.6 1.7 %collective-permute-done.5.even_ref = f32[48,128]{1,0:T(8,128)S(1)} collective-permute-done((f32[48,128]{1,0:T(8,128)S(1)}, f32[48,128]{1,0:T(8,128)S(1)}, u32[]{:S(2)}, u32[]{:S(2)}) %collective-permute-start.5) | collective-permute-done | bytes 24608 | tf_op jit(solution)/shard_map/ppermute | solution.py:331
  34.3 8.7 %relax.1 = (f32[2,128,128]{2,1,0:T(8,128)}, f32[8,128]{1,0:T(8,128)S(1)}) custom-call(s32[6]{0:T(128)S(1)} %stack.19.place_ref, f32[48,128]{1,0:T(8,128)S(1)} %pad.4.own_ref, f32[48,128]{1,0:T(8,128)S(1)} %collective-permute-done.5.even_ref, f32[48,128]{1,0:T(8,128)S(1)} %collective-permute-done.6.odd_ref, f32[192,128]{1,0:T(8,128)S(1)} %pad_maximum_fusion.anchor_ref, ...), custom_call_target="tpu_custom_call" | custom-call | tf_op jit(solution)/shard_map/relax/pallas_call | solution.py:275
  43.1 5.6 %all-gather = f32[32,128]{1,0:T(8,128)} all-gather(f32[8,128]{1,0:T(8,128)S(1)} %get-tuple-element.5), channel_id=2, replica_groups=mesh['gz'=4,'ty'=2,'tx'=4] {'gz'}, dimensions={0}, use_global_device_ids=true | all-gather | bytes 20480 | tf_op jit(solution)/shard_map/all_gather | solution.py:363
  48.7 1.5 %compose.1 = f32[8,128]{1,0:T(8,128)} custom-call(s32[6]{0:T(128)} %copy-done.5, f32[4,8,128]{2,1,0:T(8,128)} %bitcast.15), custom_call_target="tpu_custom_call" | custom-call | tf_op jit(solution)/shard_map/compose/pallas_call | solution.py:308
  50.2 1.2 %slice_bitcast_fusion = f32[1,1,1,2,128]{4,3,2,1,0:T(2,128)} fusion(f32[8,128]{1,0:T(8,128)} %compose.1), kind=kLoop, calls=%fused_computation.10 | loop fusion | bytes 2048 | tf_op jit(solution)/shard_map/reshape | solution.py:365
  (23 shorter events, 0.1 us)
Async XLA Ops:
  0.6 11.1 %collective-permute-start = (bf16[512,512]{1,0:T(8,128)(2,1)}, bf16[512,512]{1,0:T(8,128)(2,1)S(1)}, u32[]{:S(2)}, u32[]{:S(2)}) collective-permute-start(bf16[512,512]{1,0:T(8,128)(2,1)} %bitcast.10), channel_id=1, source_target_pairs={{0,4},{4,0},{8,16},{12,20},{16,8},{20,12},{24,28},{28,24},{1,5},{5... | collective-permute-start | bytes 1572872 | tf_op jit(solution)/shard_map/ppermute | solution.py:331
  3.7 8.1 %collective-permute-start.1 = (bf16[512,512]{1,0:T(8,128)(2,1)}, bf16[512,512]{1,0:T(8,128)(2,1)S(1)}, u32[]{:S(2)}, u32[]{:S(2)}) collective-permute-start(bf16[512,512]{1,0:T(8,128)(2,1)} %bitcast.11), channel_id=1, source_target_pairs={{0,8},{4,12},{8,0},{12,4},{16,24},{20,28},{24,16},{28,20},{1,9},{5... | collective-permute-start | bytes 1572872 | tf_op jit(solution)/shard_map/ppermute | solution.py:331
  3.7 18.7 %collective-permute-start.7 = (f32[128,128]{1,0:T(8,128)}, f32[128,128]{1,0:T(8,128)S(1)}, u32[]{:S(2)}, u32[]{:S(2)}) collective-permute-start(f32[128,128]{1,0:T(8,128)} %bitcast.13), channel_id=1, source_target_pairs={{0,4},{8,12},{16,20},{24,28},{4,0},{12,8},{20,16},{28,24},{1,5},{9... | collective-permute-start | bytes 196616 | tf_op jit(solution)/shard_map/ppermute | solution.py:331
  5.3 7.6 %copy-start = (bf16[1,512,512]{2,1,0:T(8,128)(2,1)S(1)}, bf16[1,512,512]{2,1,0:T(8,128)(2,1)}, u32[]{:S(2)}) copy-start(bf16[1,512,512]{2,1,0:T(8,128)(2,1)} %param.8) | copy-start | bytes 1572868
  5.3 7.6 %copy-start.1 = (bf16[4,256,256]{2,1,0:T(8,128)(2,1)S(1)}, bf16[4,256,256]{2,1,0:T(8,128)(2,1)}, u32[]{:S(2)}) copy-start(bf16[4,256,256]{2,1,0:T(8,128)(2,1)} %constant.51.clone.rights_ref) | copy-start | bytes 1572868
  5.3 7.7 %copy-start.3 = (bf16[2,128,384]{2,1,0:T(8,128)(2,1)S(1)}, bf16[2,128,384]{2,1,0:T(8,128)(2,1)}, u32[]{:S(2)}) copy-start(bf16[2,128,384]{2,1,0:T(8,128)(2,1)} %constant.52.clone.lefts_ref) | copy-start | bytes 589828
  12.9 14.6 %copy-start.7 = (f32[1,128,128]{2,1,0:T(8,128)S(1)}, f32[1,128,128]{2,1,0:T(8,128)}, u32[]{:S(2)}) copy-start(f32[1,128,128]{2,1,0:T(8,128)} %param.10) | copy-start | bytes 196612
  22.4 12.0 %copy-start.2 = (f32[144,384]{1,0:T(8,128)S(1)}, f32[144,384]{1,0:T(8,128)}, u32[]{:S(2)}) copy-start(f32[144,384]{1,0:T(8,128)} %constant.54.clone.right_ref) | copy-start | bytes 663556
  22.4 3.1 %collective-permute-start.3 = (f32[16,128]{1,0:T(8,128)S(1)}, f32[16,128]{1,0:T(8,128)S(1)}, u32[]{:S(2)}, u32[]{:S(2)}) collective-permute-start(f32[16,128]{1,0:T(8,128)S(1)} %flows.1), channel_id=1, source_target_pairs={{0,8},{8,16},{16,24},{24,0},{1,9},{9,17},{17,25},{25,1},{2,10},{10... | collective-permute-start | bytes 24584 | tf_op jit(solution)/shard_map/ppermute | solution.py:355
  22.5 6.7 %collective-permute-start.2 = (f32[16,128]{1,0:T(8,128)S(1)}, f32[16,128]{1,0:T(8,128)S(1)}, u32[]{:S(2)}, u32[]{:S(2)}) collective-permute-start(f32[16,128]{1,0:T(8,128)S(1)} %flows.1), channel_id=1, source_target_pairs={{0,4},{8,12},{16,20},{24,28},{4,0},{12,8},{20,16},{28,24},{1,5},{9... | collective-permute-start | bytes 24584 | tf_op jit(solution)/shard_map/ppermute | solution.py:331
  25.5 3.7 %collective-permute-start.4 = (f32[16,128]{1,0:T(8,128)S(1)}, f32[16,128]{1,0:T(8,128)S(1)}, u32[]{:S(2)}, u32[]{:S(2)}) collective-permute-start(f32[16,128]{1,0:T(8,128)S(1)} %collective-permute-done.3), channel_id=1, source_target_pairs={{0,4},{8,12},{16,20},{24,28},{4,0},{12,8},{20,16},{28,24},{1,5},{9... | collective-permute-start | bytes 24584 | tf_op jit(solution)/shard_map/ppermute | solution.py:331
  27.6 6.8 %copy-start.4 = (bf16[192,144]{1,0:T(8,128)(2,1)S(1)}, bf16[192,144]{1,0:T(8,128)(2,1)}, u32[]{:S(2)}) copy-start(bf16[192,144]{1,0:T(8,128)(2,1)} %constant.53.clone.left_ref) | copy-start | bytes 165892
  27.6 5.0 %collective-permute-start.8 = (f32[192,128]{1,0:T(8,128)S(1)}, f32[192,128]{1,0:T(8,128)S(1)}, u32[]{:S(2)}, u32[]{:S(2)}) collective-permute-start(f32[192,128]{1,0:T(8,128)S(1)} %pad_maximum_fusion.anchor_ref), channel_id=1, source_target_pairs={{0,1},{8,9},{16,17},{24,25},{1,0},{9,8},{17,16},{25,24},{2,3},{10,... | collective-permute-start | bytes 294920 | tf_op jit(solution)/shard_map/ppermute | solution.py:331
  29.2 3.4 %collective-permute-start.9 = (f32[192,128]{1,0:T(8,128)S(1)}, f32[192,128]{1,0:T(8,128)S(1)}, u32[]{:S(2)}, u32[]{:S(2)}) collective-permute-start(f32[192,128]{1,0:T(8,128)S(1)} %pad_maximum_fusion.anchor_ref), channel_id=1, source_target_pairs={{0,8},{8,0},{16,24},{24,16},{1,2},{9,10},{17,18},{25,26},{2,1},{10... | collective-permute-start | bytes 294920 | tf_op jit(solution)/shard_map/ppermute | solution.py:331
  29.3 5.0 %collective-permute-start.5 = (f32[48,128]{1,0:T(8,128)S(1)}, f32[48,128]{1,0:T(8,128)S(1)}, u32[]{:S(2)}, u32[]{:S(2)}) collective-permute-start(f32[48,128]{1,0:T(8,128)S(1)} %pad.4.own_ref), channel_id=1, source_target_pairs={{0,1},{8,9},{16,17},{24,25},{1,0},{9,8},{17,16},{25,24},{2,3},{10,... | collective-permute-start | bytes 73736 | tf_op jit(solution)/shard_map/ppermute | solution.py:331
  32.5 1.8 %collective-permute-start.6 = (f32[48,128]{1,0:T(8,128)S(1)}, f32[48,128]{1,0:T(8,128)S(1)}, u32[]{:S(2)}, u32[]{:S(2)}) collective-permute-start(f32[48,128]{1,0:T(8,128)S(1)} %pad.4.own_ref), channel_id=1, source_target_pairs={{0,8},{8,0},{16,24},{24,16},{1,2},{9,10},{17,18},{25,26},{2,1},{10... | collective-permute-start | bytes 73736 | tf_op jit(solution)/shard_map/ppermute | solution.py:331
  32.5 1.8 %copy-start.6 = (s32[1,384]{1,0:T(1,128)S(1)}, s32[1,384]{1,0:T(1,128)}, u32[]{:S(2)}) copy-start(s32[1,384]{1,0:T(1,128)} %constant.55.clone.lane_node_ref) | copy-start | bytes 4612
  32.6 10.5 %copy-start.5 = (s32[6]{0:T(128)}, s32[6]{0:T(128)S(1)}, u32[]{:S(2)}) copy-start(s32[6]{0:T(128)S(1)} %stack.19.place_ref) | copy-start | bytes 76
where the time goes:
time: 51.7 us; the launch traced here: 51.4 us
  Pallas kernels  19.7 us (38%)
  starting transfers between devices  13.7 us (26%)
  waiting for transfers between devices  9.13 us (18%)
  blocking collectives  5.6 us (11%)
  local copies, waits for them, and re-layouts  1.37 us (3%)
  other arithmetic  1.25 us (2%)
  between operations  0.75 us (1%)
    ppermute x9, starting transfers between devices, swap_pairs(): return lax.ppermute(value, (spare, axis) if flip else (axis, spare), moves)  13.6 us
    pallas_call x1, Pallas kernels, flows(): pl.pallas_call(flows_kernel, out_shape=jax.ShapeDtypeStruct((patches, PAT...  9.43 us
    pallas_call x1, Pallas kernels, relax(): pl.pallas_call(relax_kernel, out_shape=(jax.ShapeDtypeStruct((2, nodes, n...  8.72 us
    ppermute x9, waiting for transfers between devices, swap_pairs(): return lax.ppermute(value, (spare, axis) if flip else (axis, spare), moves)  8.18 us
    all_gather x1, blocking collectives, local(): landings = lax.all_gather(landing, 'gz', axis=0)  5.6 us
    pallas_call x1, Pallas kernels, compose(): pl.pallas_call(compose_kernel, out_shape=jax.ShapeDtypeStruct(landings.sh...  1.54 us
    reshape x1, local copies, waits for them, and re-layouts, local(): return (mesh[None], drift[:2].reshape(1, 1, 1, 2, nodes))  1.23 us
    select_n x1, other arithmetic, local(): later = jnp.where(even, chip, far)  1.16 us
  transfers between devices with their start and end apart: 10, of which 3 were waited for; matrix products, arithmetic and copies ran while one was open for 3% of the time, Pallas kernels for 18%

commit v1 on v0

v1 whole, which is shorter than its diff:
```python
import math

import jax
import jax.numpy as jnp
import numpy as np
from jax import lax
from jax.experimental import pallas as pl
from jax.experimental.pallas import tpu as pltpu
from jax.sharding import PartitionSpec as P

PATCH = 128
STRIDE = 4
SWEEPS = 32
HALF = PATCH // 2
BF16 = jnp.bfloat16
F32 = jnp.float32


def split_table(table):
    high = table.astype(BF16)
    low = (table - high.astype(np.float64)).astype(BF16)
    return (high, low)


def transform_tables():
    counter = np.arange(PATCH)
    phase = (counter[:, None] * counter[None, :] % PATCH) * (2.0 * math.pi / PATCH)
    basis = np.concatenate([np.cos(phase[:HALF]), np.sin(phase[:HALF])])
    basis[HALF] = np.cos(phase[HALF])
    gains = np.full(PATCH, 2.0)
    gains[0] = gains[HALF] = 1.0
    inverse = basis.T * gains / PATCH
    forward_pair = np.zeros((2, PATCH, 2, 2, HALF))
    inverse_pair = np.zeros((2, 2, HALF, 2, PATCH))
    for side in range(2):
        forward_pair[side, :, :, side] = basis.T.reshape(PATCH, 2, HALF)
        inverse_pair[:, side, :, side] = inverse.T.reshape(2, HALF, PATCH)
    forward_pair = forward_pair.reshape(2 * PATCH, 2 * PATCH)
    inverse_pair = inverse_pair.reshape(2 * PATCH, 2 * PATCH)
    right_high, right_low = split_table(forward_pair)
    back_high, back_low = split_table(inverse_pair)
    left_high, left_low = split_table(basis)
    undo_high, undo_low = split_table(inverse / PATCH)
    rights = np.stack([right_high, right_low, back_high, back_low])
    lefts = np.stack(
        [
            np.concatenate([left_high, left_high, left_low], axis=1),
            np.concatenate([undo_high, undo_high, undo_low], axis=1),
        ]
    )
    return (rights, lefts)


def halves(value):
    high = value.astype(BF16)
    return (high, (value - high.astype(F32)).astype(BF16))


def dot(left, right):
    return jnp.dot(left, right, preferred_element_type=F32)


def left_transform(table, value):
    high, low = halves(value)
    return dot(table, jnp.concatenate([high, low, high], axis=0))


def quarters(spec):
    return (
        (spec[:HALF, :PATCH], spec[:HALF, PATCH:]),
        (spec[HALF:, :PATCH], spec[HALF:, PATCH:]),
    )


def cross_operand(spec):
    (cc, cs), (sc, ss) = quarters(spec)
    first_row = lax.broadcasted_iota(jnp.int32, (HALF, PATCH), 0) == 0
    first_lane = lax.broadcasted_iota(jnp.int32, (HALF, PATCH), 1) % HALF == 0

    def lanes(cosine, sine):
        return (cosine, jnp.where(first_lane, sine, cosine), jnp.where(first_lane, 0.0, sine))

    return (
        lanes(cc, cs),
        lanes(jnp.where(first_row, sc, cc), jnp.where(first_row, ss, cs)),
        lanes(jnp.where(first_row, 0.0, sc), jnp.where(first_row, 0.0, ss)),
    )


def cross(operand, spec):
    (row_c, row_d, row_s) = operand
    (bc, bs) = quarters(spec)

    def cosine(a, b):
        return a[0] * b[0] + a[2] * b[1]

    def sine(a, b):
        return a[1] * b[1] - a[2] * b[0]

    cc = cosine(row_c, bc) + cosine(row_s, bs)
    cs = sine(row_c, bc) + sine(row_s, bs)
    sc = cosine(row_d, bs) - cosine(row_s, bc)
    ss = sine(row_d, bs) - sine(row_s, bc)
    return jnp.concatenate(
        [jnp.concatenate([cc, cs], axis=1), jnp.concatenate([sc, ss], axis=1)], axis=0
    )


def windows(rows, cols):
    wide = 2 * PATCH
    return [(slice(r, r + PATCH), slice(c, c + wide)) for r in range(0, rows, PATCH) for c in range(0, cols, wide)]


def side_by_side(value):
    return jnp.concatenate([value[i : i + PATCH] for i in range(0, value.shape[0], PATCH)], axis=1)


def forward(pixels, rights_ref, lefts_ref):
    right = dot(pixels, rights_ref[0]) + dot(pixels, rights_ref[1])
    return left_transform(lefts_ref[0], side_by_side(right))


def spectra_kernel(own_ref, near_ref, rights_ref, lefts_ref, own_out, near_out):
    for image, out in ((own_ref, own_out), (near_ref, near_out)):
        pixels = jnp.concatenate([image[window] for window in windows(*image.shape)], axis=0)
        out[...] = forward(pixels, rights_ref, lefts_ref)


def flows_kernel(
    place_ref, far_ref, edge_ref, own_spec, near_spec, rights_ref, lefts_ref, out_ref, stats_ref
):
    wide = 2 * PATCH
    spots = windows(*far_ref.shape)
    blocks = len(spots)
    patches = 2 * blocks
    at_edge = place_ref[5] == 0
    at_even = place_ref[5] % 2 == 0
    pixels = jnp.concatenate(
        [jnp.where(at_edge, edge_ref[spot].astype(F32), far_ref[spot].astype(F32)).astype(BF16) for spot in spots], axis=0
    )
    spec = forward(pixels, rights_ref, lefts_ref)
    products = []
    for block in range(blocks):
        lanes = slice(block * wide, (block + 1) * wide)
        far, near = spec[:, lanes], near_spec[:, lanes]
        operand = cross_operand(jnp.where(at_even, far, near))
        products.append(cross(operand, own_spec[:, lanes]))
        products.append(cross(operand, jnp.where(at_even, near, far)))
    high, low = halves(jnp.concatenate(products, axis=0))
    back = dot(high, rights_ref[2]) + dot(low, rights_ref[2]) + dot(high, rights_ref[3])
    scores = left_transform(lefts_ref[1], side_by_side(back))
    groups = scores.reshape(PATCH // 8, 8, 2 * blocks * wide)
    peak = jnp.max(groups, axis=0)
    total = jnp.zeros_like(peak)
    moment = jnp.zeros_like(peak)
    for group in range(PATCH // 8):
        weight = jnp.exp(groups[group] - peak)
        shift = 8 * group - (PATCH if group >= PATCH // 16 else 0)
        total = total + weight
        moment = moment + float(shift) * weight
    for block in range(blocks):
        for pair in range(2):
            for side in range(2):
                at = (2 * block + pair) * 2 + side
                lanes = slice(at * PATCH, (at + 1) * PATCH)
                slot = pair * patches + 2 * block + side
                stats_ref[0, slot] = peak[:, lanes]
                stats_ref[1, slot] = total[:, lanes]
                stats_ref[2, slot] = moment[:, lanes]
    peak = stats_ref[0]
    best = jnp.max(jnp.max(peak, axis=1, keepdims=True), axis=2, keepdims=True)
    scale = jnp.exp(peak - best)
    total = scale * stats_ref[1]
    within = lax.broadcasted_iota(jnp.int32, peak.shape, 1).astype(F32)
    moment = scale * stats_ref[2] + within * total
    total = jnp.sum(total, axis=1)
    lane = lax.broadcasted_iota(jnp.int32, total.shape, 1)
    signed = jnp.where(lane < HALF, lane, lane - PATCH).astype(F32)
    mass = jnp.sum(total, axis=1, keepdims=True) * STRIDE
    along_rows = jnp.sum(jnp.sum(moment, axis=1), axis=1, keepdims=True) / mass
    along_cols = jnp.sum(total * signed, axis=1, keepdims=True) / mass
    lane = lax.broadcasted_iota(jnp.int32, out_ref.shape, 1)
    near_rows, near_cols = along_rows[:patches], along_cols[:patches]
    out = jnp.where(lane == 0, near_rows, near_cols)
    out = jnp.where(lane == 2, along_rows[patches:] - near_rows, out)
    out_ref[...] = jnp.where(lane == 3, along_cols[patches:] - near_cols, out)


VMEM = pl.BlockSpec(memory_space=pltpu.VMEM)
SMEM = pl.BlockSpec(memory_space=pltpu.SMEM)
PARAMS = pltpu.CompilerParams(vmem_limit_bytes=40 * 2**20)


def spectra(own, near, rights, lefts):
    count = own.shape[0] // PATCH * (own.shape[1] // PATCH)
    spec = jax.ShapeDtypeStruct((PATCH, count * PATCH), F32)
    return pl.pallas_call(
        spectra_kernel,
        out_shape=(spec, spec),
        in_specs=[VMEM] * 4,
        out_specs=(VMEM, VMEM),
        compiler_params=PARAMS,
        cost_estimate=pl.CostEstimate(flops=3 * 10**9, bytes_accessed=3 * 2**20, transcendentals=0),
        name="spectra",
    )(own, near, rights, lefts)


def flows(place, far, edge, own_spec, near_spec, rights, lefts):
    patches = far.shape[0] // PATCH * (far.shape[1] // PATCH)
    return pl.pallas_call(
        flows_kernel,
        out_shape=jax.ShapeDtypeStruct((patches, PATCH), F32),
        in_specs=[SMEM] + [VMEM] * 6,
        out_specs=VMEM,
        scratch_shapes=[pltpu.VMEM((3, 2 * patches, 8, PATCH), F32)],
        compiler_params=PARAMS,
        cost_estimate=pl.CostEstimate(flops=4 * 10**9, bytes_accessed=3 * 2**20, transcendentals=0),
        name="flows",
    )(place, far, edge, own_spec, near_spec, rights, lefts)


def spread_weights(nodes, patches):
    node_pos = (np.arange(nodes) + 0.5) * STRIDE / PATCH - 0.5
    weights = np.maximum(0.0, 1.0 - np.abs(node_pos[:, None] - np.arange(patches)[None, :]))
    return weights / weights.sum(axis=1, keepdims=True)


def ring_nodes(nodes):
    span = np.arange(nodes + 2 * SWEEPS) - SWEEPS
    ring = np.concatenate([span[SWEEPS:], span, span[:SWEEPS]])
    part = np.zeros(len(ring), np.int32)
    part[nodes + SWEEPS : len(ring) - SWEEPS] = 1
    order = np.arange(len(ring)).reshape(PATCH, -1).T.reshape(-1)
    return (ring[order], part[order])


def row_nodes(nodes):
    span = np.arange(nodes + 2 * SWEEPS) - SWEEPS
    return span.reshape(8, -1).T.reshape(-1)


def target_tables(nodes, patches):
    ring, part = ring_nodes(nodes)
    spread = spread_weights(nodes, patches)

    def wide(positions):
        table = np.zeros((len(positions), 3, patches))
        for tile in range(3):
            at = positions - (tile - 1) * nodes
            hit = (at >= 0) & (at < nodes)
            table[hit, tile] = spread[at[hit]]
        return table

    shape = (3, 3, patches, patches)
    rows = wide(row_nodes(nodes))[:, None, :, :, None]
    cols = wide(ring).transpose(1, 2, 0)[:, None, None]
    left = np.broadcast_to(rows, (rows.shape[0],) + shape).reshape(rows.shape[0], -1)
    right = np.broadcast_to(cols, shape + (len(ring),)).reshape(-1, len(ring))
    return (left.astype(BF16), right.astype(np.float32), part[None])


def ring_tables(nodes):
    ring, part = ring_nodes(nodes)
    place = np.arange(3 * nodes)[:, None] - nodes
    into = (place == ring[None]).astype(BF16)
    column = np.arange(2 * nodes)[None]
    out = ((ring[:, None] == column % nodes) & (part[:, None] == column // nodes)).astype(BF16)
    return (into, out, ring.astype(np.int32)[None])


def permuted(value, table):
    result = None
    for piece in range(3):
        part = value.astype(BF16)
        moved = dot(part, table)
        result = moved if result is None else result + moved
        value = value - part.astype(F32)
    return result


def gains_kernel(place_ref, own_ref, even_ref, odd_ref, into_ref, ring_ref, gain_ref, pull_ref, rows_ref):
    strips = gain_ref.shape[0]
    at_even = place_ref[2] == 1
    before = jnp.where(at_even, odd_ref[...], even_ref[...])
    after = jnp.where(at_even, even_ref[...], odd_ref[...])
    weight = permuted(jnp.concatenate([before, own_ref[...], after], axis=1), into_ref[...])
    row_node = lax.broadcasted_iota(jnp.int32, weight.shape, 0) - SWEEPS + place_ref[0]
    col_node = ring_ref[...] + place_ref[1]
    inside = (row_node >= 0) & (row_node < place_ref[3]) & (col_node >= 0) & (col_node < place_ref[4])
    gain = jnp.where(inside, 1.0 / (4.0 + weight), 0.0)
    for value, out in ((gain, gain_ref), (gain * weight, pull_ref)):
        rows_ref[...] = value.reshape(value.shape[0], -1, PATCH).transpose(1, 0, 2)
        for strip in range(strips):
            for tile in range(rows_ref.shape[0]):
                out[strip, :, tile * PATCH : (tile + 1) * PATCH] = rows_ref[tile, pl.ds(strip, 8, strips), :]


def gains(place, own, even, odd, nodes):
    into, _, ring = ring_tables(nodes)
    shape = jax.ShapeDtypeStruct((own.shape[0] // 8, 8, ring.shape[1]), F32)
    return pl.pallas_call(
        gains_kernel,
        out_shape=(shape, shape),
        in_specs=[SMEM] + [VMEM] * 5,
        out_specs=(VMEM, VMEM),
        scratch_shapes=[pltpu.VMEM((ring.shape[1] // PATCH, own.shape[0], PATCH), F32)],
        compiler_params=PARAMS,
        cost_estimate=pl.CostEstimate(flops=10**9, bytes_accessed=2**20, transcendentals=0),
        name="gains",
    )(place, own, even, odd, jnp.asarray(into), jnp.asarray(ring))


def relax_kernel(
    place_ref, own_ref, even_ref, odd_ref, gain_ref, pull_ref, left_ref, right_ref, part_ref, out_table_ref,
    mesh_ref, landing_ref, work_ref, base_ref, rows_ref,
):
    strips, _, lanes = work_ref.shape
    nodes = mesh_ref.shape[2]
    at_even = place_ref[2] == 1
    before = jnp.where(at_even, odd_ref[...], even_ref[...])
    after = jnp.where(at_even, even_ref[...], odd_ref[...])
    sources = jnp.concatenate([before, own_ref[...], after], axis=0)
    spread = jnp.where(part_ref[...] == 1, sources[:, 1:2], sources[:, 0:1]) * right_ref[...]
    target = None
    for piece in range(3):
        part = spread.astype(BF16)
        term = dot(left_ref[...], part)
        target = term if target is None else target + term
        spread = spread - part.astype(F32)
    target = target.reshape(strips, 8, lanes)
    base_ref[...] = pull_ref[...] * target
    work_ref[...] = jnp.where(gain_ref[...] > 0.0, target, 0.0)
    tiles = lanes // PATCH

    def row(strip):
        return [work_ref[strip, :, i * PATCH : (i + 1) * PATCH] for i in range(tiles)]

    def sweep(counter, carry):
        here = row(0)
        above = [pltpu.roll(value, 1, 0) for value in row(strips - 1)]
        around = [pltpu.roll(value, 7, 0) for value in here]
        for strip in range(strips):
            below = row(strip + 1) if strip + 1 < strips else around
            ring = [pltpu.roll(here[-1], 1, 1)] + here + [pltpu.roll(here[0], PATCH - 1, 1)]
            for tile in range(tiles):
                at = (strip, slice(None), slice(tile * PATCH, (tile + 1) * PATCH))
                total = (above[tile] + below[tile]) + (ring[tile] + ring[tile + 2])
                work_ref[at] = gain_ref[at] * total + base_ref[at]
            above, here = here, below
        return carry

    lax.fori_loop(0, SWEEPS, sweep, 0)
    final = permuted(work_ref[...].reshape(strips * 8, lanes), out_table_ref[...])
    for strip in range(strips):
        for part in range(2):
            rows_ref[part, pl.ds(strip, 8, strips), :] = final[8 * strip : 8 * strip + 8, part * nodes : (part + 1) * nodes]
    down = rows_ref[0, SWEEPS : SWEEPS + nodes]
    across = rows_ref[1, SWEEPS : SWEEPS + nodes]
    mesh_ref[0, 0] = down
    mesh_ref[0, 1] = across
    share = 1.0 / nodes
    down_mean = jnp.sum(jnp.transpose(down), axis=0, keepdims=True) * share
    across_mean = jnp.sum(across, axis=0, keepdims=True) * share
    line = lax.broadcasted_iota(jnp.int32, landing_ref.shape, 0)
    ramp = lax.broadcasted_iota(jnp.int32, landing_ref.shape, 1).astype(F32)
    profile = jnp.where(line == 0, down_mean, across_mean)
    landing_ref[...] = jnp.clip(ramp + profile, 0.0, nodes - 1.0)


def relax(place, targets, weights, nodes, patches):
    left, right, part = target_tables(nodes, patches)
    _, out_table, _ = ring_tables(nodes)
    shape = weights[0].shape
    return pl.pallas_call(
        relax_kernel,
        out_shape=(
            jax.ShapeDtypeStruct((1, 2, nodes, nodes), F32),
            jax.ShapeDtypeStruct((8, nodes), F32),
        ),
        in_specs=[SMEM] + [VMEM] * 9,
        out_specs=(VMEM, VMEM),
        scratch_shapes=[pltpu.VMEM(shape, F32)] * 2 + [pltpu.VMEM((2, shape[0] * 8, nodes), F32)],
        compiler_params=PARAMS,
        cost_estimate=pl.CostEstimate(flops=4 * 10**9, bytes_accessed=3 * 2**20, transcendentals=0),
        name="relax",
    )(place, *targets, *weights, *map(jnp.asarray, (left, right, part, out_table)))


def compose_kernel(place_ref, *refs):
    *landing_refs, out_ref = refs
    count = len(landing_refs)
    section = place_ref[5]
    received = [ref[...] for ref in landing_refs]
    nodes = received[0].shape[1]
    ramp = lax.broadcasted_iota(jnp.int32, received[0].shape, 1).astype(F32)
    value = received[0]
    for other in range(count - 2, -1, -1):
        landing = received[0]
        for code in range(1, count):
            landing = jnp.where(section == other ^ code, received[code], landing)
        floor = jnp.minimum(jnp.floor(landing), nodes - 2.0)
        index = floor.astype(jnp.int32)
        share = landing - floor
        below = jnp.take_along_axis(value, index, axis=1)
        above = jnp.take_along_axis(value, index + 1, axis=1)
        value = jnp.where(section > other, (1.0 - share) * below + share * above, value)
    out_ref[0, 0, 0] = (value - ramp)[:2]


def compose(place, landings):
    nodes = landings[0].shape[1]
    return pl.pallas_call(
        compose_kernel,
        out_shape=jax.ShapeDtypeStruct((1, 1, 1, 2, nodes), F32),
        in_specs=[SMEM] + [VMEM] * len(landings),
        out_specs=VMEM,
        name="compose",
    )(place, *landings)


def swap_pairs(value, axis, first, spare):
    count, other = lax.axis_size(axis), lax.axis_size(spare)
    axes = ("gz", "ty", "tx")
    flip = axes.index(axis) > axes.index(spare)

    def place(here, beside):
        return beside * count + here if flip else here * other + beside

    moves = []
    for here in range(count):
        there = ((here + first) ^ 1) - first
        for beside in range(other):
            target = place(there, beside) if 0 <= there < count else place(here, beside ^ 1)
            moves.append((place(here, beside), target))
    return lax.ppermute(value, (spare, axis) if flip else (axis, spare), moves)


def rows_beside(value):
    count = lax.axis_size("ty")
    if count == 2:
        other = swap_pairs(value, "ty", 0, "gz")
        return (other, other)
    even = swap_pairs(value, "ty", 0, "gz")
    odd = swap_pairs(value, "ty", 1, "gz")
    at_even = lax.axis_index("ty") % 2 == 0
    return (jnp.where(at_even, odd, even), jnp.where(at_even, even, odd))


def ring_rows(value):
    up, down = rows_beside(value)
    return jnp.concatenate([up, value, down], axis=0)


def to_next(value, turn):
    count, rows = lax.axis_size("gz"), lax.axis_size("ty")
    if not turn:
        return lax.ppermute(value, "gz", [(i, (i + 1) % count) for i in range(count)])
    moves = [(i * rows + j, (i + 1) % count * rows + (j ^ 1)) for i in range(count) for j in range(rows)]
    return lax.ppermute(value, ("gz", "ty"), moves)


def local(images, boundary, anchor):
    nodes = anchor.shape[1]
    own = images[0]
    patches = own.shape[0] // PATCH
    section, ty, tx = (lax.axis_index(axis) for axis in ("gz", "ty", "tx"))
    sections, n_ty, n_tx = (lax.axis_size(axis) for axis in ("gz", "ty", "tx"))
    place = jnp.stack([ty * nodes, tx * nodes, 1 - tx % 2, n_ty * nodes, n_tx * nodes, section]).astype(jnp.int32)
    rights, lefts = map(jnp.asarray, transform_tables())
    far = swap_pairs(own, "gz", 1, "ty")
    near = swap_pairs(own, "gz", 0, "ty")
    own_spec, near_spec = spectra(own, near, rights, lefts)
    up, down = rows_beside(anchor[0])
    rows = jnp.concatenate([up[nodes - SWEEPS :], anchor[0], down[:SWEEPS]], axis=0)
    weights = gains(place, rows, swap_pairs(rows, "tx", 0, "gz"), swap_pairs(rows, "tx", 1, "gz"), nodes)
    far, weights = lax.optimization_barrier((far, weights))
    flow = flows(place, far, boundary, own_spec, near_spec, rights, lefts)
    around = ring_rows(flow)
    before = to_next(flow, 0)
    if n_ty == 2:
        beside = to_next(flow, 1)
        before = jnp.concatenate([beside, before, beside], axis=0)
    else:
        before = ring_rows(before)
    column = jnp.where(section <= 1, around[:, 0:2], 0.5 * (around[:, 0:2] + before[:, 2:4]))
    column = jnp.pad(column, ((0, 0), (0, PATCH - 2)))
    targets = (column, swap_pairs(column, "tx", 0, "gz"), swap_pairs(column, "tx", 1, "gz"))
    mesh, landing = relax(place, targets, weights, nodes, patches)
    landings = [landing]
    for code in range(1, sections):
        landings.append(lax.ppermute(landing, "gz", [(i, i ^ code) for i in range(sections)]))
    drift = compose(place, landings)
    return (mesh, drift)


def solution(mesh):
    return jax.shard_map(
        local,
        mesh=mesh,
        in_specs=(P("gz", "ty", "tx"), P("ty", "tx"), P("gz", "ty", "tx")),
        out_specs=(P("gz", None, "ty", "tx"), P("gz", "ty", "tx", None, None)),
        check_vma=False,
    )
```

time: 51.7 us -> 44.6 us (0.86)
  blocking collectives: 5.6 us -> 0 us
  Pallas kernels: 19.7 us -> 14.7 us
  waiting for transfers between devices: 9.13 us -> 12 us
  starting transfers between devices: 13.7 us -> 14.7 us
    all_gather x1 -> x0, blocking collectives: 5.6 us -> none  [local(): landings = lax.all_gather(landing, 'gz', axis=0)]
    pallas_call x1, Pallas kernels: 9.43 us -> 4.07 us  [flows(): pl.pallas_call(flows_kernel, out_shape=jax.ShapeDtypeStruct((patches, PAT...]
    ppermute x1 -> x5, starting transfers between devices: 0.06 us -> 5.29 us  [the longest x1 3.37 us: to_next(): return lax.ppermute(value, ('gz', 'ty'), moves)]
    ppermute x9 -> x8, starting transfers between devices: 13.6 us -> 9.37 us  [swap_pairs(): return lax.ppermute(value, (spare, axis) if flip else (axis, spare), moves)]
    ppermute x1 -> x5, waiting for transfers between devices: 0.95 us -> 3.14 us  [the longest x3 1.78 us: local(): lax.ppermute(landing, 'gz', [(i, i ^ code) for i in range(sections)])]
    reshape x1 -> x0, local copies, waits for them, and re-layouts: 1.23 us -> none  [local(): return (mesh[None], drift[:2].reshape(1, 1, 1, 2, nodes))]
    unnamed x16 -> x30, local copies, waits for them, and re-layouts: 0.04 us -> 1.22 us
    select_n x2 -> x1, other arithmetic: 1.24 us -> 0.08 us  [local(): jnp.where(section <= 1, around[:, 0:2], 0.5 * (around[:, 0:2] + before[:,...]
  transfers between devices with their start and end apart: 10 -> 13, of which waited for: 3 -> 7; matrix products, arithmetic and copies ran while one was open for 3% -> 2% of each run, Pallas kernels for 18% -> 3%
where the time goes in v1:
time: 44.6 us; the launch traced here: 44.4 us
  starting transfers between devices  14.7 us (33%)
  Pallas kernels  14.7 us (33%)
  waiting for transfers between devices  12 us (27%)
  local copies, waits for them, and re-layouts  1.31 us (3%)
  other arithmetic  0.92 us (2%)
  between operations  0.84 us (2%)
    ppermute x8, starting transfers between devices, swap_pairs(): return lax.ppermute(value, (spare, axis) if flip else (axis, spare), moves)  9.37 us
    ppermute x8, waiting for transfers between devices, swap_pairs(): return lax.ppermute(value, (spare, axis) if flip else (axis, spare), moves)  8.87 us
    pallas_call x1, Pallas kernels, relax(): pl.pallas_call(relax_kernel, out_shape=(jax.ShapeDtypeStruct((1, 2, nodes...  6.2 us
    pallas_call x1, Pallas kernels, flows(): pl.pallas_call(flows_kernel, out_shape=jax.ShapeDtypeStruct((patches, PAT...  4.07 us
    ppermute x1, starting transfers between devices, to_next(): return lax.ppermute(value, ('gz', 'ty'), moves)  3.37 us
    ppermute x3, starting transfers between devices, local(): lax.ppermute(landing, 'gz', [(i, i ^ code) for i in range(sections)])  1.86 us
    ppermute x3, waiting for transfers between devices, local(): lax.ppermute(landing, 'gz', [(i, i ^ code) for i in range(sections)])  1.78 us
    pallas_call x1, Pallas kernels, spectra(): pl.pallas_call(spectra_kernel, out_shape=(spec, spec), in_specs=[VMEM] *...  1.68 us
  transfers between devices with their start and end apart: 13, of which 7 were waited for; matrix products, arithmetic and copies ran while one was open for 2% of the time, Pallas kernels for 3%

profile of v1, /device:TPU:0, one launch (start us, length us, event | category | flops | bytes accessed | tf_op | source)
XLA Modules:
  0.0 44.4 jit_solution(16938489576029592562)
XLA Ops:
  0.6 3.0 %collective-permute-start.1 = (f32[128,128]{1,0:T(8,128)}, f32[128,128]{1,0:T(8,128)S(1)}, u32[]{:S(2)}, u32[]{:S(2)}) collective-permute-start(f32[128,128]{1,0:T(8,128)} %bitcast.9), channel_id=1, source_target_pairs={{0,4},{8,12},{16,20},{24,28},{4,0},{12,8},{20,16},{28,24},{1,5},{9... | collective-permute-start | bytes 196616 | tf_op jit(solution)/shard_map/ppermute | solution.py:435
  3.7 0.2 collective-permute-start
  3.8 2.3 %collective-permute-done.1 = f32[128,128]{1,0:T(8,128)S(1)} collective-permute-done((f32[128,128]{1,0:T(8,128)}, f32[128,128]{1,0:T(8,128)S(1)}, u32[]{:S(2)}, u32[]{:S(2)}) %collective-permute-start.1) | collective-permute-done | bytes 65568 | tf_op jit(solution)/shard_map/ppermute | solution.py:435
  6.1 0.8 %pad_maximum_fusion.own_ref = f32[192,128]{1,0:T(8,128)S(1)} fusion(f32[32,128]{1,0:T(8,128)S(1)} %get-tuple-element.21, f32[128,128]{1,0:T(8,128)} %bitcast.10, f32[32,128]{1,0:T(8,128)S(1)} %get-tuple-element.20), kind=kLoop, calls=%fused_computation | loop fusion | flops 49152 | bytes 196608 | tf_op jit(solution)/shard_map/concatenate | solution.py:474
  7.0 3.6 %collective-permute-start.2 = (f32[192,128]{1,0:T(8,128)S(1)}, f32[192,128]{1,0:T(8,128)S(1)}, u32[]{:S(2)}, u32[]{:S(2)}) collective-permute-start(f32[192,128]{1,0:T(8,128)S(1)} %pad_maximum_fusion.own_ref), channel_id=1, source_target_pairs={{0,1},{8,9},{16,17},{24,25},{1,0},{9,8},{17,16},{25,24},{2,3},{10,... | collective-permute-start | bytes 294920 | tf_op jit(solution)/shard_map/ppermute | solution.py:435
  10.6 0.1 stack.19.place_ref
  10.8 2.5 %collective-permute-done.2.even_ref = f32[192,128]{1,0:T(8,128)S(1)} collective-permute-done((f32[192,128]{1,0:T(8,128)S(1)}, f32[192,128]{1,0:T(8,128)S(1)}, u32[]{:S(2)}, u32[]{:S(2)}) %collective-permute-start.2) | collective-permute-done | bytes 98336 | tf_op jit(solution)/shard_map/ppermute | solution.py:435
  13.2 1.1 %gains.1 = (f32[24,8,384]{2,1,0:T(8,128)S(1)}, f32[24,8,384]{2,1,0:T(8,128)S(1)}) custom-call(s32[6]{0:T(128)S(1)} %stack.19.place_ref, f32[192,128]{1,0:T(8,128)S(1)} %pad_maximum_fusion.own_ref, f32[192,128]{1,0:T(8,128)S(1)} %collective-permute-done.2.even_ref, f32[192,128]{1,0:T(8,128)S(1)} %collective-permute-done.3.odd_ref, ...), custom_call_target="tpu_custom_call" | custom-call | flops 1000000000 | bytes 1048576 | tf_op jit(solution)/shard_map/gains/pallas_call | solution.py:301
  14.4 1.7 %spectra.1 = (f32[128,2048]{1,0:T(8,128)S(1)}, f32[128,2048]{1,0:T(8,128)S(1)}) custom-call(bf16[512,512]{1,0:T(8,128)(2,1)S(1)} %bitcast.8, bf16[512,512]{1,0:T(8,128)(2,1)S(1)} %collective-permute-done.4.near_ref, bf16[4,256,256]{2,1,0:T(8,128)(2,1)S(1)} %copy-done.4, bf16[2,128,384]{2,1,0:T(8,128)(2,1)S(1)} %copy-done.8), custom_call_target="tpu_custom_call" | custom-call | flops 3000000000 | bytes 3145728 | tf_op jit(solution)/shard_map/spectra/pallas_call | solution.py:197
  16.2 4.1 %flows.1 = f32[16,128]{1,0:T(8,128)S(1)} custom-call(s32[6]{0:T(128)S(1)} %stack.19.place_ref, bf16[512,512]{1,0:T(8,128)(2,1)S(1)} %collective-permute-done.far_ref, bf16[512,512]{1,0:T(8,128)(2,1)S(1)} %copy-done.3, f32[128,2048]{1,0:T(8,128)S(1)} %get-tuple-element.14.own_spec, f32[128,2048]{1,0:T(8,128)S(1)} %get-tuple-element.15.near_spec, ...), custom_call_target="tpu_custom_call" | custom-call | flops 4000000000 | bytes 3145728 | tf_op jit(solution)/shard_map/flows/pallas_call | solution.py:210
  20.3 3.4 %collective-permute-start.6 = (f32[16,128]{1,0:T(8,128)S(1)}, f32[16,128]{1,0:T(8,128)S(1)}, u32[]{:S(2)}, u32[]{:S(2)}) collective-permute-start(f32[16,128]{1,0:T(8,128)S(1)} %flows.1), channel_id=1, source_target_pairs={{0,12},{4,8},{8,20},{12,16},{16,28},{20,24},{24,4},{28,0},{1,13},{... | collective-permute-start | bytes 24584 | tf_op jit(solution)/shard_map/ppermute | solution.py:459
  23.7 1.4 %collective-permute-done.6 = f32[16,128]{1,0:T(8,128)S(1)} collective-permute-done((f32[16,128]{1,0:T(8,128)S(1)}, f32[16,128]{1,0:T(8,128)S(1)}, u32[]{:S(2)}, u32[]{:S(2)}) %collective-permute-start.6) | collective-permute-done | bytes 8224 | tf_op jit(solution)/shard_map/ppermute | solution.py:459
  25.1 2.3 %collective-permute-done.5 = f32[16,128]{1,0:T(8,128)S(1)} collective-permute-done((f32[16,128]{1,0:T(8,128)S(1)}, f32[16,128]{1,0:T(8,128)S(1)}, u32[]{:S(2)}, u32[]{:S(2)}) %collective-permute-start.5) | collective-permute-done | bytes 8224 | tf_op jit(solution)/shard_map/ppermute | solution.py:435
  27.3 0.1 fusion.2
  27.5 2.5 %collective-permute-start.8 = (f32[48,128]{1,0:T(8,128)S(1)}, f32[48,128]{1,0:T(8,128)S(1)}, u32[]{:S(2)}, u32[]{:S(2)}) collective-permute-start(f32[48,128]{1,0:T(8,128)S(1)} %pad.4.own_ref), channel_id=1, source_target_pairs={{0,1},{8,9},{16,17},{24,25},{1,0},{9,8},{17,16},{25,24},{2,3},{10,... | collective-permute-start | bytes 73736 | tf_op jit(solution)/shard_map/ppermute | solution.py:435
  30.0 1.8 %collective-permute-done.8.even_ref = f32[48,128]{1,0:T(8,128)S(1)} collective-permute-done((f32[48,128]{1,0:T(8,128)S(1)}, f32[48,128]{1,0:T(8,128)S(1)}, u32[]{:S(2)}, u32[]{:S(2)}) %collective-permute-start.8) | collective-permute-done | bytes 24608 | tf_op jit(solution)/shard_map/ppermute | solution.py:435
  31.8 6.2 %relax.1 = (f32[1,2,128,128]{3,2,1,0:T(8,128)}, f32[8,128]{1,0:T(8,128)S(1)}) custom-call(s32[6]{0:T(128)S(1)} %stack.19.place_ref, f32[48,128]{1,0:T(8,128)S(1)} %pad.4.own_ref, f32[48,128]{1,0:T(8,128)S(1)} %collective-permute-done.8.even_ref, f32[48,128]{1,0:T(8,128)S(1)} %collective-permute-done.9.odd_ref, f32[24,8,384]{2,1,0:T(8,128)S(1)} %get-tuple-element.16.gain_ref, ...), custom_call_target="tpu_custom_call" | custom-call | flops 4000000000 | bytes 3145728 | tf_op jit(solution)/shard_map/relax/pallas_call | solution.py:374
  38.0 0.6 %collective-permute-start.11 = (f32[8,128]{1,0:T(8,128)S(1)}, f32[8,128]{1,0:T(8,128)S(1)}, u32[]{:S(2)}, u32[]{:S(2)}) collective-permute-start(f32[8,128]{1,0:T(8,128)S(1)} %get-tuple-element.19.refs_0_), channel_id=1, source_target_pairs={{0,16},{8,24},{16,0},{24,8},{1,17},{9,25},{17,1},{25,9},{2,18},{10... | collective-permute-start | bytes 12296 | tf_op jit(solution)/shard_map/ppermute | solution.py:491
  38.6 1.3 %collective-permute-start.10 = (f32[8,128]{1,0:T(8,128)S(1)}, f32[8,128]{1,0:T(8,128)S(1)}, u32[]{:S(2)}, u32[]{:S(2)}) collective-permute-start(f32[8,128]{1,0:T(8,128)S(1)} %get-tuple-element.19.refs_0_), channel_id=1, source_target_pairs={{0,8},{8,0},{16,24},{24,16},{1,9},{9,1},{17,25},{25,17},{2,10},{10... | collective-permute-start | bytes 12296 | tf_op jit(solution)/shard_map/ppermute | solution.py:491
  39.9 1.2 %collective-permute-done.12.refs_3_ = f32[8,128]{1,0:T(8,128)S(1)} collective-permute-done((f32[8,128]{1,0:T(8,128)S(1)}, f32[8,128]{1,0:T(8,128)S(1)}, u32[]{:S(2)}, u32[]{:S(2)}) %collective-permute-start.12) | collective-permute-done | bytes 4128 | tf_op jit(solution)/shard_map/ppermute | solution.py:491
  41.0 0.6 %collective-permute-done.11.refs_2_ = f32[8,128]{1,0:T(8,128)S(1)} collective-permute-done((f32[8,128]{1,0:T(8,128)S(1)}, f32[8,128]{1,0:T(8,128)S(1)}, u32[]{:S(2)}, u32[]{:S(2)}) %collective-permute-start.11) | collective-permute-done | bytes 4128 | tf_op jit(solution)/shard_map/ppermute | solution.py:491
  41.7 0.6 %copy-done.13 = f32[8,128]{1,0:T(8,128)} copy-done((f32[8,128]{1,0:T(8,128)}, f32[8,128]{1,0:T(8,128)S(1)}, u32[]{:S(2)}) %copy-start.13) | copy-done | bytes 4120
  42.2 0.6 %copy-done.14 = f32[8,128]{1,0:T(8,128)} copy-done((f32[8,128]{1,0:T(8,128)}, f32[8,128]{1,0:T(8,128)S(1)}, u32[]{:S(2)}) %copy-start.14) | copy-done | bytes 4120
  42.8 1.6 %compose.1 = f32[1,1,1,2,128]{4,3,2,1,0:T(2,128)} custom-call(s32[6]{0:T(128)} %copy-done.1, f32[8,128]{1,0:T(8,128)} %copy-done, f32[8,128]{1,0:T(8,128)} %copy-done.14, f32[8,128]{1,0:T(8,128)} %copy-done.13, f32[8,128]{1,0:T(8,128)} %copy-done.12), custom_call_target="tpu_custom_call" | custom-call | tf_op jit(solution)/shard_map/compose/pallas_call | solution.py:412
  (42 shorter events, 0.2 us)
Async XLA Ops:
  0.6 12.6 %copy-start.5 = (bf16[384,384]{1,0:T(8,128)(2,1)S(1)}, bf16[384,384]{1,0:T(8,128)(2,1)}, u32[]{:S(2)}) copy-start(bf16[384,384]{1,0:T(8,128)(2,1)} %constant.55.clone.into_ref) | copy-start | bytes 884740
  0.6 5.5 %collective-permute-start.1 = (f32[128,128]{1,0:T(8,128)}, f32[128,128]{1,0:T(8,128)S(1)}, u32[]{:S(2)}, u32[]{:S(2)}) collective-permute-start(f32[128,128]{1,0:T(8,128)} %bitcast.9), channel_id=1, source_target_pairs={{0,4},{8,12},{16,20},{24,28},{4,0},{12,8},{20,16},{28,24},{1,5},{9... | collective-permute-start | bytes 196616 | tf_op jit(solution)/shard_map/ppermute | solution.py:435
  3.7 10.7 %collective-permute-start.4 = (bf16[512,512]{1,0:T(8,128)(2,1)}, bf16[512,512]{1,0:T(8,128)(2,1)S(1)}, u32[]{:S(2)}, u32[]{:S(2)}) collective-permute-start(bf16[512,512]{1,0:T(8,128)(2,1)} %bitcast.6), channel_id=1, source_target_pairs={{0,8},{4,12},{8,0},{12,4},{16,24},{20,28},{24,16},{28,20},{1,9},{5... | collective-permute-start | bytes 1572872 | tf_op jit(solution)/shard_map/ppermute | solution.py:435
  3.7 10.7 %collective-permute-start = (bf16[512,512]{1,0:T(8,128)(2,1)}, bf16[512,512]{1,0:T(8,128)(2,1)S(1)}, u32[]{:S(2)}, u32[]{:S(2)}) collective-permute-start(bf16[512,512]{1,0:T(8,128)(2,1)} %bitcast.7), channel_id=1, source_target_pairs={{0,4},{4,0},{8,16},{12,20},{16,8},{20,12},{24,28},{28,24},{1,5},{5... | collective-permute-start | bytes 1572872 | tf_op jit(solution)/shard_map/ppermute | solution.py:435
  7.0 3.8 %collective-permute-start.3 = (f32[192,128]{1,0:T(8,128)S(1)}, f32[192,128]{1,0:T(8,128)S(1)}, u32[]{:S(2)}, u32[]{:S(2)}) collective-permute-start(f32[192,128]{1,0:T(8,128)S(1)} %pad_maximum_fusion.own_ref), channel_id=1, source_target_pairs={{0,8},{8,0},{16,24},{24,16},{1,2},{9,10},{17,18},{25,26},{2,1},{10... | collective-permute-start | bytes 294920 | tf_op jit(solution)/shard_map/ppermute | solution.py:435
  7.0 6.2 %collective-permute-start.2 = (f32[192,128]{1,0:T(8,128)S(1)}, f32[192,128]{1,0:T(8,128)S(1)}, u32[]{:S(2)}, u32[]{:S(2)}) collective-permute-start(f32[192,128]{1,0:T(8,128)S(1)} %pad_maximum_fusion.own_ref), channel_id=1, source_target_pairs={{0,1},{8,9},{16,17},{24,25},{1,0},{9,8},{17,16},{25,24},{2,3},{10,... | collective-permute-start | bytes 294920 | tf_op jit(solution)/shard_map/ppermute | solution.py:435
  10.6 2.6 %copy-start.11 = (s32[1,384]{1,0:T(1,128)S(1)}, s32[1,384]{1,0:T(1,128)}, u32[]{:S(2)}) copy-start(s32[1,384]{1,0:T(1,128)} %constant.56.clone.ring_ref) | copy-start | bytes 4612
  10.7 21.1 %copy-start.1 = (s32[6]{0:T(128)}, s32[6]{0:T(128)S(1)}, u32[]{:S(2)}) copy-start(s32[6]{0:T(128)S(1)} %stack.19.place_ref) | copy-start | bytes 76
  10.7 3.7 %copy-start.2 = (bf16[1,512,512]{2,1,0:T(8,128)(2,1)S(1)}, bf16[1,512,512]{2,1,0:T(8,128)(2,1)}, u32[]{:S(2)}) copy-start(bf16[1,512,512]{2,1,0:T(8,128)(2,1)} %param.11) | copy-start | bytes 1572868
  10.7 3.7 %copy-start.4 = (bf16[4,256,256]{2,1,0:T(8,128)(2,1)S(1)}, bf16[4,256,256]{2,1,0:T(8,128)(2,1)}, u32[]{:S(2)}) copy-start(bf16[4,256,256]{2,1,0:T(8,128)(2,1)} %constant.53.clone.rights_ref) | copy-start | bytes 1572868
  10.7 3.7 %copy-start.8 = (bf16[2,128,384]{2,1,0:T(8,128)(2,1)S(1)}, bf16[2,128,384]{2,1,0:T(8,128)(2,1)}, u32[]{:S(2)}) copy-start(bf16[2,128,384]{2,1,0:T(8,128)(2,1)} %constant.54.clone.lefts_ref) | copy-start | bytes 589828
  16.1 15.6 %copy-start.6 = (f32[144,384]{1,0:T(8,128)S(1)}, f32[144,384]{1,0:T(8,128)}, u32[]{:S(2)}) copy-start(f32[144,384]{1,0:T(8,128)} %constant.58.clone.right_ref) | copy-start | bytes 663556
  16.2 15.6 %copy-start.7 = (bf16[384,256]{1,0:T(8,128)(2,1)S(1)}, bf16[384,256]{1,0:T(8,128)(2,1)}, u32[]{:S(2)}) copy-start(bf16[384,256]{1,0:T(8,128)(2,1)} %constant.60.clone.out_table_ref) | copy-start | bytes 589828
  20.2 11.5 %copy-start.9 = (bf16[192,144]{1,0:T(8,128)(2,1)S(1)}, bf16[192,144]{1,0:T(8,128)(2,1)}, u32[]{:S(2)}) copy-start(bf16[192,144]{1,0:T(8,128)(2,1)} %constant.57.clone.left_ref) | copy-start | bytes 165892
  20.3 3.4 %collective-permute-start.7 = (f32[16,128]{1,0:T(8,128)S(1)}, f32[16,128]{1,0:T(8,128)S(1)}, u32[]{:S(2)}, u32[]{:S(2)}) collective-permute-start(f32[16,128]{1,0:T(8,128)S(1)} %flows.1), channel_id=1, source_target_pairs={{0,8},{8,16},{16,24},{24,0},{1,9},{9,17},{17,25},{25,1},{2,10},{10... | collective-permute-start | bytes 24584 | tf_op jit(solution)/shard_map/ppermute | solution.py:457
  20.3 4.7 %collective-permute-start.6 = (f32[16,128]{1,0:T(8,128)S(1)}, f32[16,128]{1,0:T(8,128)S(1)}, u32[]{:S(2)}, u32[]{:S(2)}) collective-permute-start(f32[16,128]{1,0:T(8,128)S(1)} %flows.1), channel_id=1, source_target_pairs={{0,12},{4,8},{8,20},{12,16},{16,28},{20,24},{24,4},{28,0},{1,13},{... | collective-permute-start | bytes 24584 | tf_op jit(solution)/shard_map/ppermute | solution.py:459
  23.7 3.7 %collective-permute-start.5 = (f32[16,128]{1,0:T(8,128)S(1)}, f32[16,128]{1,0:T(8,128)S(1)}, u32[]{:S(2)}, u32[]{:S(2)}) collective-permute-start(f32[16,128]{1,0:T(8,128)S(1)} %flows.1), channel_id=1, source_target_pairs={{0,4},{8,12},{16,20},{24,28},{4,0},{12,8},{20,16},{28,24},{1,5},{9... | collective-permute-start | bytes 24584 | tf_op jit(solution)/shard_map/ppermute | solution.py:435
  27.4 4.4 %copy-start.10 = (s32[1,384]{1,0:T(1,128)S(1)}, s32[1,384]{1,0:T(1,128)}, u32[]{:S(2)}) copy-start(s32[1,384]{1,0:T(1,128)} %constant.59.clone.part_ref) | copy-start | bytes 4612
  27.4 2.5 %collective-permute-start.9 = (f32[48,128]{1,0:T(8,128)S(1)}, f32[48,128]{1,0:T(8,128)S(1)}, u32[]{:S(2)}, u32[]{:S(2)}) collective-permute-start(f32[48,128]{1,0:T(8,128)S(1)} %pad.4.own_ref), channel_id=1, source_target_pairs={{0,8},{8,0},{16,24},{24,16},{1,2},{9,10},{17,18},{25,26},{2,1},{10... | collective-permute-start | bytes 73736 | tf_op jit(solution)/shard_map/ppermute | solution.py:435
  27.5 4.3 %collective-permute-start.8 = (f32[48,128]{1,0:T(8,128)S(1)}, f32[48,128]{1,0:T(8,128)S(1)}, u32[]{:S(2)}, u32[]{:S(2)}) collective-permute-start(f32[48,128]{1,0:T(8,128)S(1)} %pad.4.own_ref), channel_id=1, source_target_pairs={{0,1},{8,9},{16,17},{24,25},{1,0},{9,8},{17,16},{25,24},{2,3},{10,... | collective-permute-start | bytes 73736 | tf_op jit(solution)/shard_map/ppermute | solution.py:435
  38.0 3.7 %copy-start = (f32[8,128]{1,0:T(8,128)}, f32[8,128]{1,0:T(8,128)S(1)}, u32[]{:S(2)}) copy-start(f32[8,128]{1,0:T(8,128)S(1)} %get-tuple-element.19.refs_0_) | copy-start | bytes 12292
  38.0 3.0 %collective-permute-start.12 = (f32[8,128]{1,0:T(8,128)S(1)}, f32[8,128]{1,0:T(8,128)S(1)}, u32[]{:S(2)}, u32[]{:S(2)}) collective-permute-start(f32[8,128]{1,0:T(8,128)S(1)} %get-tuple-element.19.refs_0_), channel_id=1, source_target_pairs={{0,24},{8,16},{16,8},{24,0},{1,25},{9,17},{17,9},{25,1},{2,26},{10... | collective-permute-start | bytes 12296 | tf_op jit(solution)/shard_map/ppermute | solution.py:491
  38.0 3.6 %collective-permute-start.11 = (f32[8,128]{1,0:T(8,128)S(1)}, f32[8,128]{1,0:T(8,128)S(1)}, u32[]{:S(2)}, u32[]{:S(2)}) collective-permute-start(f32[8,128]{1,0:T(8,128)S(1)} %get-tuple-element.19.refs_0_), channel_id=1, source_target_pairs={{0,16},{8,24},{16,0},{24,8},{1,17},{9,25},{17,1},{25,9},{2,18},{10... | collective-permute-start | bytes 12296 | tf_op jit(solution)/shard_map/ppermute | solution.py:491
  38.6 3.1 %collective-permute-start.10 = (f32[8,128]{1,0:T(8,128)S(1)}, f32[8,128]{1,0:T(8,128)S(1)}, u32[]{:S(2)}, u32[]{:S(2)}) collective-permute-start(f32[8,128]{1,0:T(8,128)S(1)} %get-tuple-element.19.refs_0_), channel_id=1, source_target_pairs={{0,8},{8,0},{16,24},{24,16},{1,9},{9,1},{17,25},{25,17},{2,10},{10... | collective-permute-start | bytes 12296 | tf_op jit(solution)/shard_map/ppermute | solution.py:491
  (4 other events, 3.5 us)

commit v2 on v1

--- a/solution.py
+++ b/solution.py
@@ -127,14 +127,14 @@
 
 
 def flows_kernel(
-    place_ref, far_ref, edge_ref, own_spec, near_spec, rights_ref, lefts_ref, out_ref, stats_ref
+    far_ref, edge_ref, own_spec, near_spec, rights_ref, lefts_ref, out_ref, stats_ref
 ):
     wide = 2 * PATCH
     spots = windows(*far_ref.shape)
     blocks = len(spots)
     patches = 2 * blocks
-    at_edge = place_ref[5] == 0
-    at_even = place_ref[5] % 2 == 0
+    at_edge = lax.axis_index("gz") == 0
+    at_even = lax.axis_index("gz") % 2 == 0
     pixels = jnp.concatenate(
         [jnp.where(at_edge, edge_ref[spot].astype(F32), far_ref[spot].astype(F32)).astype(BF16) for spot in spots], axis=0
     )
@@ -179,15 +179,23 @@
     mass = jnp.sum(total, axis=1, keepdims=True) * STRIDE
     along_rows = jnp.sum(jnp.sum(moment, axis=1), axis=1, keepdims=True) / mass
     along_cols = jnp.sum(total * signed, axis=1, keepdims=True) / mass
-    lane = lax.broadcasted_iota(jnp.int32, out_ref.shape, 1)
-    near_rows, near_cols = along_rows[:patches], along_cols[:patches]
-    out = jnp.where(lane == 0, near_rows, near_cols)
-    out = jnp.where(lane == 2, along_rows[patches:] - near_rows, out)
-    out_ref[...] = jnp.where(lane == 3, along_cols[patches:] - near_cols, out)
+    values = (
+        along_rows[:patches],
+        along_cols[:patches],
+        along_rows[patches:] - along_rows[:patches],
+        along_cols[patches:] - along_cols[:patches],
+    )
+    lane = lax.broadcasted_iota(jnp.int32, (patches, PATCH), 1)
+    patch = lax.broadcasted_iota(jnp.int32, (patches, PATCH), 0)
+    lines = []
+    for first, second in (values[:2], values[2:]):
+        line = jnp.where(lane == patch, first, jnp.where(lane == patches + patch, second, 0.0))
+        lines.append(jnp.sum(line, axis=0, keepdims=True))
+    line = lax.broadcasted_iota(jnp.int32, out_ref.shape, 0)
+    out_ref[...] = jnp.where(line == 0, lines[0], lines[1])
 
 
 VMEM = pl.BlockSpec(memory_space=pltpu.VMEM)
-SMEM = pl.BlockSpec(memory_space=pltpu.SMEM)
 PARAMS = pltpu.CompilerParams(vmem_limit_bytes=40 * 2**20)
 
 
@@ -205,18 +213,18 @@
     )(own, near, rights, lefts)
 
 
-def flows(place, far, edge, own_spec, near_spec, rights, lefts):
+def flows(far, edge, own_spec, near_spec, rights, lefts):
     patches = far.shape[0] // PATCH * (far.shape[1] // PATCH)
     return pl.pallas_call(
         flows_kernel,
-        out_shape=jax.ShapeDtypeStruct((patches, PATCH), F32),
-        in_specs=[SMEM] + [VMEM] * 6,
+        out_shape=jax.ShapeDtypeStruct((8, PATCH), F32),
+        in_specs=[VMEM] * 6,
         out_specs=VMEM,
         scratch_shapes=[pltpu.VMEM((3, 2 * patches, 8, PATCH), F32)],
         compiler_params=PARAMS,
         cost_estimate=pl.CostEstimate(flops=4 * 10**9, bytes_accessed=3 * 2**20, transcendentals=0),
         name="flows",
-    )(place, far, edge, own_spec, near_spec, rights, lefts)
+    )(far, edge, own_spec, near_spec, rights, lefts)
 
 
 def spread_weights(nodes, patches):
@@ -278,15 +286,22 @@
     return result
 
 
-def gains_kernel(place_ref, own_ref, even_ref, odd_ref, into_ref, ring_ref, gain_ref, pull_ref, rows_ref):
+def tiles_beside(even_ref, odd_ref):
+    at_even = lax.axis_index("tx") % 2 == 0
+    even, odd = even_ref[...], odd_ref[...]
+    return (jnp.where(at_even, odd, even), jnp.where(at_even, even, odd))
+
+
+def gains_kernel(own_ref, even_ref, odd_ref, into_ref, ring_ref, gain_ref, pull_ref, rows_ref):
     strips = gain_ref.shape[0]
-    at_even = place_ref[2] == 1
-    before = jnp.where(at_even, odd_ref[...], even_ref[...])
-    after = jnp.where(at_even, even_ref[...], odd_ref[...])
+    nodes = own_ref.shape[1]
+    before, after = tiles_beside(even_ref, odd_ref)
     weight = permuted(jnp.concatenate([before, own_ref[...], after], axis=1), into_ref[...])
-    row_node = lax.broadcasted_iota(jnp.int32, weight.shape, 0) - SWEEPS + place_ref[0]
-    col_node = ring_ref[...] + place_ref[1]
-    inside = (row_node >= 0) & (row_node < place_ref[3]) & (col_node >= 0) & (col_node < place_ref[4])
+    row_node = lax.broadcasted_iota(jnp.int32, weight.shape, 0) - SWEEPS
+    row_node = row_node + lax.axis_index("ty") * nodes
+    col_node = ring_ref[...] + lax.axis_index("tx") * nodes
+    inside = (row_node >= 0) & (row_node < lax.axis_size("ty") * nodes)
+    inside = inside & (col_node >= 0) & (col_node < lax.axis_size("tx") * nodes)
     gain = jnp.where(inside, 1.0 / (4.0 + weight), 0.0)
     for value, out in ((gain, gain_ref), (gain * weight, pull_ref)):
         rows_ref[...] = value.reshape(value.shape[0], -1, PATCH).transpose(1, 0, 2)
@@ -295,32 +310,38 @@
                 out[strip, :, tile * PATCH : (tile + 1) * PATCH] = rows_ref[tile, pl.ds(strip, 8, strips), :]
 
 
-def gains(place, own, even, odd, nodes):
+def gains(own, even, odd, nodes):
     into, _, ring = ring_tables(nodes)
     shape = jax.ShapeDtypeStruct((own.shape[0] // 8, 8, ring.shape[1]), F32)
     return pl.pallas_call(
         gains_kernel,
         out_shape=(shape, shape),
-        in_specs=[SMEM] + [VMEM] * 5,
+        in_specs=[VMEM] * 5,
         out_specs=(VMEM, VMEM),
         scratch_shapes=[pltpu.VMEM((ring.shape[1] // PATCH, own.shape[0], PATCH), F32)],
         compiler_params=PARAMS,
         cost_estimate=pl.CostEstimate(flops=10**9, bytes_accessed=2**20, transcendentals=0),
         name="gains",
-    )(place, own, even, odd, jnp.asarray(into), jnp.asarray(ring))
+    )(own, even, odd, jnp.asarray(into), jnp.asarray(ring))
 
 
 def relax_kernel(
-    place_ref, own_ref, even_ref, odd_ref, gain_ref, pull_ref, left_ref, right_ref, part_ref, out_table_ref,
+    own_ref, even_ref, odd_ref, gain_ref, pull_ref, left_ref, right_ref, part_ref, out_table_ref,
     mesh_ref, landing_ref, work_ref, base_ref, rows_ref,
 ):
     strips, _, lanes = work_ref.shape
     nodes = mesh_ref.shape[2]
-    at_even = place_ref[2] == 1
-    before = jnp.where(at_even, odd_ref[...], even_ref[...])
-    after = jnp.where(at_even, even_ref[...], odd_ref[...])
-    sources = jnp.concatenate([before, own_ref[...], after], axis=0)
-    spread = jnp.where(part_ref[...] == 1, sources[:, 1:2], sources[:, 0:1]) * right_ref[...]
+    patches = left_ref.shape[1] // 9
+    before, after = tiles_beside(even_ref, odd_ref)
+    rows = [before[:3], own_ref[:3], after[:3]]
+    rows.append(jnp.zeros((PATCH - 9, PATCH), F32))
+    columns = jnp.transpose(jnp.concatenate(rows, axis=0))
+
+    def sources(part):
+        lines = slice(part * patches, (part + 1) * patches)
+        return jnp.concatenate([columns[lines, i : i + 1] for i in range(9)], axis=0)
+
+    spread = jnp.where(part_ref[...] == 1, sources(1), sources(0)) * right_ref[...]
     target = None
     for piece in range(3):
         part = spread.astype(BF16)
@@ -349,7 +370,7 @@
             above, here = here, below
         return carry
 
-    lax.fori_loop(0, SWEEPS, sweep, 0)
+    lax.fori_loop(0, SWEEPS, sweep, 0, unroll=8)
     final = permuted(work_ref[...].reshape(strips * 8, lanes), out_table_ref[...])
     for strip in range(strips):
         for part in range(2):
@@ -367,7 +388,7 @@
     landing_ref[...] = jnp.clip(ramp + profile, 0.0, nodes - 1.0)
 
 
-def relax(place, targets, weights, nodes, patches):
+def relax(targets, weights, nodes, patches):
     left, right, part = target_tables(nodes, patches)
     _, out_table, _ = ring_tables(nodes)
     shape = weights[0].shape
@@ -377,19 +398,19 @@
             jax.ShapeDtypeStruct((1, 2, nodes, nodes), F32),
             jax.ShapeDtypeStruct((8, nodes), F32),
         ),
-        in_specs=[SMEM] + [VMEM] * 9,
+        in_specs=[VMEM] * 9,
         out_specs=(VMEM, VMEM),
         scratch_shapes=[pltpu.VMEM(shape, F32)] * 2 + [pltpu.VMEM((2, shape[0] * 8, nodes), F32)],
         compiler_params=PARAMS,
         cost_estimate=pl.CostEstimate(flops=4 * 10**9, bytes_accessed=3 * 2**20, transcendentals=0),
         name="relax",
-    )(place, *targets, *weights, *map(jnp.asarray, (left, right, part, out_table)))
-
-
-def compose_kernel(place_ref, *refs):
+    )(*targets, *weights, *map(jnp.asarray, (left, right, part, out_table)))
+
+
+def compose_kernel(*refs):
     *landing_refs, out_ref = refs
     count = len(landing_refs)
-    section = place_ref[5]
+    section = lax.axis_index("gz")
     received = [ref[...] for ref in landing_refs]
     nodes = received[0].shape[1]
     ramp = lax.broadcasted_iota(jnp.int32, received[0].shape, 1).astype(F32)
@@ -407,15 +428,16 @@
     out_ref[0, 0, 0] = (value - ramp)[:2]
 
 
-def compose(place, landings):
+def compose(landings):
     nodes = landings[0].shape[1]
     return pl.pallas_call(
         compose_kernel,
         out_shape=jax.ShapeDtypeStruct((1, 1, 1, 2, nodes), F32),
-        in_specs=[SMEM] + [VMEM] * len(landings),
+        in_specs=[VMEM] * len(landings),
         out_specs=VMEM,
+        compiler_params=pltpu.CompilerParams(vmem_limit_bytes=2**20),
         name="compose",
-    )(place, *landings)
+    )(*landings)
 
 
 def swap_pairs(value, axis, first, spare):
@@ -446,11 +468,6 @@
     return (jnp.where(at_even, odd, even), jnp.where(at_even, even, odd))
 
 
-def ring_rows(value):
-    up, down = rows_beside(value)
-    return jnp.concatenate([up, value, down], axis=0)
-
-
 def to_next(value, turn):
     count, rows = lax.axis_size("gz"), lax.axis_size("ty")
     if not turn:
@@ -459,37 +476,44 @@
     return lax.ppermute(value, ("gz", "ty"), moves)
 
 
+def patch_targets(flow):
+    first = lax.axis_index("gz") <= 1
+    before = to_next(flow, 0)
+
+    def target(near, earlier):
+        return jnp.where(first, near[0:1], 0.5 * (near[0:1] + earlier[1:2]))
+
+    if lax.axis_size("ty") == 2:
+        beside = target(rows_beside(flow)[0], to_next(flow, 1))
+        lines = [beside, target(flow, before), beside]
+    else:
+        (up, down), (up_before, down_before) = rows_beside(flow), rows_beside(before)
+        lines = [target(up, up_before), target(flow, before), target(down, down_before)]
+    return jnp.concatenate(lines + [jnp.zeros((5, flow.shape[1]), F32)], axis=0)
+
+
 def local(images, boundary, anchor):
     nodes = anchor.shape[1]
     own = images[0]
     patches = own.shape[0] // PATCH
-    section, ty, tx = (lax.axis_index(axis) for axis in ("gz", "ty", "tx"))
-    sections, n_ty, n_tx = (lax.axis_size(axis) for axis in ("gz", "ty", "tx"))
-    place = jnp.stack([ty * nodes, tx * nodes, 1 - tx % 2, n_ty * nodes, n_tx * nodes, section]).astype(jnp.int32)
+    sections = lax.axis_size("gz")
     rights, lefts = map(jnp.asarray, transform_tables())
     far = swap_pairs(own, "gz", 1, "ty")
     near = swap_pairs(own, "gz", 0, "ty")
-    own_spec, near_spec = spectra(own, near, rights, lefts)
     up, down = rows_beside(anchor[0])
     rows = jnp.concatenate([up[nodes - SWEEPS :], anchor[0], down[:SWEEPS]], axis=0)
-    weights = gains(place, rows, swap_pairs(rows, "tx", 0, "gz"), swap_pairs(rows, "tx", 1, "gz"), nodes)
-    far, weights = lax.optimization_barrier((far, weights))
-    flow = flows(place, far, boundary, own_spec, near_spec, rights, lefts)
-    around = ring_rows(flow)
-    before = to_next(flow, 0)
-    if n_ty == 2:
-        beside = to_next(flow, 1)
-        before = jnp.concatenate([beside, before, beside], axis=0)
-    else:
-        before = ring_rows(before)
-    column = jnp.where(section <= 1, around[:, 0:2], 0.5 * (around[:, 0:2] + before[:, 2:4]))
-    column = jnp.pad(column, ((0, 0), (0, PATCH - 2)))
-    targets = (column, swap_pairs(column, "tx", 0, "gz"), swap_pairs(column, "tx", 1, "gz"))
-    mesh, landing = relax(place, targets, weights, nodes, patches)
+    near, rows = lax.optimization_barrier((near, rows))
+    specs = spectra(own, near, rights, lefts)
+    weights = gains(rows, swap_pairs(rows, "tx", 0, "gz"), swap_pairs(rows, "tx", 1, "gz"), nodes)
+    far, weights, specs = lax.optimization_barrier((far, weights, specs))
+    flow = flows(far, boundary, *specs, rights, lefts)
+    line = patch_targets(flow)
+    targets = (line, swap_pairs(line, "tx", 0, "gz"), swap_pairs(line, "tx", 1, "gz"))
+    mesh, landing = relax(targets, weights, nodes, patches)
     landings = [landing]
     for code in range(1, sections):
         landings.append(lax.ppermute(landing, "gz", [(i, i ^ code) for i in range(sections)]))
-    drift = compose(place, landings)
+    drift = compose(landings)
     return (mesh, drift)
 
 

time: 44.6 us -> 38.8 us (0.87)
  Pallas kernels: 14.7 us -> 11 us
  waiting for transfers between devices: 12 us -> 9.44 us
  local copies, waits for them, and re-layouts: 1.31 us -> 2.74 us
  starting transfers between devices: 14.7 us -> 13.7 us
    ppermute x8, waiting for transfers between devices: 8.87 us -> 4.71 us  [swap_pairs(): return lax.ppermute(value, (spare, axis) if flip else (axis, spare), moves)]
    ppermute x1, starting transfers between devices: 3.37 us -> 1.22 us  [to_next(): return lax.ppermute(value, ('gz', 'ty'), moves)]
    pallas_call x1, Pallas kernels: 6.2 us -> 4.34 us  [relax(): pl.pallas_call(relax_kernel, out_shape=(jax.ShapeDtypeStruct((1, 2, nodes...]
    unnamed x30 -> x22, local copies, waits for them, and re-layouts: 1.22 us -> 2.66 us
    ppermute x3, waiting for transfers between devices: 1.78 us -> 2.89 us  [local(): lax.ppermute(landing, 'gz', [(i, i ^ code) for i in range(sections)])]
    pallas_call x2, Pallas kernels: 5.21 us -> 4.16 us  [the longest x1 3.58 us: flows(): pl.pallas_call(flows_kernel, out_shape=jax.ShapeDtypeStruct((8, PATCH), F...]
    pallas_call x1, Pallas kernels: 1.6 us -> 0.79 us  [compose(): pl.pallas_call(compose_kernel, out_shape=jax.ShapeDtypeStruct((1, 1, 1, 2...]
    ppermute x1, starting transfers between devices: 0.06 us -> 0.56 us  [to_next(): lax.ppermute(value, 'gz', [(i, (i + 1) % count) for i in range(count)])]
  transfers between devices with their start and end apart: 13 -> 13, of which waited for: 7 -> 6; matrix products, arithmetic and copies ran while one was open for 2% -> 2% of each run, Pallas kernels for 3% -> 6%
where the time goes in v2:
time: 38.8 us; the launch traced here: 38.6 us
  starting transfers between devices  13.7 us (35%)
  Pallas kernels  11 us (28%)
  waiting for transfers between devices  9.44 us (24%)
  local copies, waits for them, and re-layouts  2.74 us (7%)
  other arithmetic  0.94 us (2%)
  between operations  0.76 us (2%)
    ppermute x8, starting transfers between devices, swap_pairs(): return lax.ppermute(value, (spare, axis) if flip else (axis, spare), moves)  9.84 us
    ppermute x8, waiting for transfers between devices, swap_pairs(): return lax.ppermute(value, (spare, axis) if flip else (axis, spare), moves)  4.71 us
    pallas_call x1, Pallas kernels, relax(): pl.pallas_call(relax_kernel, out_shape=(jax.ShapeDtypeStruct((1, 2, nodes...  4.34 us
    pallas_call x1, Pallas kernels, flows(): pl.pallas_call(flows_kernel, out_shape=jax.ShapeDtypeStruct((8, PATCH), F...  3.58 us
    ppermute x3, waiting for transfers between devices, local(): lax.ppermute(landing, 'gz', [(i, i ^ code) for i in range(sections)])  2.89 us
    unnamed x22, local copies, waits for them, and re-layouts  2.66 us
    ppermute x3, starting transfers between devices, local(): lax.ppermute(landing, 'gz', [(i, i ^ code) for i in range(sections)])  2.08 us
    ppermute x1, waiting for transfers between devices, to_next(): return lax.ppermute(value, ('gz', 'ty'), moves)  1.84 us
  transfers between devices with their start and end apart: 13, of which 6 were waited for; matrix products, arithmetic and copies ran while one was open for 2% of the time, Pallas kernels for 6%

profile of v2, /device:TPU:0, one launch (start us, length us, event | category | flops | bytes accessed | tf_op | source)
XLA Modules:
  0.0 38.6 jit_solution(13061382039993582879)
XLA Ops:
  0.6 0.5 %collective-permute-start.1 = (bf16[512,512]{1,0:T(8,128)(2,1)}, bf16[512,512]{1,0:T(8,128)(2,1)S(1)}, u32[]{:S(2)}, u32[]{:S(2)}) collective-permute-start(bf16[512,512]{1,0:T(8,128)(2,1)} %bitcast.2), channel_id=1, source_target_pairs={{0,8},{4,12},{8,0},{12,4},{16,24},{20,28},{24,16},{28,20},{1,9},{5... | collective-permute-start | bytes 1572872 | tf_op jit(solution)/shard_map/ppermute | solution.py:457
  1.2 2.6 %collective-permute-start.2 = (f32[128,128]{1,0:T(8,128)}, f32[128,128]{1,0:T(8,128)S(1)}, u32[]{:S(2)}, u32[]{:S(2)}) collective-permute-start(f32[128,128]{1,0:T(8,128)} %bitcast.5), channel_id=1, source_target_pairs={{0,4},{8,12},{16,20},{24,28},{4,0},{12,8},{20,16},{28,24},{1,5},{9... | collective-permute-start | bytes 196616 | tf_op jit(solution)/shard_map/ppermute | solution.py:457
  3.8 2.8 %collective-permute-done.2 = f32[128,128]{1,0:T(8,128)S(1)} collective-permute-done((f32[128,128]{1,0:T(8,128)}, f32[128,128]{1,0:T(8,128)S(1)}, u32[]{:S(2)}, u32[]{:S(2)}) %collective-permute-start.2) | collective-permute-done | bytes 65568 | tf_op jit(solution)/shard_map/ppermute | solution.py:457
  6.7 0.9 %pad_maximum_fusion.own_ref = f32[192,128]{1,0:T(8,128)S(1)} fusion(f32[32,128]{1,0:T(8,128)S(1)} %get-tuple-element.29, f32[128,128]{1,0:T(8,128)} %bitcast.6, f32[32,128]{1,0:T(8,128)S(1)} %get-tuple-element.28), kind=kLoop, calls=%fused_computation | loop fusion | flops 49152 | bytes 196608 | tf_op jit(solution)/shard_map/concatenate | solution.py:504
  7.5 1.9 %collective-permute-start.3 = (f32[192,128]{1,0:T(8,128)S(1)}, f32[192,128]{1,0:T(8,128)S(1)}, u32[]{:S(2)}, u32[]{:S(2)}) collective-permute-start(f32[192,128]{1,0:T(8,128)S(1)} %pad_maximum_fusion.own_ref), channel_id=1, source_target_pairs={{0,1},{8,9},{16,17},{24,25},{1,0},{9,8},{17,16},{25,24},{2,3},{10,... | collective-permute-start | bytes 294920 | tf_op jit(solution)/shard_map/ppermute | solution.py:457
  9.4 1.0 %copy-done = bf16[1,512,512]{2,1,0:T(8,128)(2,1)S(1)} copy-done((bf16[1,512,512]{2,1,0:T(8,128)(2,1)S(1)}, bf16[1,512,512]{2,1,0:T(8,128)(2,1)}, u32[]{:S(2)}) %copy-start) | copy-done | bytes 524312
  10.5 1.0 %copy-done.2 = bf16[4,256,256]{2,1,0:T(8,128)(2,1)S(1)} copy-done((bf16[4,256,256]{2,1,0:T(8,128)(2,1)S(1)}, bf16[4,256,256]{2,1,0:T(8,128)(2,1)}, u32[]{:S(2)}) %copy-start.2) | copy-done | bytes 524312
  11.5 1.7 %spectra.1 = (f32[128,2048]{1,0:T(8,128)S(1)}, f32[128,2048]{1,0:T(8,128)S(1)}) custom-call(bf16[512,512]{1,0:T(8,128)(2,1)S(1)} %bitcast.4, bf16[512,512]{1,0:T(8,128)(2,1)S(1)} %collective-permute-done.1.near_ref, bf16[4,256,256]{2,1,0:T(8,128)(2,1)S(1)} %copy-done.2, bf16[2,128,384]{2,1,0:T(8,128)(2,1)S(1)} %copy-done.7), custom_call_target="tpu_custom_call" | custom-call | flops 3000000000 | bytes 3145728 | tf_op jit(solution)/shard_map/spectra/pallas_call | solution.py:205
  13.2 0.6 %gains.1 = (f32[24,8,384]{2,1,0:T(8,128)S(1)}, f32[24,8,384]{2,1,0:T(8,128)S(1)}) custom-call(f32[192,128]{1,0:T(8,128)S(1)} %pad_maximum_fusion.own_ref, f32[192,128]{1,0:T(8,128)S(1)} %collective-permute-done.3.even_ref, f32[192,128]{1,0:T(8,128)S(1)} %collective-permute-done.4.odd_ref, bf16[384,384]{1,0:T(8,128)(2,1)S(1)} %copy-done.4, ...), custom_call_target="tpu_custom_call" | custom-call | flops 1000000000 | bytes 1048576 | tf_op jit(solution)/shard_map/gains/pallas_call | solution.py:316
  13.8 0.4 copy-done.1
  14.4 3.6 %flows.1 = f32[8,128]{1,0:T(8,128)S(1)} custom-call(bf16[512,512]{1,0:T(8,128)(2,1)S(1)} %collective-permute-done.far_ref, bf16[512,512]{1,0:T(8,128)(2,1)S(1)} %copy-done.1, f32[128,2048]{1,0:T(8,128)S(1)} %get-tuple-element.22.own_spec, f32[128,2048]{1,0:T(8,128)S(1)} %get-tuple-element.23.near_spec, bf16[4,256,256]{2,1,0:T(8,128)(2,1)S(1)} %copy-done.3, ...), custom_call_target="tpu_custom_call" | custom-call | flops 4000000000 | bytes 3145728 | tf_op jit(solution)/shard_map/flows/pallas_call | solution.py:218
  18.0 0.6 %collective-permute-start.7 = (f32[8,128]{1,0:T(8,128)S(1)}, f32[8,128]{1,0:T(8,128)S(1)}, u32[]{:S(2)}, u32[]{:S(2)}) collective-permute-start(f32[8,128]{1,0:T(8,128)S(1)} %flows.1), channel_id=1, source_target_pairs={{0,8},{8,16},{16,24},{24,0},{1,9},{9,17},{17,25},{25,1},{2,10},{10... | collective-permute-start | bytes 12296 | tf_op jit(solution)/shard_map/ppermute | solution.py:474
  18.6 1.5 %collective-permute-start.5 = (f32[8,128]{1,0:T(8,128)S(1)}, f32[8,128]{1,0:T(8,128)S(1)}, u32[]{:S(2)}, u32[]{:S(2)}) collective-permute-start(f32[8,128]{1,0:T(8,128)S(1)} %flows.1), channel_id=1, source_target_pairs={{0,4},{8,12},{16,20},{24,28},{4,0},{12,8},{20,16},{28,24},{1,5},{9... | collective-permute-start | bytes 12296 | tf_op jit(solution)/shard_map/ppermute | solution.py:457
  20.1 1.2 %collective-permute-start.6 = (f32[8,128]{1,0:T(8,128)S(1)}, f32[8,128]{1,0:T(8,128)S(1)}, u32[]{:S(2)}, u32[]{:S(2)}) collective-permute-start(f32[8,128]{1,0:T(8,128)S(1)} %flows.1), channel_id=1, source_target_pairs={{0,12},{4,8},{8,20},{12,16},{16,28},{20,24},{24,4},{28,0},{1,13},{... | collective-permute-start | bytes 12296 | tf_op jit(solution)/shard_map/ppermute | solution.py:476
  21.4 0.9 %collective-permute-done.5 = f32[8,128]{1,0:T(8,128)S(1)} collective-permute-done((f32[8,128]{1,0:T(8,128)S(1)}, f32[8,128]{1,0:T(8,128)S(1)}, u32[]{:S(2)}, u32[]{:S(2)}) %collective-permute-start.5) | collective-permute-done | bytes 4128 | tf_op jit(solution)/shard_map/ppermute | solution.py:457
  22.2 1.8 %collective-permute-done.6 = f32[8,128]{1,0:T(8,128)S(1)} collective-permute-done((f32[8,128]{1,0:T(8,128)S(1)}, f32[8,128]{1,0:T(8,128)S(1)}, u32[]{:S(2)}, u32[]{:S(2)}) %collective-permute-start.6) | collective-permute-done | bytes 4128 | tf_op jit(solution)/shard_map/ppermute | solution.py:476
  24.1 2.7 %collective-permute-start.8 = (f32[8,128]{1,0:T(8,128)S(1)}, f32[8,128]{1,0:T(8,128)S(1)}, u32[]{:S(2)}, u32[]{:S(2)}) collective-permute-start(f32[8,128]{1,0:T(8,128)S(1)} %maximum_maximum_fusion.own_ref), channel_id=1, source_target_pairs={{0,1},{8,9},{16,17},{24,25},{1,0},{9,8},{17,16},{25,24},{2,3},{10,... | collective-permute-start | bytes 12296 | tf_op jit(solution)/shard_map/ppermute | solution.py:457
  26.8 0.6 %collective-permute-start.9 = (f32[8,128]{1,0:T(8,128)S(1)}, f32[8,128]{1,0:T(8,128)S(1)}, u32[]{:S(2)}, u32[]{:S(2)}) collective-permute-start(f32[8,128]{1,0:T(8,128)S(1)} %maximum_maximum_fusion.own_ref), channel_id=1, source_target_pairs={{0,8},{8,0},{16,24},{24,16},{1,2},{9,10},{17,18},{25,26},{2,1},{10... | collective-permute-start | bytes 12296 | tf_op jit(solution)/shard_map/ppermute | solution.py:457
  27.4 1.0 %collective-permute-done.8.even_ref = f32[8,128]{1,0:T(8,128)S(1)} collective-permute-done((f32[8,128]{1,0:T(8,128)S(1)}, f32[8,128]{1,0:T(8,128)S(1)}, u32[]{:S(2)}, u32[]{:S(2)}) %collective-permute-start.8) | collective-permute-done | bytes 4128 | tf_op jit(solution)/shard_map/ppermute | solution.py:457
  28.4 4.3 %relax.1 = (f32[1,2,128,128]{3,2,1,0:T(8,128)}, f32[8,128]{1,0:T(8,128)S(1)}) custom-call(f32[8,128]{1,0:T(8,128)S(1)} %maximum_maximum_fusion.own_ref, f32[8,128]{1,0:T(8,128)S(1)} %collective-permute-done.8.even_ref, f32[8,128]{1,0:T(8,128)S(1)} %collective-permute-done.9.odd_ref, f32[24,8,384]{2,1,0:T(8,128)S(1)} %get-tuple-element.24.gain_ref, ...), custom_call_target="tpu_custom_call" | custom-call | flops 4000000000 | bytes 3145728 | tf_op jit(solution)/shard_map/relax/pallas_call | solution.py:395
  32.9 1.8 %collective-permute-start.11 = (f32[8,128]{1,0:T(8,128)S(1)}, f32[8,128]{1,0:T(8,128)S(1)}, u32[]{:S(2)}, u32[]{:S(2)}) collective-permute-start(f32[8,128]{1,0:T(8,128)S(1)} %get-tuple-element.27.refs_0_), channel_id=1, source_target_pairs={{0,16},{8,24},{16,0},{24,8},{1,17},{9,25},{17,1},{25,9},{2,18},{10... | collective-permute-start | bytes 12296 | tf_op jit(solution)/shard_map/ppermute | solution.py:515
  34.9 1.7 %collective-permute-done.11.refs_2_ = f32[8,128]{1,0:T(8,128)S(1)} collective-permute-done((f32[8,128]{1,0:T(8,128)S(1)}, f32[8,128]{1,0:T(8,128)S(1)}, u32[]{:S(2)}, u32[]{:S(2)}) %collective-permute-start.11) | collective-permute-done | bytes 4128 | tf_op jit(solution)/shard_map/ppermute | solution.py:515
  36.5 1.2 %collective-permute-done.12.refs_3_ = f32[8,128]{1,0:T(8,128)S(1)} collective-permute-done((f32[8,128]{1,0:T(8,128)S(1)}, f32[8,128]{1,0:T(8,128)S(1)}, u32[]{:S(2)}, u32[]{:S(2)}) %collective-permute-start.12) | collective-permute-done | bytes 4128 | tf_op jit(solution)/shard_map/ppermute | solution.py:515
  37.8 0.8 %compose.1 = f32[1,1,1,2,128]{4,3,2,1,0:T(2,128)} custom-call(f32[8,128]{1,0:T(8,128)S(1)} %get-tuple-element.27.refs_0_, f32[8,128]{1,0:T(8,128)S(1)} %collective-permute-done.10.refs_1_, f32[8,128]{1,0:T(8,128)S(1)} %collective-permute-done.11.refs_2_, f32[8,128]{1,0:T(8,128)S(1)} %collective-permute-done.12.refs_3_), custom_call_target="tpu_custom_call" | custom-call | tf_op jit(solution)/shard_map/compose/pallas_call | solution.py:433
  (36 shorter events, 0.7 us)
Async XLA Ops:
  0.6 8.8 %copy-start.7 = (bf16[2,128,384]{2,1,0:T(8,128)(2,1)S(1)}, bf16[2,128,384]{2,1,0:T(8,128)(2,1)}, u32[]{:S(2)}) copy-start(bf16[2,128,384]{2,1,0:T(8,128)(2,1)} %constant.28.clone.lefts_ref) | copy-start | bytes 589828
  0.6 6.9 %collective-permute-start.1 = (bf16[512,512]{1,0:T(8,128)(2,1)}, bf16[512,512]{1,0:T(8,128)(2,1)S(1)}, u32[]{:S(2)}, u32[]{:S(2)}) collective-permute-start(bf16[512,512]{1,0:T(8,128)(2,1)} %bitcast.2), channel_id=1, source_target_pairs={{0,8},{4,12},{8,0},{12,4},{16,24},{20,28},{24,16},{28,20},{1,9},{5... | collective-permute-start | bytes 1572872 | tf_op jit(solution)/shard_map/ppermute | solution.py:457
  1.2 5.5 %collective-permute-start.2 = (f32[128,128]{1,0:T(8,128)}, f32[128,128]{1,0:T(8,128)S(1)}, u32[]{:S(2)}, u32[]{:S(2)}) collective-permute-start(f32[128,128]{1,0:T(8,128)} %bitcast.5), channel_id=1, source_target_pairs={{0,4},{8,12},{16,20},{24,28},{4,0},{12,8},{20,16},{28,24},{1,5},{9... | collective-permute-start | bytes 196616 | tf_op jit(solution)/shard_map/ppermute | solution.py:457
  3.8 10.1 %collective-permute-start = (bf16[512,512]{1,0:T(8,128)(2,1)}, bf16[512,512]{1,0:T(8,128)(2,1)S(1)}, u32[]{:S(2)}, u32[]{:S(2)}) collective-permute-start(bf16[512,512]{1,0:T(8,128)(2,1)} %bitcast.3), channel_id=1, source_target_pairs={{0,4},{4,0},{8,16},{12,20},{16,8},{20,12},{24,28},{28,24},{1,5},{5... | collective-permute-start | bytes 1572872 | tf_op jit(solution)/shard_map/ppermute | solution.py:457
  6.7 6.6 %copy-start.10 = (s32[1,384]{1,0:T(1,128)S(1)}, s32[1,384]{1,0:T(1,128)}, u32[]{:S(2)}) copy-start(s32[1,384]{1,0:T(1,128)} %constant.30.clone.ring_ref) | copy-start | bytes 4612
  7.5 5.7 %collective-permute-start.3 = (f32[192,128]{1,0:T(8,128)S(1)}, f32[192,128]{1,0:T(8,128)S(1)}, u32[]{:S(2)}, u32[]{:S(2)}) collective-permute-start(f32[192,128]{1,0:T(8,128)S(1)} %pad_maximum_fusion.own_ref), channel_id=1, source_target_pairs={{0,1},{8,9},{16,17},{24,25},{1,0},{9,8},{17,16},{25,24},{2,3},{10,... | collective-permute-start | bytes 294920 | tf_op jit(solution)/shard_map/ppermute | solution.py:457
  9.4 3.8 %collective-permute-start.4 = (f32[192,128]{1,0:T(8,128)S(1)}, f32[192,128]{1,0:T(8,128)S(1)}, u32[]{:S(2)}, u32[]{:S(2)}) collective-permute-start(f32[192,128]{1,0:T(8,128)S(1)} %pad_maximum_fusion.own_ref), channel_id=1, source_target_pairs={{0,8},{8,0},{16,24},{24,16},{1,2},{9,10},{17,18},{25,26},{2,1},{10... | collective-permute-start | bytes 294920 | tf_op jit(solution)/shard_map/ppermute | solution.py:457
  9.4 1.0 %copy-start = (bf16[1,512,512]{2,1,0:T(8,128)(2,1)S(1)}, bf16[1,512,512]{2,1,0:T(8,128)(2,1)}, u32[]{:S(2)}) copy-start(bf16[1,512,512]{2,1,0:T(8,128)(2,1)} %param.11) | copy-start | bytes 1572868
  10.5 1.0 %copy-start.2 = (bf16[4,256,256]{2,1,0:T(8,128)(2,1)S(1)}, bf16[4,256,256]{2,1,0:T(8,128)(2,1)}, u32[]{:S(2)}) copy-start(bf16[4,256,256]{2,1,0:T(8,128)(2,1)} %constant.27.clone.rights_ref) | copy-start | bytes 1572868
  11.5 1.7 %copy-start.4 = (bf16[384,384]{1,0:T(8,128)(2,1)S(1)}, bf16[384,384]{1,0:T(8,128)(2,1)}, u32[]{:S(2)}) copy-start(bf16[384,384]{1,0:T(8,128)(2,1)} %constant.29.clone.into_ref) | copy-start | bytes 884740
  13.2 1.0 %copy-start.1 = (bf16[512,512]{1,0:T(8,128)(2,1)S(1)}, bf16[512,512]{1,0:T(8,128)(2,1)}, u32[]{:S(2)}) copy-start(bf16[512,512]{1,0:T(8,128)(2,1)} %edge_ref.1) | copy-start | bytes 1572868
  13.2 1.2 %copy-start.3 = (bf16[4,256,256]{2,1,0:T(8,128)(2,1)S(1)}, bf16[4,256,256]{2,1,0:T(8,128)(2,1)}, u32[]{:S(2)}) copy-start(bf16[4,256,256]{2,1,0:T(8,128)(2,1)} %constant.27.clone.rights_ref) | copy-start | bytes 1572868
  14.4 14.0 %copy-start.5 = (f32[144,384]{1,0:T(8,128)S(1)}, f32[144,384]{1,0:T(8,128)}, u32[]{:S(2)}) copy-start(f32[144,384]{1,0:T(8,128)} %constant.32.clone.right_ref) | copy-start | bytes 663556
  14.4 14.0 %copy-start.6 = (bf16[384,256]{1,0:T(8,128)(2,1)S(1)}, bf16[384,256]{1,0:T(8,128)(2,1)}, u32[]{:S(2)}) copy-start(bf16[384,256]{1,0:T(8,128)(2,1)} %constant.34.clone.out_table_ref) | copy-start | bytes 589828
  14.4 14.0 %copy-start.8 = (bf16[192,144]{1,0:T(8,128)(2,1)S(1)}, bf16[192,144]{1,0:T(8,128)(2,1)}, u32[]{:S(2)}) copy-start(bf16[192,144]{1,0:T(8,128)(2,1)} %constant.31.clone.left_ref) | copy-start | bytes 165892
  18.0 3.4 %collective-permute-start.7 = (f32[8,128]{1,0:T(8,128)S(1)}, f32[8,128]{1,0:T(8,128)S(1)}, u32[]{:S(2)}, u32[]{:S(2)}) collective-permute-start(f32[8,128]{1,0:T(8,128)S(1)} %flows.1), channel_id=1, source_target_pairs={{0,8},{8,16},{16,24},{24,0},{1,9},{9,17},{17,25},{25,1},{2,10},{10... | collective-permute-start | bytes 12296 | tf_op jit(solution)/shard_map/ppermute | solution.py:474
  18.6 3.6 %collective-permute-start.5 = (f32[8,128]{1,0:T(8,128)S(1)}, f32[8,128]{1,0:T(8,128)S(1)}, u32[]{:S(2)}, u32[]{:S(2)}) collective-permute-start(f32[8,128]{1,0:T(8,128)S(1)} %flows.1), channel_id=1, source_target_pairs={{0,4},{8,12},{16,20},{24,28},{4,0},{12,8},{20,16},{28,24},{1,5},{9... | collective-permute-start | bytes 12296 | tf_op jit(solution)/shard_map/ppermute | solution.py:457
  20.1 3.9 %collective-permute-start.6 = (f32[8,128]{1,0:T(8,128)S(1)}, f32[8,128]{1,0:T(8,128)S(1)}, u32[]{:S(2)}, u32[]{:S(2)}) collective-permute-start(f32[8,128]{1,0:T(8,128)S(1)} %flows.1), channel_id=1, source_target_pairs={{0,12},{4,8},{8,20},{12,16},{16,28},{20,24},{24,4},{28,0},{1,13},{... | collective-permute-start | bytes 12296 | tf_op jit(solution)/shard_map/ppermute | solution.py:476
  24.1 4.4 %copy-start.9 = (s32[1,384]{1,0:T(1,128)S(1)}, s32[1,384]{1,0:T(1,128)}, u32[]{:S(2)}) copy-start(s32[1,384]{1,0:T(1,128)} %constant.33.clone.part_ref) | copy-start | bytes 4612
  24.1 4.3 %collective-permute-start.8 = (f32[8,128]{1,0:T(8,128)S(1)}, f32[8,128]{1,0:T(8,128)S(1)}, u32[]{:S(2)}, u32[]{:S(2)}) collective-permute-start(f32[8,128]{1,0:T(8,128)S(1)} %maximum_maximum_fusion.own_ref), channel_id=1, source_target_pairs={{0,1},{8,9},{16,17},{24,25},{1,0},{9,8},{17,16},{25,24},{2,3},{10,... | collective-permute-start | bytes 12296 | tf_op jit(solution)/shard_map/ppermute | solution.py:457
  26.8 1.6 %collective-permute-start.9 = (f32[8,128]{1,0:T(8,128)S(1)}, f32[8,128]{1,0:T(8,128)S(1)}, u32[]{:S(2)}, u32[]{:S(2)}) collective-permute-start(f32[8,128]{1,0:T(8,128)S(1)} %maximum_maximum_fusion.own_ref), channel_id=1, source_target_pairs={{0,8},{8,0},{16,24},{24,16},{1,2},{9,10},{17,18},{25,26},{2,1},{10... | collective-permute-start | bytes 12296 | tf_op jit(solution)/shard_map/ppermute | solution.py:457
  32.8 2.1 %collective-permute-start.10 = (f32[8,128]{1,0:T(8,128)S(1)}, f32[8,128]{1,0:T(8,128)S(1)}, u32[]{:S(2)}, u32[]{:S(2)}) collective-permute-start(f32[8,128]{1,0:T(8,128)S(1)} %get-tuple-element.27.refs_0_), channel_id=1, source_target_pairs={{0,8},{8,0},{16,24},{24,16},{1,9},{9,1},{17,25},{25,17},{2,10},{10... | collective-permute-start | bytes 12296 | tf_op jit(solution)/shard_map/ppermute | solution.py:515
  32.9 3.6 %collective-permute-start.11 = (f32[8,128]{1,0:T(8,128)S(1)}, f32[8,128]{1,0:T(8,128)S(1)}, u32[]{:S(2)}, u32[]{:S(2)}) collective-permute-start(f32[8,128]{1,0:T(8,128)S(1)} %get-tuple-element.27.refs_0_), channel_id=1, source_target_pairs={{0,16},{8,24},{16,0},{24,8},{1,17},{9,25},{17,1},{25,9},{2,18},{10... | collective-permute-start | bytes 12296 | tf_op jit(solution)/shard_map/ppermute | solution.py:515
  34.7 3.0 %collective-permute-start.12 = (f32[8,128]{1,0:T(8,128)S(1)}, f32[8,128]{1,0:T(8,128)S(1)}, u32[]{:S(2)}, u32[]{:S(2)}) collective-permute-start(f32[8,128]{1,0:T(8,128)S(1)} %get-tuple-element.27.refs_0_), channel_id=1, source_target_pairs={{0,24},{8,16},{16,8},{24,0},{1,25},{9,17},{17,9},{25,1},{2,26},{10... | collective-permute-start | bytes 12296 | tf_op jit(solution)/shard_map/ppermute | solution.py:515

commit v3 on v2

--- a/solution.py
+++ b/solution.py
@@ -30,25 +30,26 @@
     gains = np.full(PATCH, 2.0)
     gains[0] = gains[HALF] = 1.0
     inverse = basis.T * gains / PATCH
-    forward_pair = np.zeros((2, PATCH, 2, 2, HALF))
-    inverse_pair = np.zeros((2, 2, HALF, 2, PATCH))
-    for side in range(2):
-        forward_pair[side, :, :, side] = basis.T.reshape(PATCH, 2, HALF)
-        inverse_pair[:, side, :, side] = inverse.T.reshape(2, HALF, PATCH)
-    forward_pair = forward_pair.reshape(2 * PATCH, 2 * PATCH)
-    inverse_pair = inverse_pair.reshape(2 * PATCH, 2 * PATCH)
-    right_high, right_low = split_table(forward_pair)
-    back_high, back_low = split_table(inverse_pair)
-    left_high, left_low = split_table(basis)
-    undo_high, undo_low = split_table(inverse / PATCH)
-    rights = np.stack([right_high, right_low, back_high, back_low])
-    lefts = np.stack(
-        [
-            np.concatenate([left_high, left_high, left_low], axis=1),
-            np.concatenate([undo_high, undo_high, undo_low], axis=1),
-        ]
-    )
-    return (rights, lefts)
+    tables = [part for table in (basis.T, inverse.T, basis, inverse / PATCH) for part in split_table(table)]
+    return jnp.asarray(np.stack(tables))
+
+
+def pair_tables(tables_ref):
+    lower = lax.broadcasted_iota(jnp.int32, (PATCH, PATCH), 1) < HALF
+    forwards, inverses = [], []
+    for index in range(2):
+        table = tables_ref[index].astype(F32)
+        turned = pltpu.roll(table, HALF, 1)
+        first = jnp.concatenate([jnp.where(lower, table, 0.0), jnp.where(lower, turned, 0.0)], axis=1)
+        second = jnp.concatenate([jnp.where(lower, 0.0, turned), jnp.where(lower, 0.0, table)], axis=1)
+        forwards.append(jnp.concatenate([first, second], axis=0).astype(BF16))
+        table = tables_ref[2 + index]
+        empty = jnp.zeros((HALF, PATCH), BF16)
+        rows = []
+        for part in (table[:HALF], table[HALF:]):
+            rows += [jnp.concatenate([part, empty], axis=1), jnp.concatenate([empty, part], axis=1)]
+        inverses.append(jnp.concatenate(rows, axis=0))
+    return forwards + inverses
 
 
 def halves(value):
@@ -60,8 +61,9 @@
     return jnp.dot(left, right, preferred_element_type=F32)
 
 
-def left_transform(table, value):
+def left_transform(table_high, table_low, value):
     high, low = halves(value)
+    table = jnp.concatenate([table_high, table_high, table_low], axis=1)
     return dot(table, jnp.concatenate([high, low, high], axis=0))
 
 
@@ -115,19 +117,36 @@
     return jnp.concatenate([value[i : i + PATCH] for i in range(0, value.shape[0], PATCH)], axis=1)
 
 
-def forward(pixels, rights_ref, lefts_ref):
-    right = dot(pixels, rights_ref[0]) + dot(pixels, rights_ref[1])
-    return left_transform(lefts_ref[0], side_by_side(right))
-
-
-def spectra_kernel(own_ref, near_ref, rights_ref, lefts_ref, own_out, near_out):
-    for image, out in ((own_ref, own_out), (near_ref, near_out)):
-        pixels = jnp.concatenate([image[window] for window in windows(*image.shape)], axis=0)
-        out[...] = forward(pixels, rights_ref, lefts_ref)
+def forward(pixels, pairs, tables_ref):
+    right = dot(pixels, pairs[0]) + dot(pixels, pairs[1])
+    return left_transform(tables_ref[4], tables_ref[5], side_by_side(right))
+
+
+def image_spectra(image_ref, pairs, tables_ref):
+    pixels = jnp.concatenate([image_ref[window] for window in windows(*image_ref.shape)], axis=0)
+    return forward(pixels, pairs, tables_ref)
+
+
+def near_kernel(image_ref, tables_ref, spec_out, pairs_out):
+    pairs = pair_tables(tables_ref)
+    for index, pair in enumerate(pairs):
+        pairs_out[index] = pair
+    spec_out[...] = image_spectra(image_ref, pairs, tables_ref)
+
+
+def own_kernel(image_ref, pairs_ref, tables_ref, spec_out):
+    spec_out[...] = image_spectra(image_ref, pairs_ref, tables_ref)
+
+
+def rows_kernel(up_ref, own_ref, down_ref, out_ref):
+    nodes = own_ref.shape[0]
+    out_ref[:SWEEPS] = up_ref[nodes - SWEEPS :]
+    out_ref[SWEEPS : SWEEPS + nodes] = own_ref[...]
+    out_ref[SWEEPS + nodes :] = down_ref[:SWEEPS]
 
 
 def flows_kernel(
-    far_ref, edge_ref, own_spec, near_spec, rights_ref, lefts_ref, out_ref, stats_ref
+    far_ref, edge_ref, own_spec, near_spec, rights_ref, tables_ref, out_ref, stats_ref
 ):
     wide = 2 * PATCH
     spots = windows(*far_ref.shape)
@@ -138,7 +157,7 @@
     pixels = jnp.concatenate(
         [jnp.where(at_edge, edge_ref[spot].astype(F32), far_ref[spot].astype(F32)).astype(BF16) for spot in spots], axis=0
     )
-    spec = forward(pixels, rights_ref, lefts_ref)
+    spec = forward(pixels, rights_ref, tables_ref)
     products = []
     for block in range(blocks):
         lanes = slice(block * wide, (block + 1) * wide)
@@ -148,7 +167,7 @@
         products.append(cross(operand, jnp.where(at_even, near, far)))
     high, low = halves(jnp.concatenate(products, axis=0))
     back = dot(high, rights_ref[2]) + dot(low, rights_ref[2]) + dot(high, rights_ref[3])
-    scores = left_transform(lefts_ref[1], side_by_side(back))
+    scores = left_transform(tables_ref[6], tables_ref[7], side_by_side(back))
     groups = scores.reshape(PATCH // 8, 8, 2 * blocks * wide)
     peak = jnp.max(groups, axis=0)
     total = jnp.zeros_like(peak)
@@ -199,21 +218,48 @@
 PARAMS = pltpu.CompilerParams(vmem_limit_bytes=40 * 2**20)
 
 
-def spectra(own, near, rights, lefts):
-    count = own.shape[0] // PATCH * (own.shape[1] // PATCH)
-    spec = jax.ShapeDtypeStruct((PATCH, count * PATCH), F32)
-    return pl.pallas_call(
-        spectra_kernel,
-        out_shape=(spec, spec),
-        in_specs=[VMEM] * 4,
+def spec_shape(image):
+    return jax.ShapeDtypeStruct((PATCH, image.shape[0] // PATCH * image.shape[1]), F32)
+
+
+def near_spectra(near, tables):
+    pairs = jax.ShapeDtypeStruct((4, 2 * PATCH, 2 * PATCH), BF16)
+    return pl.pallas_call(
+        near_kernel,
+        out_shape=(spec_shape(near), pairs),
+        in_specs=[VMEM] * 2,
         out_specs=(VMEM, VMEM),
         compiler_params=PARAMS,
-        cost_estimate=pl.CostEstimate(flops=3 * 10**9, bytes_accessed=3 * 2**20, transcendentals=0),
-        name="spectra",
-    )(own, near, rights, lefts)
-
-
-def flows(far, edge, own_spec, near_spec, rights, lefts):
+        cost_estimate=pl.CostEstimate(flops=2 * 10**9, bytes_accessed=2 * 2**20, transcendentals=0),
+        name="near_spectra",
+    )(near, tables)
+
+
+def own_spectra(own, pairs, tables):
+    return pl.pallas_call(
+        own_kernel,
+        out_shape=spec_shape(own),
+        in_specs=[VMEM] * 3,
+        out_specs=VMEM,
+        compiler_params=PARAMS,
+        cost_estimate=pl.CostEstimate(flops=10**9, bytes_accessed=2 * 2**20, transcendentals=0),
+        name="own_spectra",
+    )(own, pairs, tables)
+
+
+def anchor_rows(up, own, down):
+    nodes = own.shape[0]
+    return pl.pallas_call(
+        rows_kernel,
+        out_shape=jax.ShapeDtypeStruct((nodes + 2 * SWEEPS, nodes), F32),
+        in_specs=[VMEM] * 3,
+        out_specs=VMEM,
+        compiler_params=pltpu.CompilerParams(vmem_limit_bytes=2**20),
+        name="anchor_rows",
+    )(up, own, down)
+
+
+def flows(far, edge, own_spec, near_spec, pairs, tables):
     patches = far.shape[0] // PATCH * (far.shape[1] // PATCH)
     return pl.pallas_call(
         flows_kernel,
@@ -224,7 +270,7 @@
         compiler_params=PARAMS,
         cost_estimate=pl.CostEstimate(flops=4 * 10**9, bytes_accessed=3 * 2**20, transcendentals=0),
         name="flows",
-    )(far, edge, own_spec, near_spec, rights, lefts)
+    )(far, edge, own_spec, near_spec, pairs, tables)
 
 
 def spread_weights(nodes, patches):
@@ -326,11 +372,11 @@
 
 
 def relax_kernel(
-    own_ref, even_ref, odd_ref, gain_ref, pull_ref, left_ref, right_ref, part_ref, out_table_ref,
-    mesh_ref, landing_ref, work_ref, base_ref, rows_ref,
+    own_ref, even_ref, odd_ref, gain_ref, pull_ref, left_ref, right_ref, part_ref, ones_ref, cols_table_ref, rows_table_ref,
+    work_ref, landing_ref, base_ref,
 ):
     strips, _, lanes = work_ref.shape
-    nodes = mesh_ref.shape[2]
+    nodes = landing_ref.shape[1]
     patches = left_ref.shape[1] // 9
     before, after = tiles_beside(even_ref, odd_ref)
     rows = [before[:3], own_ref[:3], after[:3]]
@@ -371,17 +417,20 @@
         return carry
 
     lax.fori_loop(0, SWEEPS, sweep, 0, unroll=8)
-    final = permuted(work_ref[...].reshape(strips * 8, lanes), out_table_ref[...])
-    for strip in range(strips):
-        for part in range(2):
-            rows_ref[part, pl.ds(strip, 8, strips), :] = final[8 * strip : 8 * strip + 8, part * nodes : (part + 1) * nodes]
-    down = rows_ref[0, SWEEPS : SWEEPS + nodes]
-    across = rows_ref[1, SWEEPS : SWEEPS + nodes]
-    mesh_ref[0, 0] = down
-    mesh_ref[0, 1] = across
-    share = 1.0 / nodes
-    down_mean = jnp.sum(jnp.transpose(down), axis=0, keepdims=True) * share
-    across_mean = jnp.sum(across, axis=0, keepdims=True) * share
+    mesh = work_ref[...].reshape(strips * 8, lanes)
+    ones = ones_ref[...]
+    sums = None
+    for piece in range(3):
+        part = mesh.astype(BF16)
+        term = lax.dot_general(ones, part, (((1,), (1,)), ((), ())), preferred_element_type=F32)
+        sums = term if sums is None else sums + term
+        mesh = mesh - part.astype(F32)
+    down_mean = permuted(sums, rows_table_ref[...])[:1] / nodes
+    strip = lax.broadcasted_iota(jnp.int32, (strips, 8, lanes), 0)
+    row = lax.broadcasted_iota(jnp.int32, (strips, 8, lanes), 1) * strips + strip
+    kept = jnp.where((row >= SWEEPS) & (row < SWEEPS + nodes), work_ref[...], 0.0)
+    across = permuted(jnp.sum(kept, axis=0), cols_table_ref[...])
+    across_mean = jnp.sum(across, axis=0, keepdims=True) / nodes
     line = lax.broadcasted_iota(jnp.int32, landing_ref.shape, 0)
     ramp = lax.broadcasted_iota(jnp.int32, landing_ref.shape, 1).astype(F32)
     profile = jnp.where(line == 0, down_mean, across_mean)
@@ -390,21 +439,49 @@
 
 def relax(targets, weights, nodes, patches):
     left, right, part = target_tables(nodes, patches)
-    _, out_table, _ = ring_tables(nodes)
+    ring, ring_part = ring_nodes(nodes)
+    own = (ring >= 0) & (ring < nodes)
+    ones = np.broadcast_to(own & (ring_part == 0), (16, len(ring))).astype(BF16)
+    node = np.arange(nodes)[None]
+    cols_table = ((ring[:, None] == node) & (ring_part[:, None] == 1)).astype(BF16)
+    rows_table = (row_nodes(nodes)[:, None] == node).astype(BF16)
+    tables = map(jnp.asarray, (left, right, part, ones, cols_table, rows_table))
     shape = weights[0].shape
     return pl.pallas_call(
         relax_kernel,
-        out_shape=(
-            jax.ShapeDtypeStruct((1, 2, nodes, nodes), F32),
-            jax.ShapeDtypeStruct((8, nodes), F32),
-        ),
-        in_specs=[VMEM] * 9,
+        out_shape=(jax.ShapeDtypeStruct(shape, F32), jax.ShapeDtypeStruct((8, nodes), F32)),
+        in_specs=[VMEM] * 11,
         out_specs=(VMEM, VMEM),
-        scratch_shapes=[pltpu.VMEM(shape, F32)] * 2 + [pltpu.VMEM((2, shape[0] * 8, nodes), F32)],
+        scratch_shapes=[pltpu.VMEM(shape, F32)],
         compiler_params=PARAMS,
         cost_estimate=pl.CostEstimate(flops=4 * 10**9, bytes_accessed=3 * 2**20, transcendentals=0),
         name="relax",
-    )(*targets, *weights, *map(jnp.asarray, (left, right, part, out_table)))
+    )(*targets, *weights, *tables)
+
+
+def mesh_kernel(ring_ref, table_ref, mesh_ref, rows_ref):
+    strips, _, lanes = ring_ref.shape
+    nodes = mesh_ref.shape[2]
+    final = permuted(ring_ref[...].reshape(strips * 8, lanes), table_ref[...])
+    for strip in range(strips):
+        for part in range(2):
+            columns = slice(part * nodes, (part + 1) * nodes)
+            rows_ref[part, pl.ds(strip, 8, strips), :] = final[8 * strip : 8 * strip + 8, columns]
+    mesh_ref[0] = rows_ref[:, SWEEPS : SWEEPS + nodes]
+
+
+def natural_mesh(ring, nodes):
+    _, table, _ = ring_tables(nodes)
+    return pl.pallas_call(
+        mesh_kernel,
+        out_shape=jax.ShapeDtypeStruct((1, 2, nodes, nodes), F32),
+        in_specs=[VMEM] * 2,
+        out_specs=VMEM,
+        scratch_shapes=[pltpu.VMEM((2, ring.shape[0] * 8, nodes), F32)],
+        compiler_params=PARAMS,
+        cost_estimate=pl.CostEstimate(flops=10**9, bytes_accessed=2**20, transcendentals=0),
+        name="natural_mesh",
+    )(ring, jnp.asarray(table))
 
 
 def compose_kernel(*refs):
@@ -497,22 +574,25 @@
     own = images[0]
     patches = own.shape[0] // PATCH
     sections = lax.axis_size("gz")
-    rights, lefts = map(jnp.asarray, transform_tables())
+    tables = transform_tables()
     far = swap_pairs(own, "gz", 1, "ty")
     near = swap_pairs(own, "gz", 0, "ty")
     up, down = rows_beside(anchor[0])
-    rows = jnp.concatenate([up[nodes - SWEEPS :], anchor[0], down[:SWEEPS]], axis=0)
-    near, rows = lax.optimization_barrier((near, rows))
-    specs = spectra(own, near, rights, lefts)
+    near_spec, pairs = near_spectra(near, tables)
+    own_spec = own_spectra(own, pairs, tables)
+    up, down, own_spec = lax.optimization_barrier((up, down, own_spec))
+    rows = anchor_rows(up, anchor[0], down)
     weights = gains(rows, swap_pairs(rows, "tx", 0, "gz"), swap_pairs(rows, "tx", 1, "gz"), nodes)
-    far, weights, specs = lax.optimization_barrier((far, weights, specs))
-    flow = flows(far, boundary, *specs, rights, lefts)
+    far, own_spec, near_spec = lax.optimization_barrier((far, own_spec, near_spec))
+    flow = flows(far, boundary, own_spec, near_spec, pairs, tables)
     line = patch_targets(flow)
     targets = (line, swap_pairs(line, "tx", 0, "gz"), swap_pairs(line, "tx", 1, "gz"))
-    mesh, landing = relax(targets, weights, nodes, patches)
+    ring, landing = relax(targets, weights, nodes, patches)
     landings = [landing]
     for code in range(1, sections):
         landings.append(lax.ppermute(landing, "gz", [(i, i ^ code) for i in range(sections)]))
+    mesh = natural_mesh(ring, nodes)
+    mesh, landings = lax.optimization_barrier((mesh, landings))
     drift = compose(landings)
     return (mesh, drift)
 

time: 38.8 us -> 36 us (0.928)
  starting transfers between devices: 13.7 us -> 12 us
  local copies, waits for them, and re-layouts: 2.74 us -> 1.14 us
  Pallas kernels: 11 us -> 12.2 us
  other arithmetic: 0.94 us -> 0.08 us
    ppermute x8, waiting for transfers between devices: 4.71 us -> 6.66 us  [swap_pairs(): return lax.ppermute(value, (spare, axis) if flip else (axis, spare), moves)]
    ppermute x8, starting transfers between devices: 9.84 us -> 8.07 us  [swap_pairs(): return lax.ppermute(value, (spare, axis) if flip else (axis, spare), moves)]
    unnamed x22 -> x28, local copies, waits for them, and re-layouts: 2.66 us -> 1.06 us
    ppermute x1, waiting for transfers between devices: 1.84 us -> 0.53 us  [to_next(): return lax.ppermute(value, ('gz', 'ty'), moves)]
    pallas_call x2 -> x5, Pallas kernels: 6.01 us -> 7.31 us  [the longest x1 4.01 us: relax(): pl.pallas_call(relax_kernel, out_shape=(jax.ShapeDtypeStruct(shape, F32),...]
    ppermute x3, waiting for transfers between devices: 2.89 us -> 1.98 us  [local(): lax.ppermute(landing, 'gz', [(i, i ^ code) for i in range(sections)])]
    concatenate x1 -> x0, other arithmetic: 0.86 us -> none  [local(): jnp.concatenate([up[nodes - SWEEPS:], anchor[0], down[:SWEEPS]], axis=0)]
    ppermute x3, starting transfers between devices: 2.08 us -> 2.63 us  [local(): lax.ppermute(landing, 'gz', [(i, i ^ code) for i in range(sections)])]
  transfers between devices with their start and end apart: 13 -> 13, of which waited for: 6 -> 7; matrix products, arithmetic and copies ran while one was open for 2% -> 0% of each run, Pallas kernels for 6% -> 11%
where the time goes in v3:
time: 36 us; the launch traced here: 35.4 us
  Pallas kernels  12.2 us (34%)
  starting transfers between devices  12 us (33%)
  waiting for transfers between devices  9.17 us (25%)
  local copies, waits for them, and re-layouts  1.14 us (3%)
  between operations  0.81 us (2%)
    ppermute x8, starting transfers between devices, swap_pairs(): return lax.ppermute(value, (spare, axis) if flip else (axis, spare), moves)  8.07 us
    ppermute x8, waiting for transfers between devices, swap_pairs(): return lax.ppermute(value, (spare, axis) if flip else (axis, spare), moves)  6.66 us
    pallas_call x1, Pallas kernels, relax(): pl.pallas_call(relax_kernel, out_shape=(jax.ShapeDtypeStruct(shape, F32),...  4.01 us
    pallas_call x1, Pallas kernels, flows(): pl.pallas_call(flows_kernel, out_shape=jax.ShapeDtypeStruct((8, PATCH), F...  3.54 us
    ppermute x3, starting transfers between devices, local(): lax.ppermute(landing, 'gz', [(i, i ^ code) for i in range(sections)])  2.63 us
    ppermute x3, waiting for transfers between devices, local(): lax.ppermute(landing, 'gz', [(i, i ^ code) for i in range(sections)])  1.98 us
    ppermute x1, starting transfers between devices, to_next(): return lax.ppermute(value, ('gz', 'ty'), moves)  1.21 us
    pallas_call x1, Pallas kernels, near_spectra(): pl.pallas_call(near_kernel, out_shape=(spec_shape(near), pairs), in_specs...  1.19 us
  transfers between devices with their start and end apart: 13, of which 7 were waited for; matrix products, arithmetic and copies ran while one was open for 0% of the time, Pallas kernels for 11%

profile of v3, /device:TPU:0, one launch (start us, length us, event | category | flops | bytes accessed | tf_op | source)
XLA Modules:
  0.0 35.4 jit_solution(18105462162331795559)
XLA Ops:
  0.6 0.5 %collective-permute-start.2 = (bf16[512,512]{1,0:T(8,128)(2,1)}, bf16[512,512]{1,0:T(8,128)(2,1)S(1)}, u32[]{:S(2)}, u32[]{:S(2)}) collective-permute-start(bf16[512,512]{1,0:T(8,128)(2,1)} %bitcast.4), channel_id=1, source_target_pairs={{0,8},{4,12},{8,0},{12,4},{16,24},{20,28},{24,16},{28,20},{1,9},{5... | collective-permute-start | bytes 1572872 | tf_op jit(solution)/shard_map/ppermute | solution.py:534
  1.1 2.6 %collective-permute-start = (bf16[512,512]{1,0:T(8,128)(2,1)}, bf16[512,512]{1,0:T(8,128)(2,1)S(1)}, u32[]{:S(2)}, u32[]{:S(2)}) collective-permute-start(bf16[512,512]{1,0:T(8,128)(2,1)} %bitcast.5), channel_id=1, source_target_pairs={{0,4},{4,0},{8,16},{12,20},{16,8},{20,12},{24,28},{28,24},{1,5},{5... | collective-permute-start | bytes 1572872 | tf_op jit(solution)/shard_map/ppermute | solution.py:534
  3.8 1.0 %copy-done.4 = bf16[8,128,128]{2,1,0:T(8,128)(2,1)S(1)} copy-done((bf16[8,128,128]{2,1,0:T(8,128)(2,1)S(1)}, bf16[8,128,128]{2,1,0:T(8,128)(2,1)}, u32[]{:S(2)}) %copy-start.4) | copy-done | bytes 262168
  4.8 1.2 %near_spectra.1 = (f32[128,2048]{1,0:T(8,128)S(1)}, bf16[4,256,256]{2,1,0:T(8,128)(2,1)S(1)}) custom-call(bf16[512,512]{1,0:T(8,128)(2,1)S(1)} %collective-permute-done.2.image_ref, bf16[8,128,128]{2,1,0:T(8,128)(2,1)S(1)} %copy-done.4), custom_call_target="tpu_custom_call" | custom-call | flops 2000000000 | bytes 2097152 | tf_op jit(solution)/shard_map/near_spectra/pallas_call | solution.py:227
  6.1 1.1 %own_spectra.1.own_spec = f32[128,2048]{1,0:T(8,128)S(1)} custom-call(bf16[512,512]{1,0:T(8,128)(2,1)S(1)} %bitcast.6, bf16[4,256,256]{2,1,0:T(8,128)(2,1)S(1)} %get-tuple-element.19.pairs_ref.rights_ref, bf16[8,128,128]{2,1,0:T(8,128)(2,1)S(1)} %copy-done.5), custom_call_target="tpu_custom_call" | custom-call | flops 1000000000 | bytes 2097152 | tf_op jit(solution)/shard_map/own_spectra/pallas_call | solution.py:239
  7.2 5.3 %collective-permute-done.1.up_ref.down_ref = f32[128,128]{1,0:T(8,128)S(1)} collective-permute-done((f32[128,128]{1,0:T(8,128)}, f32[128,128]{1,0:T(8,128)S(1)}, u32[]{:S(2)}, u32[]{:S(2)}) %collective-permute-start.1) | collective-permute-done | bytes 65568 | tf_op jit(solution)/shard_map/ppermute | solution.py:534
  12.5 3.5 %flows.1 = f32[8,128]{1,0:T(8,128)S(1)} custom-call(bf16[512,512]{1,0:T(8,128)(2,1)S(1)} %collective-permute-done.far_ref, bf16[512,512]{1,0:T(8,128)(2,1)S(1)} %copy-done.2, f32[128,2048]{1,0:T(8,128)S(1)} %own_spectra.1.own_spec, f32[128,2048]{1,0:T(8,128)S(1)} %get-tuple-element.24.near_spec, ...), custom_call_target="tpu_custom_call" | custom-call | flops 4000000000 | bytes 3145728 | tf_op jit(solution)/shard_map/flows/pallas_call | solution.py:264
  16.2 1.2 %collective-permute-start.4 = (f32[8,128]{1,0:T(8,128)S(1)}, f32[8,128]{1,0:T(8,128)S(1)}, u32[]{:S(2)}, u32[]{:S(2)}) collective-permute-start(f32[8,128]{1,0:T(8,128)S(1)} %flows.1), channel_id=1, source_target_pairs={{0,12},{4,8},{8,20},{12,16},{16,28},{20,24},{24,4},{28,0},{1,13},{... | collective-permute-start | bytes 12296 | tf_op jit(solution)/shard_map/ppermute | solution.py:553
  17.5 0.9 %collective-permute-start.3 = (f32[8,128]{1,0:T(8,128)S(1)}, f32[8,128]{1,0:T(8,128)S(1)}, u32[]{:S(2)}, u32[]{:S(2)}) collective-permute-start(f32[8,128]{1,0:T(8,128)S(1)} %flows.1), channel_id=1, source_target_pairs={{0,4},{8,12},{16,20},{24,28},{4,0},{12,8},{20,16},{28,24},{1,5},{9... | collective-permute-start | bytes 12296 | tf_op jit(solution)/shard_map/ppermute | solution.py:534
  18.3 1.6 %collective-permute-start.8 = (f32[192,128]{1,0:T(8,128)S(1)}, f32[192,128]{1,0:T(8,128)S(1)}, u32[]{:S(2)}, u32[]{:S(2)}) collective-permute-start(f32[192,128]{1,0:T(8,128)S(1)} %anchor_rows.1.own_ref), channel_id=1, source_target_pairs={{0,1},{8,9},{16,17},{24,25},{1,0},{9,8},{17,16},{25,24},{2,3},{10,... | collective-permute-start | bytes 294920 | tf_op jit(solution)/shard_map/ppermute | solution.py:534
  20.0 0.2 collective-permute-start.9
  20.2 0.5 %collective-permute-done.4 = f32[8,128]{1,0:T(8,128)S(1)} collective-permute-done((f32[8,128]{1,0:T(8,128)S(1)}, f32[8,128]{1,0:T(8,128)S(1)}, u32[]{:S(2)}, u32[]{:S(2)}) %collective-permute-start.4) | collective-permute-done | bytes 4128 | tf_op jit(solution)/shard_map/ppermute | solution.py:553
  20.7 0.4 %collective-permute-done.3 = f32[8,128]{1,0:T(8,128)S(1)} collective-permute-done((f32[8,128]{1,0:T(8,128)S(1)}, f32[8,128]{1,0:T(8,128)S(1)}, u32[]{:S(2)}, u32[]{:S(2)}) %collective-permute-start.3) | collective-permute-done | bytes 4128 | tf_op jit(solution)/shard_map/ppermute | solution.py:534
  21.2 2.2 %collective-permute-start.6 = (f32[8,128]{1,0:T(8,128)S(1)}, f32[8,128]{1,0:T(8,128)S(1)}, u32[]{:S(2)}, u32[]{:S(2)}) collective-permute-start(f32[8,128]{1,0:T(8,128)S(1)} %maximum_maximum_fusion.own_ref), channel_id=1, source_target_pairs={{0,1},{8,9},{16,17},{24,25},{1,0},{9,8},{17,16},{25,24},{2,3},{10,... | collective-permute-start | bytes 12296 | tf_op jit(solution)/shard_map/ppermute | solution.py:534
  23.4 0.2 collective-permute-done.8.even_ref
  23.6 0.6 %gains.1 = (f32[24,8,384]{2,1,0:T(8,128)S(1)}, f32[24,8,384]{2,1,0:T(8,128)S(1)}) custom-call(f32[192,128]{1,0:T(8,128)S(1)} %anchor_rows.1.own_ref, f32[192,128]{1,0:T(8,128)S(1)} %collective-permute-done.8.even_ref, f32[192,128]{1,0:T(8,128)S(1)} %collective-permute-done.9.odd_ref, bf16[384,384]{1,0:T(8,128)(2,1)S(1)} %copy-done.3, s32[1,384]{1,0:T(1,128)S(1)} %copy-done.13), custom_call_target="tpu_custom_call" | custom-call | flops 1000000000 | bytes 1048576 | tf_op jit(solution)/shard_map/gains/pallas_call | solution.py:362
  24.2 0.8 %collective-permute-done.6.even_ref = f32[8,128]{1,0:T(8,128)S(1)} collective-permute-done((f32[8,128]{1,0:T(8,128)S(1)}, f32[8,128]{1,0:T(8,128)S(1)}, u32[]{:S(2)}, u32[]{:S(2)}) %collective-permute-start.6) | collective-permute-done | bytes 4128 | tf_op jit(solution)/shard_map/ppermute | solution.py:534
  25.0 4.0 %relax.1 = (f32[24,8,384]{2,1,0:T(8,128)S(1)}, f32[8,128]{1,0:T(8,128)S(1)}) custom-call(f32[8,128]{1,0:T(8,128)S(1)} %maximum_maximum_fusion.own_ref, f32[8,128]{1,0:T(8,128)S(1)} %collective-permute-done.6.even_ref, f32[8,128]{1,0:T(8,128)S(1)} %collective-permute-done.7.odd_ref, f32[24,8,384]{2,1,0:T(8,128)S(1)} %get-tuple-element.27.gain_ref, ...), custom_call_target="tpu_custom_call" | custom-call | flops 4000000000 | bytes 3145728 | tf_op jit(solution)/shard_map/relax/pallas_call | solution.py:450
  29.0 0.2 collective-permute-start.10
  29.2 2.3 %collective-permute-start.11 = (f32[8,128]{1,0:T(8,128)S(1)}, f32[8,128]{1,0:T(8,128)S(1)}, u32[]{:S(2)}, u32[]{:S(2)}) collective-permute-start(f32[8,128]{1,0:T(8,128)S(1)} %get-tuple-element.32.refs_0_), channel_id=1, source_target_pairs={{0,16},{8,24},{16,0},{24,8},{1,17},{9,25},{17,1},{25,9},{2,18},{10... | collective-permute-start | bytes 12296 | tf_op jit(solution)/shard_map/ppermute | solution.py:593
  31.7 1.0 %natural_mesh.1 = f32[1,2,128,128]{3,2,1,0:T(8,128)} custom-call(f32[24,8,384]{2,1,0:T(8,128)S(1)} %get-tuple-element.29.ring_ref, bf16[384,256]{1,0:T(8,128)(2,1)S(1)} %copy-done.7), custom_call_target="tpu_custom_call" | custom-call | flops 1000000000 | bytes 1048576 | tf_op jit(solution)/shard_map/natural_mesh/pallas_call | solution.py:475
  32.6 0.5 %collective-permute-done.11.refs_2_ = f32[8,128]{1,0:T(8,128)S(1)} collective-permute-done((f32[8,128]{1,0:T(8,128)S(1)}, f32[8,128]{1,0:T(8,128)S(1)}, u32[]{:S(2)}, u32[]{:S(2)}) %collective-permute-start.11) | collective-permute-done | bytes 4128 | tf_op jit(solution)/shard_map/ppermute | solution.py:593
  33.2 1.4 %collective-permute-done.12.refs_3_ = f32[8,128]{1,0:T(8,128)S(1)} collective-permute-done((f32[8,128]{1,0:T(8,128)S(1)}, f32[8,128]{1,0:T(8,128)S(1)}, u32[]{:S(2)}, u32[]{:S(2)}) %collective-permute-start.12) | collective-permute-done | bytes 4128 | tf_op jit(solution)/shard_map/ppermute | solution.py:593
  34.6 0.8 %compose.1 = f32[1,1,1,2,128]{4,3,2,1,0:T(2,128)} custom-call(f32[8,128]{1,0:T(8,128)S(1)} %get-tuple-element.32.refs_0_, f32[8,128]{1,0:T(8,128)S(1)} %collective-permute-done.10.refs_1_, f32[8,128]{1,0:T(8,128)S(1)} %collective-permute-done.11.refs_2_, f32[8,128]{1,0:T(8,128)S(1)} %collective-permute-done.12.refs_3_), custom_call_target="tpu_custom_call" | custom-call | tf_op jit(solution)/shard_map/compose/pallas_call | solution.py:510
  (43 shorter events, 0.5 us)
Async XLA Ops:
  0.6 3.2 %collective-permute-start.2 = (bf16[512,512]{1,0:T(8,128)(2,1)}, bf16[512,512]{1,0:T(8,128)(2,1)S(1)}, u32[]{:S(2)}, u32[]{:S(2)}) collective-permute-start(bf16[512,512]{1,0:T(8,128)(2,1)} %bitcast.4), channel_id=1, source_target_pairs={{0,8},{4,12},{8,0},{12,4},{16,24},{20,28},{24,16},{28,20},{1,9},{5... | collective-permute-start | bytes 1572872 | tf_op jit(solution)/shard_map/ppermute | solution.py:534
  1.1 11.4 %collective-permute-start = (bf16[512,512]{1,0:T(8,128)(2,1)}, bf16[512,512]{1,0:T(8,128)(2,1)S(1)}, u32[]{:S(2)}, u32[]{:S(2)}) collective-permute-start(bf16[512,512]{1,0:T(8,128)(2,1)} %bitcast.5), channel_id=1, source_target_pairs={{0,4},{4,0},{8,16},{12,20},{16,8},{20,12},{24,28},{28,24},{1,5},{5... | collective-permute-start | bytes 1572872 | tf_op jit(solution)/shard_map/ppermute | solution.py:534
  3.7 2.3 %copy-start.1 = (bf16[1,512,512]{2,1,0:T(8,128)(2,1)S(1)}, bf16[1,512,512]{2,1,0:T(8,128)(2,1)}, u32[]{:S(2)}) copy-start(bf16[1,512,512]{2,1,0:T(8,128)(2,1)} %param.13) | copy-start | bytes 1572868
  3.7 8.8 %collective-permute-start.1 = (f32[128,128]{1,0:T(8,128)}, f32[128,128]{1,0:T(8,128)S(1)}, u32[]{:S(2)}, u32[]{:S(2)}) collective-permute-start(f32[128,128]{1,0:T(8,128)} %bitcast.2), channel_id=1, source_target_pairs={{0,4},{8,12},{16,20},{24,28},{4,0},{12,8},{20,16},{28,24},{1,5},{9... | collective-permute-start | bytes 196616 | tf_op jit(solution)/shard_map/ppermute | solution.py:534
  6.1 6.5 %copy-start.2 = (bf16[512,512]{1,0:T(8,128)(2,1)S(1)}, bf16[512,512]{1,0:T(8,128)(2,1)}, u32[]{:S(2)}) copy-start(bf16[512,512]{1,0:T(8,128)(2,1)} %edge_ref.1) | copy-start | bytes 1572868
  12.5 5.8 %copy-start = (f32[1,128,128]{2,1,0:T(8,128)S(1)}, f32[1,128,128]{2,1,0:T(8,128)}, u32[]{:S(2)}) copy-start(f32[1,128,128]{2,1,0:T(8,128)} %param.15) | copy-start | bytes 196612
  16.1 7.5 %copy-start.3 = (bf16[384,384]{1,0:T(8,128)(2,1)S(1)}, bf16[384,384]{1,0:T(8,128)(2,1)}, u32[]{:S(2)}) copy-start(bf16[384,384]{1,0:T(8,128)(2,1)} %constant.32.clone.into_ref) | copy-start | bytes 884740
  16.1 4.1 %collective-permute-start.5 = (f32[8,128]{1,0:T(8,128)S(1)}, f32[8,128]{1,0:T(8,128)S(1)}, u32[]{:S(2)}, u32[]{:S(2)}) collective-permute-start(f32[8,128]{1,0:T(8,128)S(1)} %flows.1), channel_id=1, source_target_pairs={{0,8},{8,16},{16,24},{24,0},{1,9},{9,17},{17,25},{25,1},{2,10},{10... | collective-permute-start | bytes 12296 | tf_op jit(solution)/shard_map/ppermute | solution.py:551
  16.2 4.5 %collective-permute-start.4 = (f32[8,128]{1,0:T(8,128)S(1)}, f32[8,128]{1,0:T(8,128)S(1)}, u32[]{:S(2)}, u32[]{:S(2)}) collective-permute-start(f32[8,128]{1,0:T(8,128)S(1)} %flows.1), channel_id=1, source_target_pairs={{0,12},{4,8},{8,20},{12,16},{16,28},{20,24},{24,4},{28,0},{1,13},{... | collective-permute-start | bytes 12296 | tf_op jit(solution)/shard_map/ppermute | solution.py:553
  17.5 3.6 %collective-permute-start.3 = (f32[8,128]{1,0:T(8,128)S(1)}, f32[8,128]{1,0:T(8,128)S(1)}, u32[]{:S(2)}, u32[]{:S(2)}) collective-permute-start(f32[8,128]{1,0:T(8,128)S(1)} %flows.1), channel_id=1, source_target_pairs={{0,4},{8,12},{16,20},{24,28},{4,0},{12,8},{20,16},{28,24},{1,5},{9... | collective-permute-start | bytes 12296 | tf_op jit(solution)/shard_map/ppermute | solution.py:534
  18.3 5.2 %collective-permute-start.8 = (f32[192,128]{1,0:T(8,128)S(1)}, f32[192,128]{1,0:T(8,128)S(1)}, u32[]{:S(2)}, u32[]{:S(2)}) collective-permute-start(f32[192,128]{1,0:T(8,128)S(1)} %anchor_rows.1.own_ref), channel_id=1, source_target_pairs={{0,1},{8,9},{16,17},{24,25},{1,0},{9,8},{17,16},{25,24},{2,3},{10,... | collective-permute-start | bytes 294920 | tf_op jit(solution)/shard_map/ppermute | solution.py:534
  20.0 3.6 %collective-permute-start.9 = (f32[192,128]{1,0:T(8,128)S(1)}, f32[192,128]{1,0:T(8,128)S(1)}, u32[]{:S(2)}, u32[]{:S(2)}) collective-permute-start(f32[192,128]{1,0:T(8,128)S(1)} %anchor_rows.1.own_ref), channel_id=1, source_target_pairs={{0,8},{8,0},{16,24},{24,16},{1,2},{9,10},{17,18},{25,26},{2,1},{10... | collective-permute-start | bytes 294920 | tf_op jit(solution)/shard_map/ppermute | solution.py:534
  21.1 2.5 %copy-start.13 = (s32[1,384]{1,0:T(1,128)S(1)}, s32[1,384]{1,0:T(1,128)}, u32[]{:S(2)}) copy-start(s32[1,384]{1,0:T(1,128)} %constant.33.clone.ring_ref) | copy-start | bytes 4612
  21.2 3.8 %copy-start.6 = (f32[144,384]{1,0:T(8,128)S(1)}, f32[144,384]{1,0:T(8,128)}, u32[]{:S(2)}) copy-start(f32[144,384]{1,0:T(8,128)} %constant.35.clone.right_ref) | copy-start | bytes 663556
  21.2 3.8 %copy-start.8 = (bf16[192,144]{1,0:T(8,128)(2,1)S(1)}, bf16[192,144]{1,0:T(8,128)(2,1)}, u32[]{:S(2)}) copy-start(bf16[192,144]{1,0:T(8,128)(2,1)} %constant.34.clone.left_ref) | copy-start | bytes 165892
  21.2 3.8 %copy-start.9 = (bf16[384,128]{1,0:T(8,128)(2,1)S(1)}, bf16[384,128]{1,0:T(8,128)(2,1)}, u32[]{:S(2)}) copy-start(bf16[384,128]{1,0:T(8,128)(2,1)} %constant.38.clone.cols_table_ref) | copy-start | bytes 294916
  21.2 3.8 %copy-start.10 = (bf16[192,128]{1,0:T(8,128)(2,1)S(1)}, bf16[192,128]{1,0:T(8,128)(2,1)}, u32[]{:S(2)}) copy-start(bf16[192,128]{1,0:T(8,128)(2,1)} %constant.39.clone.rows_table_ref) | copy-start | bytes 147460
  21.2 3.8 %copy-start.11 = (bf16[16,384]{1,0:T(8,128)(2,1)S(1)}, bf16[16,384]{1,0:T(8,128)(2,1)}, u32[]{:S(2)}) copy-start(bf16[16,384]{1,0:T(8,128)(2,1)} %constant.37.clone.ones_ref) | copy-start | bytes 36868
  21.2 3.8 %collective-permute-start.6 = (f32[8,128]{1,0:T(8,128)S(1)}, f32[8,128]{1,0:T(8,128)S(1)}, u32[]{:S(2)}, u32[]{:S(2)}) collective-permute-start(f32[8,128]{1,0:T(8,128)S(1)} %maximum_maximum_fusion.own_ref), channel_id=1, source_target_pairs={{0,1},{8,9},{16,17},{24,25},{1,0},{9,8},{17,16},{25,24},{2,3},{10,... | collective-permute-start | bytes 12296 | tf_op jit(solution)/shard_map/ppermute | solution.py:534
  23.4 1.6 %collective-permute-start.7 = (f32[8,128]{1,0:T(8,128)S(1)}, f32[8,128]{1,0:T(8,128)S(1)}, u32[]{:S(2)}, u32[]{:S(2)}) collective-permute-start(f32[8,128]{1,0:T(8,128)S(1)} %maximum_maximum_fusion.own_ref), channel_id=1, source_target_pairs={{0,8},{8,0},{16,24},{24,16},{1,2},{9,10},{17,18},{25,26},{2,1},{10... | collective-permute-start | bytes 12296 | tf_op jit(solution)/shard_map/ppermute | solution.py:534
  25.0 6.7 %copy-start.7 = (bf16[384,256]{1,0:T(8,128)(2,1)S(1)}, bf16[384,256]{1,0:T(8,128)(2,1)}, u32[]{:S(2)}) copy-start(bf16[384,256]{1,0:T(8,128)(2,1)} %constant.40.clone.table_ref) | copy-start | bytes 589828
  29.0 3.6 %collective-permute-start.10 = (f32[8,128]{1,0:T(8,128)S(1)}, f32[8,128]{1,0:T(8,128)S(1)}, u32[]{:S(2)}, u32[]{:S(2)}) collective-permute-start(f32[8,128]{1,0:T(8,128)S(1)} %get-tuple-element.32.refs_0_), channel_id=1, source_target_pairs={{0,8},{8,0},{16,24},{24,16},{1,9},{9,1},{17,25},{25,17},{2,10},{10... | collective-permute-start | bytes 12296 | tf_op jit(solution)/shard_map/ppermute | solution.py:593
  29.2 3.9 %collective-permute-start.11 = (f32[8,128]{1,0:T(8,128)S(1)}, f32[8,128]{1,0:T(8,128)S(1)}, u32[]{:S(2)}, u32[]{:S(2)}) collective-permute-start(f32[8,128]{1,0:T(8,128)S(1)} %get-tuple-element.32.refs_0_), channel_id=1, source_target_pairs={{0,16},{8,24},{16,0},{24,8},{1,17},{9,25},{17,1},{25,9},{2,18},{10... | collective-permute-start | bytes 12296 | tf_op jit(solution)/shard_map/ppermute | solution.py:593
  31.6 3.0 %collective-permute-start.12 = (f32[8,128]{1,0:T(8,128)S(1)}, f32[8,128]{1,0:T(8,128)S(1)}, u32[]{:S(2)}, u32[]{:S(2)}) collective-permute-start(f32[8,128]{1,0:T(8,128)S(1)} %get-tuple-element.32.refs_0_), channel_id=1, source_target_pairs={{0,24},{8,16},{16,8},{24,0},{1,25},{9,17},{17,9},{25,1},{2,26},{10... | collective-permute-start | bytes 12296 | tf_op jit(solution)/shard_map/ppermute | solution.py:593
  (3 other events, 3.0 us)

commit v4 on v3

--- a/solution.py
+++ b/solution.py
@@ -294,7 +294,7 @@
 
 
 def target_tables(nodes, patches):
-    ring, part = ring_nodes(nodes)
+    ring, _ = ring_nodes(nodes)
     spread = spread_weights(nodes, patches)
 
     def wide(positions):
@@ -310,7 +310,7 @@
     cols = wide(ring).transpose(1, 2, 0)[:, None, None]
     left = np.broadcast_to(rows, (rows.shape[0],) + shape).reshape(rows.shape[0], -1)
     right = np.broadcast_to(cols, shape + (len(ring),)).reshape(-1, len(ring))
-    return (left.astype(BF16), right.astype(np.float32), part[None])
+    return (left.astype(BF16), right.astype(BF16))
 
 
 def ring_tables(nodes):
@@ -319,7 +319,7 @@
     into = (place == ring[None]).astype(BF16)
     column = np.arange(2 * nodes)[None]
     out = ((ring[:, None] == column % nodes) & (part[:, None] == column // nodes)).astype(BF16)
-    return (into, out, ring.astype(np.int32)[None])
+    return (into, out)
 
 
 def permuted(value, table):
@@ -332,20 +332,28 @@
     return result
 
 
+def ring_place(rows, lanes):
+    lane = lax.broadcasted_iota(jnp.int32, (rows, lanes), 1)
+    return lane % PATCH * (lanes // PATCH) + lane // PATCH
+
+
 def tiles_beside(even_ref, odd_ref):
     at_even = lax.axis_index("tx") % 2 == 0
     even, odd = even_ref[...], odd_ref[...]
     return (jnp.where(at_even, odd, even), jnp.where(at_even, even, odd))
 
 
-def gains_kernel(own_ref, even_ref, odd_ref, into_ref, ring_ref, gain_ref, pull_ref, rows_ref):
+def gains_kernel(own_ref, even_ref, odd_ref, into_ref, gain_ref, pull_ref, rows_ref):
     strips = gain_ref.shape[0]
     nodes = own_ref.shape[1]
     before, after = tiles_beside(even_ref, odd_ref)
     weight = permuted(jnp.concatenate([before, own_ref[...], after], axis=1), into_ref[...])
     row_node = lax.broadcasted_iota(jnp.int32, weight.shape, 0) - SWEEPS
     row_node = row_node + lax.axis_index("ty") * nodes
-    col_node = ring_ref[...] + lax.axis_index("tx") * nodes
+    lanes = into_ref.shape[1]
+    place = ring_place(1, lanes)
+    shift = jnp.where(place < nodes + SWEEPS, 0, jnp.where(place < lanes - SWEEPS, nodes + 2 * SWEEPS, lanes))
+    col_node = place - shift + lax.axis_index("tx") * nodes
     inside = (row_node >= 0) & (row_node < lax.axis_size("ty") * nodes)
     inside = inside & (col_node >= 0) & (col_node < lax.axis_size("tx") * nodes)
     gain = jnp.where(inside, 1.0 / (4.0 + weight), 0.0)
@@ -357,22 +365,22 @@
 
 
 def gains(own, even, odd, nodes):
-    into, _, ring = ring_tables(nodes)
-    shape = jax.ShapeDtypeStruct((own.shape[0] // 8, 8, ring.shape[1]), F32)
+    into, _ = ring_tables(nodes)
+    shape = jax.ShapeDtypeStruct((own.shape[0] // 8, 8, into.shape[1]), F32)
     return pl.pallas_call(
         gains_kernel,
         out_shape=(shape, shape),
-        in_specs=[VMEM] * 5,
+        in_specs=[VMEM] * 4,
         out_specs=(VMEM, VMEM),
-        scratch_shapes=[pltpu.VMEM((ring.shape[1] // PATCH, own.shape[0], PATCH), F32)],
+        scratch_shapes=[pltpu.VMEM((into.shape[1] // PATCH, own.shape[0], PATCH), F32)],
         compiler_params=PARAMS,
         cost_estimate=pl.CostEstimate(flops=10**9, bytes_accessed=2**20, transcendentals=0),
         name="gains",
-    )(own, even, odd, jnp.asarray(into), jnp.asarray(ring))
+    )(own, even, odd, jnp.asarray(into))
 
 
 def relax_kernel(
-    own_ref, even_ref, odd_ref, gain_ref, pull_ref, left_ref, right_ref, part_ref, ones_ref, cols_table_ref, rows_table_ref,
+    own_ref, even_ref, odd_ref, gain_ref, pull_ref, left_ref, right_ref, cols_table_ref, rows_table_ref,
     work_ref, landing_ref, base_ref,
 ):
     strips, _, lanes = work_ref.shape
@@ -387,7 +395,9 @@
         lines = slice(part * patches, (part + 1) * patches)
         return jnp.concatenate([columns[lines, i : i + 1] for i in range(9)], axis=0)
 
-    spread = jnp.where(part_ref[...] == 1, sources(1), sources(0)) * right_ref[...]
+    place = ring_place(1, lanes)
+    second = (place >= nodes + SWEEPS) & (place < lanes - SWEEPS)
+    spread = jnp.where(second, sources(1), sources(0)) * right_ref[...].astype(F32)
     target = None
     for piece in range(3):
         part = spread.astype(BF16)
@@ -416,9 +426,9 @@
             above, here = here, below
         return carry
 
-    lax.fori_loop(0, SWEEPS, sweep, 0, unroll=8)
+    lax.fori_loop(0, SWEEPS, sweep, 0, unroll=16)
     mesh = work_ref[...].reshape(strips * 8, lanes)
-    ones = ones_ref[...]
+    ones = jnp.where(ring_place(16, lanes) < nodes, 1.0, 0.0).astype(BF16)
     sums = None
     for piece in range(3):
         part = mesh.astype(BF16)
@@ -438,19 +448,17 @@
 
 
 def relax(targets, weights, nodes, patches):
-    left, right, part = target_tables(nodes, patches)
+    left, right = target_tables(nodes, patches)
     ring, ring_part = ring_nodes(nodes)
-    own = (ring >= 0) & (ring < nodes)
-    ones = np.broadcast_to(own & (ring_part == 0), (16, len(ring))).astype(BF16)
     node = np.arange(nodes)[None]
     cols_table = ((ring[:, None] == node) & (ring_part[:, None] == 1)).astype(BF16)
     rows_table = (row_nodes(nodes)[:, None] == node).astype(BF16)
-    tables = map(jnp.asarray, (left, right, part, ones, cols_table, rows_table))
+    tables = map(jnp.asarray, (left, right, cols_table, rows_table))
     shape = weights[0].shape
     return pl.pallas_call(
         relax_kernel,
         out_shape=(jax.ShapeDtypeStruct(shape, F32), jax.ShapeDtypeStruct((8, nodes), F32)),
-        in_specs=[VMEM] * 11,
+        in_specs=[VMEM] * 9,
         out_specs=(VMEM, VMEM),
         scratch_shapes=[pltpu.VMEM(shape, F32)],
         compiler_params=PARAMS,
@@ -471,7 +479,7 @@
 
 
 def natural_mesh(ring, nodes):
-    _, table, _ = ring_tables(nodes)
+    _, table = ring_tables(nodes)
     return pl.pallas_call(
         mesh_kernel,
         out_shape=jax.ShapeDtypeStruct((1, 2, nodes, nodes), F32),
@@ -580,11 +588,11 @@
     up, down = rows_beside(anchor[0])
     near_spec, pairs = near_spectra(near, tables)
     own_spec = own_spectra(own, pairs, tables)
-    up, down, own_spec = lax.optimization_barrier((up, down, own_spec))
+    far, own_spec, near_spec = lax.optimization_barrier((far, own_spec, near_spec))
+    flow = flows(far, boundary, own_spec, near_spec, pairs, tables)
+    flow, up, down = lax.optimization_barrier((flow, up, down))
     rows = anchor_rows(up, anchor[0], down)
     weights = gains(rows, swap_pairs(rows, "tx", 0, "gz"), swap_pairs(rows, "tx", 1, "gz"), nodes)
-    far, own_spec, near_spec = lax.optimization_barrier((far, own_spec, near_spec))
-    flow = flows(far, boundary, own_spec, near_spec, pairs, tables)
     line = patch_targets(flow)
     targets = (line, swap_pairs(line, "tx", 0, "gz"), swap_pairs(line, "tx", 1, "gz"))
     ring, landing = relax(targets, weights, nodes, patches)

time: 36 us -> 35.1 us (0.975)
  starting transfers between devices: 12 us -> 11.2 us
    ppermute x8, starting transfers between devices: 8.07 us -> 7.19 us  [swap_pairs(): return lax.ppermute(value, (spare, axis) if flip else (axis, spare), moves)]
    ppermute x1, starting transfers between devices: 1.21 us -> 1.93 us  [to_next(): return lax.ppermute(value, ('gz', 'ty'), moves)]
    ppermute x3, starting transfers between devices: 2.63 us -> 1.99 us  [local(): lax.ppermute(landing, 'gz', [(i, i ^ code) for i in range(sections)])]
    unnamed x28 -> x22, local copies, waits for them, and re-layouts: 1.06 us -> 1.05 us
  transfers between devices with their start and end apart: 13 -> 13, of which waited for: 7 -> 6; matrix products, arithmetic and copies ran while one was open for 0% -> 0% of each run, Pallas kernels for 11% -> 22%
where the time goes in v4:
time: 35.1 us; the launch traced here: 34.5 us
  Pallas kernels  12 us (34%)
  starting transfers between devices  11.2 us (32%)
  waiting for transfers between devices  9.28 us (26%)
  local copies, waits for them, and re-layouts  1.12 us (3%)
  between operations  0.79 us (2%)
    ppermute x8, starting transfers between devices, swap_pairs(): return lax.ppermute(value, (spare, axis) if flip else (axis, spare), moves)  7.19 us
    ppermute x8, waiting for transfers between devices, swap_pairs(): return lax.ppermute(value, (spare, axis) if flip else (axis, spare), moves)  6.97 us
    pallas_call x1, Pallas kernels, relax(): pl.pallas_call(relax_kernel, out_shape=(jax.ShapeDtypeStruct(shape, F32),...  3.81 us
    pallas_call x1, Pallas kernels, flows(): pl.pallas_call(flows_kernel, out_shape=jax.ShapeDtypeStruct((8, PATCH), F...  3.54 us
    ppermute x3, starting transfers between devices, local(): lax.ppermute(landing, 'gz', [(i, i ^ code) for i in range(sections)])  1.99 us
    ppermute x3, waiting for transfers between devices, local(): lax.ppermute(landing, 'gz', [(i, i ^ code) for i in range(sections)])  1.98 us
    ppermute x1, starting transfers between devices, to_next(): return lax.ppermute(value, ('gz', 'ty'), moves)  1.93 us
    pallas_call x1, Pallas kernels, near_spectra(): pl.pallas_call(near_kernel, out_shape=(spec_shape(near), pairs), in_specs...  1.19 us
  transfers between devices with their start and end apart: 13, of which 6 were waited for; matrix products, arithmetic and copies ran while one was open for 0% of the time, Pallas kernels for 22%

profile of v4, /device:TPU:0, one launch (start us, length us, event | category | flops | bytes accessed | tf_op | source)
XLA Modules:
  0.0 34.5 jit_solution(10611354329837940404)
XLA Ops:
  0.6 0.5 %collective-permute-start.1 = (bf16[512,512]{1,0:T(8,128)(2,1)}, bf16[512,512]{1,0:T(8,128)(2,1)S(1)}, u32[]{:S(2)}, u32[]{:S(2)}) collective-permute-start(bf16[512,512]{1,0:T(8,128)(2,1)} %bitcast.4), channel_id=1, source_target_pairs={{0,8},{4,12},{8,0},{12,4},{16,24},{20,28},{24,16},{28,20},{1,9},{5... | collective-permute-start | bytes 1572872 | tf_op jit(solution)/shard_map/ppermute | solution.py:542
  1.1 2.6 %collective-permute-start = (bf16[512,512]{1,0:T(8,128)(2,1)}, bf16[512,512]{1,0:T(8,128)(2,1)S(1)}, u32[]{:S(2)}, u32[]{:S(2)}) collective-permute-start(bf16[512,512]{1,0:T(8,128)(2,1)} %bitcast.5), channel_id=1, source_target_pairs={{0,4},{4,0},{8,16},{12,20},{16,8},{20,12},{24,28},{28,24},{1,5},{5... | collective-permute-start | bytes 1572872 | tf_op jit(solution)/shard_map/ppermute | solution.py:542
  3.7 0.1 collective-permute-start.2
  3.8 1.0 %copy-done.4 = bf16[8,128,128]{2,1,0:T(8,128)(2,1)S(1)} copy-done((bf16[8,128,128]{2,1,0:T(8,128)(2,1)S(1)}, bf16[8,128,128]{2,1,0:T(8,128)(2,1)}, u32[]{:S(2)}) %copy-start.4) | copy-done | bytes 262168
  4.8 1.2 %near_spectra.1 = (f32[128,2048]{1,0:T(8,128)S(1)}, bf16[4,256,256]{2,1,0:T(8,128)(2,1)S(1)}) custom-call(bf16[512,512]{1,0:T(8,128)(2,1)S(1)} %collective-permute-done.1.image_ref, bf16[8,128,128]{2,1,0:T(8,128)(2,1)S(1)} %copy-done.4), custom_call_target="tpu_custom_call" | custom-call | flops 2000000000 | bytes 2097152 | tf_op jit(solution)/shard_map/near_spectra/pallas_call | solution.py:227
  6.1 1.1 %own_spectra.1.own_spec = f32[128,2048]{1,0:T(8,128)S(1)} custom-call(bf16[512,512]{1,0:T(8,128)(2,1)S(1)} %bitcast.6, bf16[4,256,256]{2,1,0:T(8,128)(2,1)S(1)} %get-tuple-element.19.pairs_ref.rights_ref, bf16[8,128,128]{2,1,0:T(8,128)(2,1)S(1)} %copy-done.5), custom_call_target="tpu_custom_call" | custom-call | flops 1000000000 | bytes 2097152 | tf_op jit(solution)/shard_map/own_spectra/pallas_call | solution.py:239
  7.2 4.6 %collective-permute-done.far_ref = bf16[512,512]{1,0:T(8,128)(2,1)S(1)} collective-permute-done((bf16[512,512]{1,0:T(8,128)(2,1)}, bf16[512,512]{1,0:T(8,128)(2,1)S(1)}, u32[]{:S(2)}, u32[]{:S(2)}) %collective-permute-start) | collective-permute-done | bytes 524320 | tf_op jit(solution)/shard_map/ppermute | solution.py:542
  11.8 3.5 %flows.1 = f32[8,128]{1,0:T(8,128)S(1)} custom-call(bf16[512,512]{1,0:T(8,128)(2,1)S(1)} %collective-permute-done.far_ref, bf16[512,512]{1,0:T(8,128)(2,1)S(1)} %copy-done.2, f32[128,2048]{1,0:T(8,128)S(1)} %own_spectra.1.own_spec, f32[128,2048]{1,0:T(8,128)S(1)} %get-tuple-element.23.near_spec, ...), custom_call_target="tpu_custom_call" | custom-call | flops 4000000000 | bytes 3145728 | tf_op jit(solution)/shard_map/flows/pallas_call | solution.py:264
  15.5 0.1 pad.3.clone
  15.5 1.9 %collective-permute-start.4 = (f32[8,128]{1,0:T(8,128)S(1)}, f32[8,128]{1,0:T(8,128)S(1)}, u32[]{:S(2)}, u32[]{:S(2)}) collective-permute-start(f32[8,128]{1,0:T(8,128)S(1)} %flows.1), channel_id=1, source_target_pairs={{0,12},{4,8},{8,20},{12,16},{16,28},{20,24},{24,4},{28,0},{1,13},{... | collective-permute-start | bytes 12296 | tf_op jit(solution)/shard_map/ppermute | solution.py:561
  17.5 0.5 %collective-permute-start.3 = (f32[8,128]{1,0:T(8,128)S(1)}, f32[8,128]{1,0:T(8,128)S(1)}, u32[]{:S(2)}, u32[]{:S(2)}) collective-permute-start(f32[8,128]{1,0:T(8,128)S(1)} %flows.1), channel_id=1, source_target_pairs={{0,4},{8,12},{16,20},{24,28},{4,0},{12,8},{20,16},{28,24},{1,5},{9... | collective-permute-start | bytes 12296 | tf_op jit(solution)/shard_map/ppermute | solution.py:542
  18.0 1.6 %collective-permute-start.8 = (f32[192,128]{1,0:T(8,128)S(1)}, f32[192,128]{1,0:T(8,128)S(1)}, u32[]{:S(2)}, u32[]{:S(2)}) collective-permute-start(f32[192,128]{1,0:T(8,128)S(1)} %anchor_rows.1.own_ref), channel_id=1, source_target_pairs={{0,1},{8,9},{16,17},{24,25},{1,0},{9,8},{17,16},{25,24},{2,3},{10,... | collective-permute-start | bytes 294920 | tf_op jit(solution)/shard_map/ppermute | solution.py:542
  19.7 0.3 collective-permute-done.4
  20.0 1.1 %collective-permute-done.3 = f32[8,128]{1,0:T(8,128)S(1)} collective-permute-done((f32[8,128]{1,0:T(8,128)S(1)}, f32[8,128]{1,0:T(8,128)S(1)}, u32[]{:S(2)}, u32[]{:S(2)}) %collective-permute-start.3) | collective-permute-done | bytes 4128 | tf_op jit(solution)/shard_map/ppermute | solution.py:542
  21.1 0.1 maximum_maximum_fusion.own_ref
  21.2 1.8 %collective-permute-start.6 = (f32[8,128]{1,0:T(8,128)S(1)}, f32[8,128]{1,0:T(8,128)S(1)}, u32[]{:S(2)}, u32[]{:S(2)}) collective-permute-start(f32[8,128]{1,0:T(8,128)S(1)} %maximum_maximum_fusion.own_ref), channel_id=1, source_target_pairs={{0,1},{8,9},{16,17},{24,25},{1,0},{9,8},{17,16},{25,24},{2,3},{10,... | collective-permute-start | bytes 12296 | tf_op jit(solution)/shard_map/ppermute | solution.py:542
  23.0 0.6 %gains.1 = (f32[24,8,384]{2,1,0:T(8,128)S(1)}, f32[24,8,384]{2,1,0:T(8,128)S(1)}) custom-call(f32[192,128]{1,0:T(8,128)S(1)} %anchor_rows.1.own_ref, f32[192,128]{1,0:T(8,128)S(1)} %collective-permute-done.8.even_ref, f32[192,128]{1,0:T(8,128)S(1)} %collective-permute-done.9.odd_ref, bf16[384,384]{1,0:T(8,128)(2,1)S(1)} %copy-done.3), custom_call_target="tpu_custom_call" | custom-call | flops 1000000000 | bytes 1048576 | tf_op jit(solution)/shard_map/gains/pallas_call | solution.py:370
  23.6 1.2 %collective-permute-done.6.even_ref = f32[8,128]{1,0:T(8,128)S(1)} collective-permute-done((f32[8,128]{1,0:T(8,128)S(1)}, f32[8,128]{1,0:T(8,128)S(1)}, u32[]{:S(2)}, u32[]{:S(2)}) %collective-permute-start.6) | collective-permute-done | bytes 4128 | tf_op jit(solution)/shard_map/ppermute | solution.py:542
  24.9 3.8 %relax.1 = (f32[24,8,384]{2,1,0:T(8,128)S(1)}, f32[8,128]{1,0:T(8,128)S(1)}) custom-call(f32[8,128]{1,0:T(8,128)S(1)} %maximum_maximum_fusion.own_ref, f32[8,128]{1,0:T(8,128)S(1)} %collective-permute-done.6.even_ref, f32[8,128]{1,0:T(8,128)S(1)} %collective-permute-done.7.odd_ref, f32[24,8,384]{2,1,0:T(8,128)S(1)} %get-tuple-element.27.gain_ref, ...), custom_call_target="tpu_custom_call" | custom-call | flops 4000000000 | bytes 3145728 | tf_op jit(solution)/shard_map/relax/pallas_call | solution.py:458
  28.8 1.8 %collective-permute-start.11 = (f32[8,128]{1,0:T(8,128)S(1)}, f32[8,128]{1,0:T(8,128)S(1)}, u32[]{:S(2)}, u32[]{:S(2)}) collective-permute-start(f32[8,128]{1,0:T(8,128)S(1)} %get-tuple-element.32.refs_0_), channel_id=1, source_target_pairs={{0,16},{8,24},{16,0},{24,8},{1,17},{9,25},{17,1},{25,9},{2,18},{10... | collective-permute-start | bytes 12296 | tf_op jit(solution)/shard_map/ppermute | solution.py:601
  30.7 1.0 %natural_mesh.1 = f32[1,2,128,128]{3,2,1,0:T(8,128)} custom-call(f32[24,8,384]{2,1,0:T(8,128)S(1)} %get-tuple-element.29.ring_ref, bf16[384,256]{1,0:T(8,128)(2,1)S(1)} %copy-done.6), custom_call_target="tpu_custom_call" | custom-call | flops 1000000000 | bytes 1048576 | tf_op jit(solution)/shard_map/natural_mesh/pallas_call | solution.py:483
  31.7 0.8 %collective-permute-done.11.refs_2_ = f32[8,128]{1,0:T(8,128)S(1)} collective-permute-done((f32[8,128]{1,0:T(8,128)S(1)}, f32[8,128]{1,0:T(8,128)S(1)}, u32[]{:S(2)}, u32[]{:S(2)}) %collective-permute-start.11) | collective-permute-done | bytes 4128 | tf_op jit(solution)/shard_map/ppermute | solution.py:601
  32.5 1.2 %collective-permute-done.12.refs_3_ = f32[8,128]{1,0:T(8,128)S(1)} collective-permute-done((f32[8,128]{1,0:T(8,128)S(1)}, f32[8,128]{1,0:T(8,128)S(1)}, u32[]{:S(2)}, u32[]{:S(2)}) %collective-permute-start.12) | collective-permute-done | bytes 4128 | tf_op jit(solution)/shard_map/ppermute | solution.py:601
  33.7 0.8 %compose.1 = f32[1,1,1,2,128]{4,3,2,1,0:T(2,128)} custom-call(f32[8,128]{1,0:T(8,128)S(1)} %get-tuple-element.32.refs_0_, f32[8,128]{1,0:T(8,128)S(1)} %collective-permute-done.10.refs_1_, f32[8,128]{1,0:T(8,128)S(1)} %collective-permute-done.11.refs_2_, f32[8,128]{1,0:T(8,128)S(1)} %collective-permute-done.12.refs_3_), custom_call_target="tpu_custom_call" | custom-call | tf_op jit(solution)/shard_map/compose/pallas_call | solution.py:518
  (37 shorter events, 0.3 us)
Async XLA Ops:
  0.6 3.2 %collective-permute-start.1 = (bf16[512,512]{1,0:T(8,128)(2,1)}, bf16[512,512]{1,0:T(8,128)(2,1)S(1)}, u32[]{:S(2)}, u32[]{:S(2)}) collective-permute-start(bf16[512,512]{1,0:T(8,128)(2,1)} %bitcast.4), channel_id=1, source_target_pairs={{0,8},{4,12},{8,0},{12,4},{16,24},{20,28},{24,16},{28,20},{1,9},{5... | collective-permute-start | bytes 1572872 | tf_op jit(solution)/shard_map/ppermute | solution.py:542
  1.1 10.7 %collective-permute-start = (bf16[512,512]{1,0:T(8,128)(2,1)}, bf16[512,512]{1,0:T(8,128)(2,1)S(1)}, u32[]{:S(2)}, u32[]{:S(2)}) collective-permute-start(bf16[512,512]{1,0:T(8,128)(2,1)} %bitcast.5), channel_id=1, source_target_pairs={{0,4},{4,0},{8,16},{12,20},{16,8},{20,12},{24,28},{28,24},{1,5},{5... | collective-permute-start | bytes 1572872 | tf_op jit(solution)/shard_map/ppermute | solution.py:542
  3.7 2.3 %copy-start.1 = (bf16[1,512,512]{2,1,0:T(8,128)(2,1)S(1)}, bf16[1,512,512]{2,1,0:T(8,128)(2,1)}, u32[]{:S(2)}) copy-start(bf16[1,512,512]{2,1,0:T(8,128)(2,1)} %param.10) | copy-start | bytes 1572868
  3.7 11.6 %collective-permute-start.2 = (f32[128,128]{1,0:T(8,128)}, f32[128,128]{1,0:T(8,128)S(1)}, u32[]{:S(2)}, u32[]{:S(2)}) collective-permute-start(f32[128,128]{1,0:T(8,128)} %bitcast.2), channel_id=1, source_target_pairs={{0,4},{8,12},{16,20},{24,28},{4,0},{12,8},{20,16},{28,24},{1,5},{9... | collective-permute-start | bytes 196616 | tf_op jit(solution)/shard_map/ppermute | solution.py:542
  3.8 1.0 %copy-start.4 = (bf16[8,128,128]{2,1,0:T(8,128)(2,1)S(1)}, bf16[8,128,128]{2,1,0:T(8,128)(2,1)}, u32[]{:S(2)}) copy-start(bf16[8,128,128]{2,1,0:T(8,128)(2,1)} %constant.25.clone.tables_ref) | copy-start | bytes 786436
  4.8 1.2 %copy-start.5 = (bf16[8,128,128]{2,1,0:T(8,128)(2,1)S(1)}, bf16[8,128,128]{2,1,0:T(8,128)(2,1)}, u32[]{:S(2)}) copy-start(bf16[8,128,128]{2,1,0:T(8,128)(2,1)} %constant.25.clone.tables_ref) | copy-start | bytes 786436
  6.1 5.8 %copy-start.2 = (bf16[512,512]{1,0:T(8,128)(2,1)S(1)}, bf16[512,512]{1,0:T(8,128)(2,1)}, u32[]{:S(2)}) copy-start(bf16[512,512]{1,0:T(8,128)(2,1)} %edge_ref.1) | copy-start | bytes 1572868
  11.8 6.2 %copy-start = (f32[1,128,128]{2,1,0:T(8,128)S(1)}, f32[1,128,128]{2,1,0:T(8,128)}, u32[]{:S(2)}) copy-start(f32[1,128,128]{2,1,0:T(8,128)} %param.12) | copy-start | bytes 196612
  15.4 7.7 %copy-start.3 = (bf16[384,384]{1,0:T(8,128)(2,1)S(1)}, bf16[384,384]{1,0:T(8,128)(2,1)}, u32[]{:S(2)}) copy-start(bf16[384,384]{1,0:T(8,128)(2,1)} %constant.26.clone.into_ref) | copy-start | bytes 884740
  15.4 4.3 %collective-permute-start.5 = (f32[8,128]{1,0:T(8,128)S(1)}, f32[8,128]{1,0:T(8,128)S(1)}, u32[]{:S(2)}, u32[]{:S(2)}) collective-permute-start(f32[8,128]{1,0:T(8,128)S(1)} %flows.1), channel_id=1, source_target_pairs={{0,8},{8,16},{16,24},{24,0},{1,9},{9,17},{17,25},{25,1},{2,10},{10... | collective-permute-start | bytes 12296 | tf_op jit(solution)/shard_map/ppermute | solution.py:559
  15.5 4.5 %collective-permute-start.4 = (f32[8,128]{1,0:T(8,128)S(1)}, f32[8,128]{1,0:T(8,128)S(1)}, u32[]{:S(2)}, u32[]{:S(2)}) collective-permute-start(f32[8,128]{1,0:T(8,128)S(1)} %flows.1), channel_id=1, source_target_pairs={{0,12},{4,8},{8,20},{12,16},{16,28},{20,24},{24,4},{28,0},{1,13},{... | collective-permute-start | bytes 12296 | tf_op jit(solution)/shard_map/ppermute | solution.py:561
  17.5 3.6 %collective-permute-start.3 = (f32[8,128]{1,0:T(8,128)S(1)}, f32[8,128]{1,0:T(8,128)S(1)}, u32[]{:S(2)}, u32[]{:S(2)}) collective-permute-start(f32[8,128]{1,0:T(8,128)S(1)} %flows.1), channel_id=1, source_target_pairs={{0,4},{8,12},{16,20},{24,28},{4,0},{12,8},{20,16},{28,24},{1,5},{9... | collective-permute-start | bytes 12296 | tf_op jit(solution)/shard_map/ppermute | solution.py:542
  18.0 5.0 %collective-permute-start.8 = (f32[192,128]{1,0:T(8,128)S(1)}, f32[192,128]{1,0:T(8,128)S(1)}, u32[]{:S(2)}, u32[]{:S(2)}) collective-permute-start(f32[192,128]{1,0:T(8,128)S(1)} %anchor_rows.1.own_ref), channel_id=1, source_target_pairs={{0,1},{8,9},{16,17},{24,25},{1,0},{9,8},{17,16},{25,24},{2,3},{10,... | collective-permute-start | bytes 294920 | tf_op jit(solution)/shard_map/ppermute | solution.py:542
  19.7 3.4 %collective-permute-start.9 = (f32[192,128]{1,0:T(8,128)S(1)}, f32[192,128]{1,0:T(8,128)S(1)}, u32[]{:S(2)}, u32[]{:S(2)}) collective-permute-start(f32[192,128]{1,0:T(8,128)S(1)} %anchor_rows.1.own_ref), channel_id=1, source_target_pairs={{0,8},{8,0},{16,24},{24,16},{1,2},{9,10},{17,18},{25,26},{2,1},{10... | collective-permute-start | bytes 294920 | tf_op jit(solution)/shard_map/ppermute | solution.py:542
  21.2 3.7 %copy-start.7 = (bf16[144,384]{1,0:T(8,128)(2,1)S(1)}, bf16[144,384]{1,0:T(8,128)(2,1)}, u32[]{:S(2)}) copy-start(bf16[144,384]{1,0:T(8,128)(2,1)} %constant.28.clone.right_ref) | copy-start | bytes 331780
  21.2 3.7 %copy-start.8 = (bf16[192,144]{1,0:T(8,128)(2,1)S(1)}, bf16[192,144]{1,0:T(8,128)(2,1)}, u32[]{:S(2)}) copy-start(bf16[192,144]{1,0:T(8,128)(2,1)} %constant.27.clone.left_ref) | copy-start | bytes 165892
  21.2 3.7 %copy-start.9 = (bf16[384,128]{1,0:T(8,128)(2,1)S(1)}, bf16[384,128]{1,0:T(8,128)(2,1)}, u32[]{:S(2)}) copy-start(bf16[384,128]{1,0:T(8,128)(2,1)} %constant.29.clone.cols_table_ref) | copy-start | bytes 294916
  21.2 3.7 %copy-start.10 = (bf16[192,128]{1,0:T(8,128)(2,1)S(1)}, bf16[192,128]{1,0:T(8,128)(2,1)}, u32[]{:S(2)}) copy-start(bf16[192,128]{1,0:T(8,128)(2,1)} %constant.30.clone.rows_table_ref) | copy-start | bytes 147460
  21.2 3.7 %collective-permute-start.6 = (f32[8,128]{1,0:T(8,128)S(1)}, f32[8,128]{1,0:T(8,128)S(1)}, u32[]{:S(2)}, u32[]{:S(2)}) collective-permute-start(f32[8,128]{1,0:T(8,128)S(1)} %maximum_maximum_fusion.own_ref), channel_id=1, source_target_pairs={{0,1},{8,9},{16,17},{24,25},{1,0},{9,8},{17,16},{25,24},{2,3},{10,... | collective-permute-start | bytes 12296 | tf_op jit(solution)/shard_map/ppermute | solution.py:542
  23.0 1.9 %collective-permute-start.7 = (f32[8,128]{1,0:T(8,128)S(1)}, f32[8,128]{1,0:T(8,128)S(1)}, u32[]{:S(2)}, u32[]{:S(2)}) collective-permute-start(f32[8,128]{1,0:T(8,128)S(1)} %maximum_maximum_fusion.own_ref), channel_id=1, source_target_pairs={{0,8},{8,0},{16,24},{24,16},{1,2},{9,10},{17,18},{25,26},{2,1},{10... | collective-permute-start | bytes 12296 | tf_op jit(solution)/shard_map/ppermute | solution.py:542
  24.9 5.8 %copy-start.6 = (bf16[384,256]{1,0:T(8,128)(2,1)S(1)}, bf16[384,256]{1,0:T(8,128)(2,1)}, u32[]{:S(2)}) copy-start(bf16[384,256]{1,0:T(8,128)(2,1)} %constant.31.clone.table_ref) | copy-start | bytes 589828
  28.7 3.0 %collective-permute-start.10 = (f32[8,128]{1,0:T(8,128)S(1)}, f32[8,128]{1,0:T(8,128)S(1)}, u32[]{:S(2)}, u32[]{:S(2)}) collective-permute-start(f32[8,128]{1,0:T(8,128)S(1)} %get-tuple-element.32.refs_0_), channel_id=1, source_target_pairs={{0,8},{8,0},{16,24},{24,16},{1,9},{9,1},{17,25},{25,17},{2,10},{10... | collective-permute-start | bytes 12296 | tf_op jit(solution)/shard_map/ppermute | solution.py:601
  28.8 3.7 %collective-permute-start.11 = (f32[8,128]{1,0:T(8,128)S(1)}, f32[8,128]{1,0:T(8,128)S(1)}, u32[]{:S(2)}, u32[]{:S(2)}) collective-permute-start(f32[8,128]{1,0:T(8,128)S(1)} %get-tuple-element.32.refs_0_), channel_id=1, source_target_pairs={{0,16},{8,24},{16,0},{24,8},{1,17},{9,25},{17,1},{25,9},{2,18},{10... | collective-permute-start | bytes 12296 | tf_op jit(solution)/shard_map/ppermute | solution.py:601
  30.7 3.0 %collective-permute-start.12 = (f32[8,128]{1,0:T(8,128)S(1)}, f32[8,128]{1,0:T(8,128)S(1)}, u32[]{:S(2)}, u32[]{:S(2)}) collective-permute-start(f32[8,128]{1,0:T(8,128)S(1)} %get-tuple-element.32.refs_0_), channel_id=1, source_target_pairs={{0,24},{8,16},{16,8},{24,0},{1,25},{9,17},{17,9},{25,1},{2,26},{10... | collective-permute-start | bytes 12296 | tf_op jit(solution)/shard_map/ppermute | solution.py:601

commit v5 on v4

--- a/solution.py
+++ b/solution.py
@@ -36,20 +36,23 @@
 
 def pair_tables(tables_ref):
     lower = lax.broadcasted_iota(jnp.int32, (PATCH, PATCH), 1) < HALF
-    forwards, inverses = [], []
+    pairs = []
     for index in range(2):
         table = tables_ref[index].astype(F32)
         turned = pltpu.roll(table, HALF, 1)
         first = jnp.concatenate([jnp.where(lower, table, 0.0), jnp.where(lower, turned, 0.0)], axis=1)
         second = jnp.concatenate([jnp.where(lower, 0.0, turned), jnp.where(lower, 0.0, table)], axis=1)
-        forwards.append(jnp.concatenate([first, second], axis=0).astype(BF16))
-        table = tables_ref[2 + index]
-        empty = jnp.zeros((HALF, PATCH), BF16)
-        rows = []
-        for part in (table[:HALF], table[HALF:]):
-            rows += [jnp.concatenate([part, empty], axis=1), jnp.concatenate([empty, part], axis=1)]
-        inverses.append(jnp.concatenate(rows, axis=0))
-    return forwards + inverses
+        pairs.append(jnp.concatenate([first, second], axis=0).astype(BF16))
+    inverse = jnp.concatenate([tables_ref[2], tables_ref[3]], axis=1)
+    return pairs + [jnp.concatenate([inverse, inverse], axis=0)]
+
+
+def single_patches(product):
+    lower = lax.broadcasted_iota(jnp.int32, (PATCH, PATCH), 1) < HALF
+    cosine, sine = product[:, :PATCH], product[:, PATCH:]
+    first = jnp.where(lower, cosine, pltpu.roll(sine, HALF, 1))
+    second = jnp.where(lower, pltpu.roll(cosine, HALF, 1), sine)
+    return [first, second]
 
 
 def halves(value):
@@ -165,8 +168,9 @@
         operand = cross_operand(jnp.where(at_even, far, near))
         products.append(cross(operand, own_spec[:, lanes]))
         products.append(cross(operand, jnp.where(at_even, near, far)))
-    high, low = halves(jnp.concatenate(products, axis=0))
-    back = dot(high, rights_ref[2]) + dot(low, rights_ref[2]) + dot(high, rights_ref[3])
+    singles = [single for product in products for single in single_patches(product)]
+    both = dot(jnp.concatenate(halves(jnp.concatenate(singles, axis=0)), axis=1), rights_ref[2])
+    back = both[:, :PATCH] + both[:, PATCH:]
     scores = left_transform(tables_ref[6], tables_ref[7], side_by_side(back))
     groups = scores.reshape(PATCH // 8, 8, 2 * blocks * wide)
     peak = jnp.max(groups, axis=0)
@@ -223,7 +227,7 @@
 
 
 def near_spectra(near, tables):
-    pairs = jax.ShapeDtypeStruct((4, 2 * PATCH, 2 * PATCH), BF16)
+    pairs = jax.ShapeDtypeStruct((3, 2 * PATCH, 2 * PATCH), BF16)
     return pl.pallas_call(
         near_kernel,
         out_shape=(spec_shape(near), pairs),

time: 35.1 us -> 34.6 us (0.986)
  Pallas kernels: 12 us -> 11.5 us
    pallas_call x1, Pallas kernels: 3.54 us -> 3.05 us  [flows(): pl.pallas_call(flows_kernel, out_shape=jax.ShapeDtypeStruct((8, PATCH), F...]
  transfers between devices with their start and end apart: 13 -> 13, of which waited for: 6 -> 6; matrix products, arithmetic and copies ran while one was open for 0% -> 0% of each run, Pallas kernels for 22% -> 20%
where the time goes in v5:
time: 34.6 us; the launch traced here: 34 us
  Pallas kernels  11.5 us (33%)
  starting transfers between devices  11.2 us (32%)
  waiting for transfers between devices  9.28 us (27%)
  local copies, waits for them, and re-layouts  1.12 us (3%)
  between operations  0.79 us (2%)
    ppermute x8, starting transfers between devices, swap_pairs(): return lax.ppermute(value, (spare, axis) if flip else (axis, spare), moves)  7.19 us
    ppermute x8, waiting for transfers between devices, swap_pairs(): return lax.ppermute(value, (spare, axis) if flip else (axis, spare), moves)  6.97 us
    pallas_call x1, Pallas kernels, relax(): pl.pallas_call(relax_kernel, out_shape=(jax.ShapeDtypeStruct(shape, F32),...  3.81 us
    pallas_call x1, Pallas kernels, flows(): pl.pallas_call(flows_kernel, out_shape=jax.ShapeDtypeStruct((8, PATCH), F...  3.05 us
    ppermute x3, starting transfers between devices, local(): lax.ppermute(landing, 'gz', [(i, i ^ code) for i in range(sections)])  1.99 us
    ppermute x3, waiting for transfers between devices, local(): lax.ppermute(landing, 'gz', [(i, i ^ code) for i in range(sections)])  1.98 us
    ppermute x1, starting transfers between devices, to_next(): return lax.ppermute(value, ('gz', 'ty'), moves)  1.93 us
    pallas_call x1, Pallas kernels, near_spectra(): pl.pallas_call(near_kernel, out_shape=(spec_shape(near), pairs), in_specs...  1.19 us
  transfers between devices with their start and end apart: 13, of which 6 were waited for; matrix products, arithmetic and copies ran while one was open for 0% of the time, Pallas kernels for 20%

profile of v5, /device:TPU:0, one launch (start us, length us, event | category | flops | bytes accessed | tf_op | source)
XLA Modules:
  0.0 34.0 jit_solution(890195663731409273)
XLA Ops:
  0.6 0.5 %collective-permute-start.1 = (bf16[512,512]{1,0:T(8,128)(2,1)}, bf16[512,512]{1,0:T(8,128)(2,1)S(1)}, u32[]{:S(2)}, u32[]{:S(2)}) collective-permute-start(bf16[512,512]{1,0:T(8,128)(2,1)} %bitcast.4), channel_id=1, source_target_pairs={{0,8},{4,12},{8,0},{12,4},{16,24},{20,28},{24,16},{28,20},{1,9},{5... | collective-permute-start | bytes 1572872 | tf_op jit(solution)/shard_map/ppermute | solution.py:546
  1.1 2.6 %collective-permute-start = (bf16[512,512]{1,0:T(8,128)(2,1)}, bf16[512,512]{1,0:T(8,128)(2,1)S(1)}, u32[]{:S(2)}, u32[]{:S(2)}) collective-permute-start(bf16[512,512]{1,0:T(8,128)(2,1)} %bitcast.5), channel_id=1, source_target_pairs={{0,4},{4,0},{8,16},{12,20},{16,8},{20,12},{24,28},{28,24},{1,5},{5... | collective-permute-start | bytes 1572872 | tf_op jit(solution)/shard_map/ppermute | solution.py:546
  3.7 0.1 collective-permute-start.2
  3.8 1.0 %copy-done.4 = bf16[8,128,128]{2,1,0:T(8,128)(2,1)S(1)} copy-done((bf16[8,128,128]{2,1,0:T(8,128)(2,1)S(1)}, bf16[8,128,128]{2,1,0:T(8,128)(2,1)}, u32[]{:S(2)}) %copy-start.4) | copy-done | bytes 262168
  4.8 1.2 %near_spectra.1 = (f32[128,2048]{1,0:T(8,128)S(1)}, bf16[3,256,256]{2,1,0:T(8,128)(2,1)S(1)}) custom-call(bf16[512,512]{1,0:T(8,128)(2,1)S(1)} %collective-permute-done.1.image_ref, bf16[8,128,128]{2,1,0:T(8,128)(2,1)S(1)} %copy-done.4), custom_call_target="tpu_custom_call" | custom-call | flops 2000000000 | bytes 2097152 | tf_op jit(solution)/shard_map/near_spectra/pallas_call | solution.py:231
  6.1 1.1 %own_spectra.1.own_spec = f32[128,2048]{1,0:T(8,128)S(1)} custom-call(bf16[512,512]{1,0:T(8,128)(2,1)S(1)} %bitcast.6, bf16[3,256,256]{2,1,0:T(8,128)(2,1)S(1)} %get-tuple-element.19.pairs_ref.rights_ref, bf16[8,128,128]{2,1,0:T(8,128)(2,1)S(1)} %copy-done.5), custom_call_target="tpu_custom_call" | custom-call | flops 1000000000 | bytes 2097152 | tf_op jit(solution)/shard_map/own_spectra/pallas_call | solution.py:243
  7.2 4.6 %collective-permute-done.far_ref = bf16[512,512]{1,0:T(8,128)(2,1)S(1)} collective-permute-done((bf16[512,512]{1,0:T(8,128)(2,1)}, bf16[512,512]{1,0:T(8,128)(2,1)S(1)}, u32[]{:S(2)}, u32[]{:S(2)}) %collective-permute-start) | collective-permute-done | bytes 524320 | tf_op jit(solution)/shard_map/ppermute | solution.py:546
  11.8 3.0 %flows.1 = f32[8,128]{1,0:T(8,128)S(1)} custom-call(bf16[512,512]{1,0:T(8,128)(2,1)S(1)} %collective-permute-done.far_ref, bf16[512,512]{1,0:T(8,128)(2,1)S(1)} %copy-done.2, f32[128,2048]{1,0:T(8,128)S(1)} %own_spectra.1.own_spec, f32[128,2048]{1,0:T(8,128)S(1)} %get-tuple-element.23.near_spec, ...), custom_call_target="tpu_custom_call" | custom-call | flops 4000000000 | bytes 3145728 | tf_op jit(solution)/shard_map/flows/pallas_call | solution.py:268
  15.0 0.1 pad.3.clone
  15.1 1.9 %collective-permute-start.4 = (f32[8,128]{1,0:T(8,128)S(1)}, f32[8,128]{1,0:T(8,128)S(1)}, u32[]{:S(2)}, u32[]{:S(2)}) collective-permute-start(f32[8,128]{1,0:T(8,128)S(1)} %flows.1), channel_id=1, source_target_pairs={{0,12},{4,8},{8,20},{12,16},{16,28},{20,24},{24,4},{28,0},{1,13},{... | collective-permute-start | bytes 12296 | tf_op jit(solution)/shard_map/ppermute | solution.py:565
  17.0 0.5 %collective-permute-start.3 = (f32[8,128]{1,0:T(8,128)S(1)}, f32[8,128]{1,0:T(8,128)S(1)}, u32[]{:S(2)}, u32[]{:S(2)}) collective-permute-start(f32[8,128]{1,0:T(8,128)S(1)} %flows.1), channel_id=1, source_target_pairs={{0,4},{8,12},{16,20},{24,28},{4,0},{12,8},{20,16},{28,24},{1,5},{9... | collective-permute-start | bytes 12296 | tf_op jit(solution)/shard_map/ppermute | solution.py:546
  17.5 1.6 %collective-permute-start.8 = (f32[192,128]{1,0:T(8,128)S(1)}, f32[192,128]{1,0:T(8,128)S(1)}, u32[]{:S(2)}, u32[]{:S(2)}) collective-permute-start(f32[192,128]{1,0:T(8,128)S(1)} %anchor_rows.1.own_ref), channel_id=1, source_target_pairs={{0,1},{8,9},{16,17},{24,25},{1,0},{9,8},{17,16},{25,24},{2,3},{10,... | collective-permute-start | bytes 294920 | tf_op jit(solution)/shard_map/ppermute | solution.py:546
  19.2 0.3 collective-permute-done.4
  19.5 1.1 %collective-permute-done.3 = f32[8,128]{1,0:T(8,128)S(1)} collective-permute-done((f32[8,128]{1,0:T(8,128)S(1)}, f32[8,128]{1,0:T(8,128)S(1)}, u32[]{:S(2)}, u32[]{:S(2)}) %collective-permute-start.3) | collective-permute-done | bytes 4128 | tf_op jit(solution)/shard_map/ppermute | solution.py:546
  20.6 0.1 maximum_maximum_fusion.own_ref
  20.7 1.8 %collective-permute-start.6 = (f32[8,128]{1,0:T(8,128)S(1)}, f32[8,128]{1,0:T(8,128)S(1)}, u32[]{:S(2)}, u32[]{:S(2)}) collective-permute-start(f32[8,128]{1,0:T(8,128)S(1)} %maximum_maximum_fusion.own_ref), channel_id=1, source_target_pairs={{0,1},{8,9},{16,17},{24,25},{1,0},{9,8},{17,16},{25,24},{2,3},{10,... | collective-permute-start | bytes 12296 | tf_op jit(solution)/shard_map/ppermute | solution.py:546
  22.5 0.6 %gains.1 = (f32[24,8,384]{2,1,0:T(8,128)S(1)}, f32[24,8,384]{2,1,0:T(8,128)S(1)}) custom-call(f32[192,128]{1,0:T(8,128)S(1)} %anchor_rows.1.own_ref, f32[192,128]{1,0:T(8,128)S(1)} %collective-permute-done.8.even_ref, f32[192,128]{1,0:T(8,128)S(1)} %collective-permute-done.9.odd_ref, bf16[384,384]{1,0:T(8,128)(2,1)S(1)} %copy-done.3), custom_call_target="tpu_custom_call" | custom-call | flops 1000000000 | bytes 1048576 | tf_op jit(solution)/shard_map/gains/pallas_call | solution.py:374
  23.1 1.2 %collective-permute-done.6.even_ref = f32[8,128]{1,0:T(8,128)S(1)} collective-permute-done((f32[8,128]{1,0:T(8,128)S(1)}, f32[8,128]{1,0:T(8,128)S(1)}, u32[]{:S(2)}, u32[]{:S(2)}) %collective-permute-start.6) | collective-permute-done | bytes 4128 | tf_op jit(solution)/shard_map/ppermute | solution.py:546
  24.4 3.8 %relax.1 = (f32[24,8,384]{2,1,0:T(8,128)S(1)}, f32[8,128]{1,0:T(8,128)S(1)}) custom-call(f32[8,128]{1,0:T(8,128)S(1)} %maximum_maximum_fusion.own_ref, f32[8,128]{1,0:T(8,128)S(1)} %collective-permute-done.6.even_ref, f32[8,128]{1,0:T(8,128)S(1)} %collective-permute-done.7.odd_ref, f32[24,8,384]{2,1,0:T(8,128)S(1)} %get-tuple-element.27.gain_ref, ...), custom_call_target="tpu_custom_call" | custom-call | flops 4000000000 | bytes 3145728 | tf_op jit(solution)/shard_map/relax/pallas_call | solution.py:462
  28.3 1.8 %collective-permute-start.11 = (f32[8,128]{1,0:T(8,128)S(1)}, f32[8,128]{1,0:T(8,128)S(1)}, u32[]{:S(2)}, u32[]{:S(2)}) collective-permute-start(f32[8,128]{1,0:T(8,128)S(1)} %get-tuple-element.32.refs_0_), channel_id=1, source_target_pairs={{0,16},{8,24},{16,0},{24,8},{1,17},{9,25},{17,1},{25,9},{2,18},{10... | collective-permute-start | bytes 12296 | tf_op jit(solution)/shard_map/ppermute | solution.py:605
  30.2 1.0 %natural_mesh.1 = f32[1,2,128,128]{3,2,1,0:T(8,128)} custom-call(f32[24,8,384]{2,1,0:T(8,128)S(1)} %get-tuple-element.29.ring_ref, bf16[384,256]{1,0:T(8,128)(2,1)S(1)} %copy-done.6), custom_call_target="tpu_custom_call" | custom-call | flops 1000000000 | bytes 1048576 | tf_op jit(solution)/shard_map/natural_mesh/pallas_call | solution.py:487
  31.2 0.8 %collective-permute-done.11.refs_2_ = f32[8,128]{1,0:T(8,128)S(1)} collective-permute-done((f32[8,128]{1,0:T(8,128)S(1)}, f32[8,128]{1,0:T(8,128)S(1)}, u32[]{:S(2)}, u32[]{:S(2)}) %collective-permute-start.11) | collective-permute-done | bytes 4128 | tf_op jit(solution)/shard_map/ppermute | solution.py:605
  32.0 1.2 %collective-permute-done.12.refs_3_ = f32[8,128]{1,0:T(8,128)S(1)} collective-permute-done((f32[8,128]{1,0:T(8,128)S(1)}, f32[8,128]{1,0:T(8,128)S(1)}, u32[]{:S(2)}, u32[]{:S(2)}) %collective-permute-start.12) | collective-permute-done | bytes 4128 | tf_op jit(solution)/shard_map/ppermute | solution.py:605
  33.2 0.8 %compose.1 = f32[1,1,1,2,128]{4,3,2,1,0:T(2,128)} custom-call(f32[8,128]{1,0:T(8,128)S(1)} %get-tuple-element.32.refs_0_, f32[8,128]{1,0:T(8,128)S(1)} %collective-permute-done.10.refs_1_, f32[8,128]{1,0:T(8,128)S(1)} %collective-permute-done.11.refs_2_, f32[8,128]{1,0:T(8,128)S(1)} %collective-permute-done.12.refs_3_), custom_call_target="tpu_custom_call" | custom-call | tf_op jit(solution)/shard_map/compose/pallas_call | solution.py:522
  (37 shorter events, 0.3 us)
Async XLA Ops:
  0.6 3.2 %collective-permute-start.1 = (bf16[512,512]{1,0:T(8,128)(2,1)}, bf16[512,512]{1,0:T(8,128)(2,1)S(1)}, u32[]{:S(2)}, u32[]{:S(2)}) collective-permute-start(bf16[512,512]{1,0:T(8,128)(2,1)} %bitcast.4), channel_id=1, source_target_pairs={{0,8},{4,12},{8,0},{12,4},{16,24},{20,28},{24,16},{28,20},{1,9},{5... | collective-permute-start | bytes 1572872 | tf_op jit(solution)/shard_map/ppermute | solution.py:546
  1.1 10.7 %collective-permute-start = (bf16[512,512]{1,0:T(8,128)(2,1)}, bf16[512,512]{1,0:T(8,128)(2,1)S(1)}, u32[]{:S(2)}, u32[]{:S(2)}) collective-permute-start(bf16[512,512]{1,0:T(8,128)(2,1)} %bitcast.5), channel_id=1, source_target_pairs={{0,4},{4,0},{8,16},{12,20},{16,8},{20,12},{24,28},{28,24},{1,5},{5... | collective-permute-start | bytes 1572872 | tf_op jit(solution)/shard_map/ppermute | solution.py:546
  3.7 2.3 %copy-start.1 = (bf16[1,512,512]{2,1,0:T(8,128)(2,1)S(1)}, bf16[1,512,512]{2,1,0:T(8,128)(2,1)}, u32[]{:S(2)}) copy-start(bf16[1,512,512]{2,1,0:T(8,128)(2,1)} %param.10) | copy-start | bytes 1572868
  3.7 11.1 %collective-permute-start.2 = (f32[128,128]{1,0:T(8,128)}, f32[128,128]{1,0:T(8,128)S(1)}, u32[]{:S(2)}, u32[]{:S(2)}) collective-permute-start(f32[128,128]{1,0:T(8,128)} %bitcast.2), channel_id=1, source_target_pairs={{0,4},{8,12},{16,20},{24,28},{4,0},{12,8},{20,16},{28,24},{1,5},{9... | collective-permute-start | bytes 196616 | tf_op jit(solution)/shard_map/ppermute | solution.py:546
  3.8 1.0 %copy-start.4 = (bf16[8,128,128]{2,1,0:T(8,128)(2,1)S(1)}, bf16[8,128,128]{2,1,0:T(8,128)(2,1)}, u32[]{:S(2)}) copy-start(bf16[8,128,128]{2,1,0:T(8,128)(2,1)} %constant.25.clone.tables_ref) | copy-start | bytes 786436
  4.8 1.2 %copy-start.5 = (bf16[8,128,128]{2,1,0:T(8,128)(2,1)S(1)}, bf16[8,128,128]{2,1,0:T(8,128)(2,1)}, u32[]{:S(2)}) copy-start(bf16[8,128,128]{2,1,0:T(8,128)(2,1)} %constant.25.clone.tables_ref) | copy-start | bytes 786436
  6.1 5.8 %copy-start.2 = (bf16[512,512]{1,0:T(8,128)(2,1)S(1)}, bf16[512,512]{1,0:T(8,128)(2,1)}, u32[]{:S(2)}) copy-start(bf16[512,512]{1,0:T(8,128)(2,1)} %edge_ref.1) | copy-start | bytes 1572868
  11.8 5.7 %copy-start = (f32[1,128,128]{2,1,0:T(8,128)S(1)}, f32[1,128,128]{2,1,0:T(8,128)}, u32[]{:S(2)}) copy-start(f32[1,128,128]{2,1,0:T(8,128)} %param.12) | copy-start | bytes 196612
  14.9 7.7 %copy-start.3 = (bf16[384,384]{1,0:T(8,128)(2,1)S(1)}, bf16[384,384]{1,0:T(8,128)(2,1)}, u32[]{:S(2)}) copy-start(bf16[384,384]{1,0:T(8,128)(2,1)} %constant.26.clone.into_ref) | copy-start | bytes 884740
  14.9 4.3 %collective-permute-start.5 = (f32[8,128]{1,0:T(8,128)S(1)}, f32[8,128]{1,0:T(8,128)S(1)}, u32[]{:S(2)}, u32[]{:S(2)}) collective-permute-start(f32[8,128]{1,0:T(8,128)S(1)} %flows.1), channel_id=1, source_target_pairs={{0,8},{8,16},{16,24},{24,0},{1,9},{9,17},{17,25},{25,1},{2,10},{10... | collective-permute-start | bytes 12296 | tf_op jit(solution)/shard_map/ppermute | solution.py:563
  15.1 4.5 %collective-permute-start.4 = (f32[8,128]{1,0:T(8,128)S(1)}, f32[8,128]{1,0:T(8,128)S(1)}, u32[]{:S(2)}, u32[]{:S(2)}) collective-permute-start(f32[8,128]{1,0:T(8,128)S(1)} %flows.1), channel_id=1, source_target_pairs={{0,12},{4,8},{8,20},{12,16},{16,28},{20,24},{24,4},{28,0},{1,13},{... | collective-permute-start | bytes 12296 | tf_op jit(solution)/shard_map/ppermute | solution.py:565
  17.0 3.6 %collective-permute-start.3 = (f32[8,128]{1,0:T(8,128)S(1)}, f32[8,128]{1,0:T(8,128)S(1)}, u32[]{:S(2)}, u32[]{:S(2)}) collective-permute-start(f32[8,128]{1,0:T(8,128)S(1)} %flows.1), channel_id=1, source_target_pairs={{0,4},{8,12},{16,20},{24,28},{4,0},{12,8},{20,16},{28,24},{1,5},{9... | collective-permute-start | bytes 12296 | tf_op jit(solution)/shard_map/ppermute | solution.py:546
  17.5 5.0 %collective-permute-start.8 = (f32[192,128]{1,0:T(8,128)S(1)}, f32[192,128]{1,0:T(8,128)S(1)}, u32[]{:S(2)}, u32[]{:S(2)}) collective-permute-start(f32[192,128]{1,0:T(8,128)S(1)} %anchor_rows.1.own_ref), channel_id=1, source_target_pairs={{0,1},{8,9},{16,17},{24,25},{1,0},{9,8},{17,16},{25,24},{2,3},{10,... | collective-permute-start | bytes 294920 | tf_op jit(solution)/shard_map/ppermute | solution.py:546
  19.2 3.4 %collective-permute-start.9 = (f32[192,128]{1,0:T(8,128)S(1)}, f32[192,128]{1,0:T(8,128)S(1)}, u32[]{:S(2)}, u32[]{:S(2)}) collective-permute-start(f32[192,128]{1,0:T(8,128)S(1)} %anchor_rows.1.own_ref), channel_id=1, source_target_pairs={{0,8},{8,0},{16,24},{24,16},{1,2},{9,10},{17,18},{25,26},{2,1},{10... | collective-permute-start | bytes 294920 | tf_op jit(solution)/shard_map/ppermute | solution.py:546
  20.7 3.7 %copy-start.7 = (bf16[144,384]{1,0:T(8,128)(2,1)S(1)}, bf16[144,384]{1,0:T(8,128)(2,1)}, u32[]{:S(2)}) copy-start(bf16[144,384]{1,0:T(8,128)(2,1)} %constant.28.clone.right_ref) | copy-start | bytes 331780
  20.7 3.7 %copy-start.8 = (bf16[192,144]{1,0:T(8,128)(2,1)S(1)}, bf16[192,144]{1,0:T(8,128)(2,1)}, u32[]{:S(2)}) copy-start(bf16[192,144]{1,0:T(8,128)(2,1)} %constant.27.clone.left_ref) | copy-start | bytes 165892
  20.7 3.7 %copy-start.9 = (bf16[384,128]{1,0:T(8,128)(2,1)S(1)}, bf16[384,128]{1,0:T(8,128)(2,1)}, u32[]{:S(2)}) copy-start(bf16[384,128]{1,0:T(8,128)(2,1)} %constant.29.clone.cols_table_ref) | copy-start | bytes 294916
  20.7 3.7 %copy-start.10 = (bf16[192,128]{1,0:T(8,128)(2,1)S(1)}, bf16[192,128]{1,0:T(8,128)(2,1)}, u32[]{:S(2)}) copy-start(bf16[192,128]{1,0:T(8,128)(2,1)} %constant.30.clone.rows_table_ref) | copy-start | bytes 147460
  20.7 3.7 %collective-permute-start.6 = (f32[8,128]{1,0:T(8,128)S(1)}, f32[8,128]{1,0:T(8,128)S(1)}, u32[]{:S(2)}, u32[]{:S(2)}) collective-permute-start(f32[8,128]{1,0:T(8,128)S(1)} %maximum_maximum_fusion.own_ref), channel_id=1, source_target_pairs={{0,1},{8,9},{16,17},{24,25},{1,0},{9,8},{17,16},{25,24},{2,3},{10,... | collective-permute-start | bytes 12296 | tf_op jit(solution)/shard_map/ppermute | solution.py:546
  22.5 1.9 %collective-permute-start.7 = (f32[8,128]{1,0:T(8,128)S(1)}, f32[8,128]{1,0:T(8,128)S(1)}, u32[]{:S(2)}, u32[]{:S(2)}) collective-permute-start(f32[8,128]{1,0:T(8,128)S(1)} %maximum_maximum_fusion.own_ref), channel_id=1, source_target_pairs={{0,8},{8,0},{16,24},{24,16},{1,2},{9,10},{17,18},{25,26},{2,1},{10... | collective-permute-start | bytes 12296 | tf_op jit(solution)/shard_map/ppermute | solution.py:546
  24.4 5.8 %copy-start.6 = (bf16[384,256]{1,0:T(8,128)(2,1)S(1)}, bf16[384,256]{1,0:T(8,128)(2,1)}, u32[]{:S(2)}) copy-start(bf16[384,256]{1,0:T(8,128)(2,1)} %constant.31.clone.table_ref) | copy-start | bytes 589828
  28.2 3.0 %collective-permute-start.10 = (f32[8,128]{1,0:T(8,128)S(1)}, f32[8,128]{1,0:T(8,128)S(1)}, u32[]{:S(2)}, u32[]{:S(2)}) collective-permute-start(f32[8,128]{1,0:T(8,128)S(1)} %get-tuple-element.32.refs_0_), channel_id=1, source_target_pairs={{0,8},{8,0},{16,24},{24,16},{1,9},{9,1},{17,25},{25,17},{2,10},{10... | collective-permute-start | bytes 12296 | tf_op jit(solution)/shard_map/ppermute | solution.py:605
  28.3 3.7 %collective-permute-start.11 = (f32[8,128]{1,0:T(8,128)S(1)}, f32[8,128]{1,0:T(8,128)S(1)}, u32[]{:S(2)}, u32[]{:S(2)}) collective-permute-start(f32[8,128]{1,0:T(8,128)S(1)} %get-tuple-element.32.refs_0_), channel_id=1, source_target_pairs={{0,16},{8,24},{16,0},{24,8},{1,17},{9,25},{17,1},{25,9},{2,18},{10... | collective-permute-start | bytes 12296 | tf_op jit(solution)/shard_map/ppermute | solution.py:605
  30.2 3.0 %collective-permute-start.12 = (f32[8,128]{1,0:T(8,128)S(1)}, f32[8,128]{1,0:T(8,128)S(1)}, u32[]{:S(2)}, u32[]{:S(2)}) collective-permute-start(f32[8,128]{1,0:T(8,128)S(1)} %get-tuple-element.32.refs_0_), channel_id=1, source_target_pairs={{0,24},{8,16},{16,8},{24,0},{1,25},{9,17},{17,9},{25,1},{2,26},{10... | collective-permute-start | bytes 12296 | tf_op jit(solution)/shard_map/ppermute | solution.py:605

commit v6 on v5

--- a/solution.py
+++ b/solution.py
@@ -34,17 +34,17 @@
     return jnp.asarray(np.stack(tables))
 
 
-def pair_tables(tables_ref):
+def product_tables(tables_ref):
+    forward_table = jnp.concatenate([tables_ref[0], tables_ref[1]], axis=1)
+    inverse = jnp.concatenate([tables_ref[2], tables_ref[3]], axis=1)
+    return [forward_table, jnp.concatenate([inverse, inverse], axis=0)]
+
+
+def paired_patches(first, second):
     lower = lax.broadcasted_iota(jnp.int32, (PATCH, PATCH), 1) < HALF
-    pairs = []
-    for index in range(2):
-        table = tables_ref[index].astype(F32)
-        turned = pltpu.roll(table, HALF, 1)
-        first = jnp.concatenate([jnp.where(lower, table, 0.0), jnp.where(lower, turned, 0.0)], axis=1)
-        second = jnp.concatenate([jnp.where(lower, 0.0, turned), jnp.where(lower, 0.0, table)], axis=1)
-        pairs.append(jnp.concatenate([first, second], axis=0).astype(BF16))
-    inverse = jnp.concatenate([tables_ref[2], tables_ref[3]], axis=1)
-    return pairs + [jnp.concatenate([inverse, inverse], axis=0)]
+    cosine = jnp.where(lower, first, pltpu.roll(second, HALF, 1))
+    sine = jnp.where(lower, pltpu.roll(first, HALF, 1), second)
+    return [cosine, sine]
 
 
 def single_patches(product):
@@ -112,33 +112,35 @@
 
 
 def windows(rows, cols):
-    wide = 2 * PATCH
-    return [(slice(r, r + PATCH), slice(c, c + wide)) for r in range(0, rows, PATCH) for c in range(0, cols, wide)]
+    return [(slice(r, r + PATCH), slice(c, c + PATCH)) for r in range(0, rows, PATCH) for c in range(0, cols, PATCH)]
 
 
 def side_by_side(value):
     return jnp.concatenate([value[i : i + PATCH] for i in range(0, value.shape[0], PATCH)], axis=1)
 
 
-def forward(pixels, pairs, tables_ref):
-    right = dot(pixels, pairs[0]) + dot(pixels, pairs[1])
-    return left_transform(tables_ref[4], tables_ref[5], side_by_side(right))
-
-
-def image_spectra(image_ref, pairs, tables_ref):
+def forward(pixels, table, tables_ref):
+    both = dot(pixels, table)
+    right = both[:, :PATCH] + both[:, PATCH:]
+    singles = [right[i : i + PATCH] for i in range(0, right.shape[0], PATCH)]
+    tiles = [tile for i in range(0, len(singles), 2) for tile in paired_patches(*singles[i : i + 2])]
+    return left_transform(tables_ref[4], tables_ref[5], jnp.concatenate(tiles, axis=1))
+
+
+def image_spectra(image_ref, table, tables_ref):
     pixels = jnp.concatenate([image_ref[window] for window in windows(*image_ref.shape)], axis=0)
-    return forward(pixels, pairs, tables_ref)
-
-
-def near_kernel(image_ref, tables_ref, spec_out, pairs_out):
-    pairs = pair_tables(tables_ref)
-    for index, pair in enumerate(pairs):
-        pairs_out[index] = pair
-    spec_out[...] = image_spectra(image_ref, pairs, tables_ref)
-
-
-def own_kernel(image_ref, pairs_ref, tables_ref, spec_out):
-    spec_out[...] = image_spectra(image_ref, pairs_ref, tables_ref)
+    return forward(pixels, table, tables_ref)
+
+
+def near_kernel(image_ref, tables_ref, spec_out, forward_out, inverse_out):
+    table, inverse = product_tables(tables_ref)
+    forward_out[...] = table
+    inverse_out[...] = inverse
+    spec_out[...] = image_spectra(image_ref, table, tables_ref)
+
+
+def own_kernel(image_ref, forward_ref, tables_ref, spec_out):
+    spec_out[...] = image_spectra(image_ref, forward_ref[...], tables_ref)
 
 
 def rows_kernel(up_ref, own_ref, down_ref, out_ref):
@@ -149,18 +151,18 @@
 
 
 def flows_kernel(
-    far_ref, edge_ref, own_spec, near_spec, rights_ref, tables_ref, out_ref, stats_ref
+    far_ref, edge_ref, own_spec, near_spec, forward_ref, inverse_ref, tables_ref, out_ref, stats_ref
 ):
     wide = 2 * PATCH
     spots = windows(*far_ref.shape)
-    blocks = len(spots)
-    patches = 2 * blocks
+    patches = len(spots)
+    blocks = patches // 2
     at_edge = lax.axis_index("gz") == 0
     at_even = lax.axis_index("gz") % 2 == 0
     pixels = jnp.concatenate(
         [jnp.where(at_edge, edge_ref[spot].astype(F32), far_ref[spot].astype(F32)).astype(BF16) for spot in spots], axis=0
     )
-    spec = forward(pixels, rights_ref, tables_ref)
+    spec = forward(pixels, forward_ref[...], tables_ref)
     products = []
     for block in range(blocks):
         lanes = slice(block * wide, (block + 1) * wide)
@@ -169,7 +171,7 @@
         products.append(cross(operand, own_spec[:, lanes]))
         products.append(cross(operand, jnp.where(at_even, near, far)))
     singles = [single for product in products for single in single_patches(product)]
-    both = dot(jnp.concatenate(halves(jnp.concatenate(singles, axis=0)), axis=1), rights_ref[2])
+    both = dot(jnp.concatenate(halves(jnp.concatenate(singles, axis=0)), axis=1), inverse_ref[...])
     back = both[:, :PATCH] + both[:, PATCH:]
     scores = left_transform(tables_ref[6], tables_ref[7], side_by_side(back))
     groups = scores.reshape(PATCH // 8, 8, 2 * blocks * wide)
@@ -227,19 +229,20 @@
 
 
 def near_spectra(near, tables):
-    pairs = jax.ShapeDtypeStruct((3, 2 * PATCH, 2 * PATCH), BF16)
+    forward_table = jax.ShapeDtypeStruct((PATCH, 2 * PATCH), BF16)
+    inverse_table = jax.ShapeDtypeStruct((2 * PATCH, 2 * PATCH), BF16)
     return pl.pallas_call(
         near_kernel,
-        out_shape=(spec_shape(near), pairs),
+        out_shape=(spec_shape(near), forward_table, inverse_table),
         in_specs=[VMEM] * 2,
-        out_specs=(VMEM, VMEM),
+        out_specs=(VMEM,) * 3,
         compiler_params=PARAMS,
         cost_estimate=pl.CostEstimate(flops=2 * 10**9, bytes_accessed=2 * 2**20, transcendentals=0),
         name="near_spectra",
     )(near, tables)
 
 
-def own_spectra(own, pairs, tables):
+def own_spectra(own, forward_table, tables):
     return pl.pallas_call(
         own_kernel,
         out_shape=spec_shape(own),
@@ -248,7 +251,7 @@
         compiler_params=PARAMS,
         cost_estimate=pl.CostEstimate(flops=10**9, bytes_accessed=2 * 2**20, transcendentals=0),
         name="own_spectra",
-    )(own, pairs, tables)
+    )(own, forward_table, tables)
 
 
 def anchor_rows(up, own, down):
@@ -264,17 +267,18 @@
 
 
 def flows(far, edge, own_spec, near_spec, pairs, tables):
+    forward_table, inverse_table = pairs
     patches = far.shape[0] // PATCH * (far.shape[1] // PATCH)
     return pl.pallas_call(
         flows_kernel,
         out_shape=jax.ShapeDtypeStruct((8, PATCH), F32),
-        in_specs=[VMEM] * 6,
+        in_specs=[VMEM] * 7,
         out_specs=VMEM,
         scratch_shapes=[pltpu.VMEM((3, 2 * patches, 8, PATCH), F32)],
         compiler_params=PARAMS,
         cost_estimate=pl.CostEstimate(flops=4 * 10**9, bytes_accessed=3 * 2**20, transcendentals=0),
         name="flows",
-    )(far, edge, own_spec, near_spec, pairs, tables)
+    )(far, edge, own_spec, near_spec, forward_table, inverse_table, tables)
 
 
 def spread_weights(nodes, patches):
@@ -430,7 +434,7 @@
             above, here = here, below
         return carry
 
-    lax.fori_loop(0, SWEEPS, sweep, 0, unroll=16)
+    lax.fori_loop(0, SWEEPS, sweep, 0, unroll=32)
     mesh = work_ref[...].reshape(strips * 8, lanes)
     ones = jnp.where(ring_place(16, lanes) < nodes, 1.0, 0.0).astype(BF16)
     sums = None
@@ -590,8 +594,8 @@
     far = swap_pairs(own, "gz", 1, "ty")
     near = swap_pairs(own, "gz", 0, "ty")
     up, down = rows_beside(anchor[0])
-    near_spec, pairs = near_spectra(near, tables)
-    own_spec = own_spectra(own, pairs, tables)
+    near_spec, *pairs = near_spectra(near, tables)
+    own_spec = own_spectra(own, pairs[0], tables)
     far, own_spec, near_spec = lax.optimization_barrier((far, own_spec, near_spec))
     flow = flows(far, boundary, own_spec, near_spec, pairs, tables)
     flow, up, down = lax.optimization_barrier((flow, up, down))

time: 34.6 us -> 34.3 us (level)
  Pallas kernels: 11.5 us -> 10.8 us
  waiting for transfers between devices: 9.28 us -> 9.7 us
    ppermute x8, waiting for transfers between devices: 6.97 us -> 7.39 us  [swap_pairs(): return lax.ppermute(value, (spare, axis) if flip else (axis, spare), moves)]
  transfers between devices with their start and end apart: 13 -> 13, of which waited for: 6 -> 6; matrix products, arithmetic and copies ran while one was open for 0% -> 0% of each run, Pallas kernels for 20% -> 19%
where the time goes in v6:
time: 34.3 us; the launch traced here: 33.7 us
  starting transfers between devices  11.2 us (33%)
  Pallas kernels  10.8 us (31%)
  waiting for transfers between devices  9.7 us (28%)
  local copies, waits for them, and re-layouts  1.12 us (3%)
  between operations  0.79 us (2%)
    ppermute x8, waiting for transfers between devices, swap_pairs(): return lax.ppermute(value, (spare, axis) if flip else (axis, spare), moves)  7.39 us
    ppermute x8, starting transfers between devices, swap_pairs(): return lax.ppermute(value, (spare, axis) if flip else (axis, spare), moves)  7.2 us
    pallas_call x1, Pallas kernels, relax(): pl.pallas_call(relax_kernel, out_shape=(jax.ShapeDtypeStruct(shape, F32),...  3.66 us
    pallas_call x1, Pallas kernels, flows(): pl.pallas_call(flows_kernel, out_shape=jax.ShapeDtypeStruct((8, PATCH), F...  2.93 us
    ppermute x3, starting transfers between devices, local(): lax.ppermute(landing, 'gz', [(i, i ^ code) for i in range(sections)])  1.99 us
    ppermute x3, waiting for transfers between devices, local(): lax.ppermute(landing, 'gz', [(i, i ^ code) for i in range(sections)])  1.98 us
    ppermute x1, starting transfers between devices, to_next(): return lax.ppermute(value, ('gz', 'ty'), moves)  1.93 us
    unnamed x22, local copies, waits for them, and re-layouts  1.05 us
  transfers between devices with their start and end apart: 13, of which 6 were waited for; matrix products, arithmetic and copies ran while one was open for 0% of the time, Pallas kernels for 19%

profile of v6, /device:TPU:0, one launch (start us, length us, event | category | flops | bytes accessed | tf_op | source)
XLA Modules:
  0.0 33.7 jit_solution(2246343016416012182)
XLA Ops:
  0.6 0.5 %collective-permute-start.1 = (bf16[512,512]{1,0:T(8,128)(2,1)}, bf16[512,512]{1,0:T(8,128)(2,1)S(1)}, u32[]{:S(2)}, u32[]{:S(2)}) collective-permute-start(bf16[512,512]{1,0:T(8,128)(2,1)} %bitcast.4), channel_id=1, source_target_pairs={{0,8},{4,12},{8,0},{12,4},{16,24},{20,28},{24,16},{28,20},{1,9},{5... | collective-permute-start | bytes 1572872 | tf_op jit(solution)/shard_map/ppermute | solution.py:550
  1.1 2.6 %collective-permute-start = (bf16[512,512]{1,0:T(8,128)(2,1)}, bf16[512,512]{1,0:T(8,128)(2,1)S(1)}, u32[]{:S(2)}, u32[]{:S(2)}) collective-permute-start(bf16[512,512]{1,0:T(8,128)(2,1)} %bitcast.5), channel_id=1, source_target_pairs={{0,4},{4,0},{8,16},{12,20},{16,8},{20,12},{24,28},{28,24},{1,5},{5... | collective-permute-start | bytes 1572872 | tf_op jit(solution)/shard_map/ppermute | solution.py:550
  3.7 0.1 collective-permute-start.2
  3.8 1.0 %copy-done.4 = bf16[8,128,128]{2,1,0:T(8,128)(2,1)S(1)} copy-done((bf16[8,128,128]{2,1,0:T(8,128)(2,1)S(1)}, bf16[8,128,128]{2,1,0:T(8,128)(2,1)}, u32[]{:S(2)}) %copy-start.4) | copy-done | bytes 262168
  4.8 0.9 %near_spectra.1 = (f32[128,2048]{1,0:T(8,128)S(1)}, bf16[128,256]{1,0:T(8,128)(2,1)S(1)}, bf16[256,256]{1,0:T(8,128)(2,1)S(1)}) custom-call(bf16[512,512]{1,0:T(8,128)(2,1)S(1)} %collective-permute-done.1.image_ref, bf16[8,128,128]{2,1,0:T(8,128)(2,1)S(1)} %copy-done.4), custom_call_target="tpu_custom_call" | custom-call | flops 2000000000 | bytes 2097152 | tf_op jit(solution)/shard_map/near_spectra/pallas_call | solution.py:234
  5.8 0.9 %own_spectra.1.own_spec = f32[128,2048]{1,0:T(8,128)S(1)} custom-call(bf16[512,512]{1,0:T(8,128)(2,1)S(1)} %bitcast.6, bf16[128,256]{1,0:T(8,128)(2,1)S(1)} %get-tuple-element.20.forward_ref, bf16[8,128,128]{2,1,0:T(8,128)(2,1)S(1)} %copy-done.5), custom_call_target="tpu_custom_call" | custom-call | flops 1000000000 | bytes 2097152 | tf_op jit(solution)/shard_map/own_spectra/pallas_call | solution.py:246
  6.8 5.0 %collective-permute-done.far_ref = bf16[512,512]{1,0:T(8,128)(2,1)S(1)} collective-permute-done((bf16[512,512]{1,0:T(8,128)(2,1)}, bf16[512,512]{1,0:T(8,128)(2,1)S(1)}, u32[]{:S(2)}, u32[]{:S(2)}) %collective-permute-start) | collective-permute-done | bytes 524320 | tf_op jit(solution)/shard_map/ppermute | solution.py:550
  11.8 2.9 %flows.1 = f32[8,128]{1,0:T(8,128)S(1)} custom-call(bf16[512,512]{1,0:T(8,128)(2,1)S(1)} %collective-permute-done.far_ref, bf16[512,512]{1,0:T(8,128)(2,1)S(1)} %copy-done.2, f32[128,2048]{1,0:T(8,128)S(1)} %own_spectra.1.own_spec, f32[128,2048]{1,0:T(8,128)S(1)} %get-tuple-element.24.near_spec, bf16[128,256]{1,0:T(8,128)(2,1)S(1)} %get-tuple-element.20.forward_ref, ...), custom_call_target="tpu_custom_call" | custom-call | flops 4000000000 | bytes 3145728 | tf_op jit(solution)/shard_map/flows/pallas_call | solution.py:272
  14.9 0.1 pad.3.clone
  14.9 1.9 %collective-permute-start.4 = (f32[8,128]{1,0:T(8,128)S(1)}, f32[8,128]{1,0:T(8,128)S(1)}, u32[]{:S(2)}, u32[]{:S(2)}) collective-permute-start(f32[8,128]{1,0:T(8,128)S(1)} %flows.1), channel_id=1, source_target_pairs={{0,12},{4,8},{8,20},{12,16},{16,28},{20,24},{24,4},{28,0},{1,13},{... | collective-permute-start | bytes 12296 | tf_op jit(solution)/shard_map/ppermute | solution.py:569
  16.9 0.5 %collective-permute-start.3 = (f32[8,128]{1,0:T(8,128)S(1)}, f32[8,128]{1,0:T(8,128)S(1)}, u32[]{:S(2)}, u32[]{:S(2)}) collective-permute-start(f32[8,128]{1,0:T(8,128)S(1)} %flows.1), channel_id=1, source_target_pairs={{0,4},{8,12},{16,20},{24,28},{4,0},{12,8},{20,16},{28,24},{1,5},{9... | collective-permute-start | bytes 12296 | tf_op jit(solution)/shard_map/ppermute | solution.py:550
  17.4 1.6 %collective-permute-start.8 = (f32[192,128]{1,0:T(8,128)S(1)}, f32[192,128]{1,0:T(8,128)S(1)}, u32[]{:S(2)}, u32[]{:S(2)}) collective-permute-start(f32[192,128]{1,0:T(8,128)S(1)} %anchor_rows.1.own_ref), channel_id=1, source_target_pairs={{0,1},{8,9},{16,17},{24,25},{1,0},{9,8},{17,16},{25,24},{2,3},{10,... | collective-permute-start | bytes 294920 | tf_op jit(solution)/shard_map/ppermute | solution.py:550
  19.1 0.3 collective-permute-done.4
  19.4 1.1 %collective-permute-done.3 = f32[8,128]{1,0:T(8,128)S(1)} collective-permute-done((f32[8,128]{1,0:T(8,128)S(1)}, f32[8,128]{1,0:T(8,128)S(1)}, u32[]{:S(2)}, u32[]{:S(2)}) %collective-permute-start.3) | collective-permute-done | bytes 4128 | tf_op jit(solution)/shard_map/ppermute | solution.py:550
  20.5 0.1 maximum_maximum_fusion.own_ref
  20.6 1.8 %collective-permute-start.6 = (f32[8,128]{1,0:T(8,128)S(1)}, f32[8,128]{1,0:T(8,128)S(1)}, u32[]{:S(2)}, u32[]{:S(2)}) collective-permute-start(f32[8,128]{1,0:T(8,128)S(1)} %maximum_maximum_fusion.own_ref), channel_id=1, source_target_pairs={{0,1},{8,9},{16,17},{24,25},{1,0},{9,8},{17,16},{25,24},{2,3},{10,... | collective-permute-start | bytes 12296 | tf_op jit(solution)/shard_map/ppermute | solution.py:550
  22.4 0.6 %gains.1 = (f32[24,8,384]{2,1,0:T(8,128)S(1)}, f32[24,8,384]{2,1,0:T(8,128)S(1)}) custom-call(f32[192,128]{1,0:T(8,128)S(1)} %anchor_rows.1.own_ref, f32[192,128]{1,0:T(8,128)S(1)} %collective-permute-done.8.even_ref, f32[192,128]{1,0:T(8,128)S(1)} %collective-permute-done.9.odd_ref, bf16[384,384]{1,0:T(8,128)(2,1)S(1)} %copy-done.3), custom_call_target="tpu_custom_call" | custom-call | flops 1000000000 | bytes 1048576 | tf_op jit(solution)/shard_map/gains/pallas_call | solution.py:378
  23.0 1.2 %collective-permute-done.6.even_ref = f32[8,128]{1,0:T(8,128)S(1)} collective-permute-done((f32[8,128]{1,0:T(8,128)S(1)}, f32[8,128]{1,0:T(8,128)S(1)}, u32[]{:S(2)}, u32[]{:S(2)}) %collective-permute-start.6) | collective-permute-done | bytes 4128 | tf_op jit(solution)/shard_map/ppermute | solution.py:550
  24.3 3.7 %relax.1 = (f32[24,8,384]{2,1,0:T(8,128)S(1)}, f32[8,128]{1,0:T(8,128)S(1)}) custom-call(f32[8,128]{1,0:T(8,128)S(1)} %maximum_maximum_fusion.own_ref, f32[8,128]{1,0:T(8,128)S(1)} %collective-permute-done.6.even_ref, f32[8,128]{1,0:T(8,128)S(1)} %collective-permute-done.7.odd_ref, f32[24,8,384]{2,1,0:T(8,128)S(1)} %get-tuple-element.29.gain_ref, ...), custom_call_target="tpu_custom_call" | custom-call | flops 4000000000 | bytes 3145728 | tf_op jit(solution)/shard_map/relax/pallas_call | solution.py:466
  28.0 1.9 %collective-permute-start.11 = (f32[8,128]{1,0:T(8,128)S(1)}, f32[8,128]{1,0:T(8,128)S(1)}, u32[]{:S(2)}, u32[]{:S(2)}) collective-permute-start(f32[8,128]{1,0:T(8,128)S(1)} %get-tuple-element.34.refs_0_), channel_id=1, source_target_pairs={{0,16},{8,24},{16,0},{24,8},{1,17},{9,25},{17,1},{25,9},{2,18},{10... | collective-permute-start | bytes 12296 | tf_op jit(solution)/shard_map/ppermute | solution.py:609
  30.0 1.0 %natural_mesh.1 = f32[1,2,128,128]{3,2,1,0:T(8,128)} custom-call(f32[24,8,384]{2,1,0:T(8,128)S(1)} %get-tuple-element.31.ring_ref, bf16[384,256]{1,0:T(8,128)(2,1)S(1)} %copy-done.6), custom_call_target="tpu_custom_call" | custom-call | flops 1000000000 | bytes 1048576 | tf_op jit(solution)/shard_map/natural_mesh/pallas_call | solution.py:491
  31.0 0.8 %collective-permute-done.11.refs_2_ = f32[8,128]{1,0:T(8,128)S(1)} collective-permute-done((f32[8,128]{1,0:T(8,128)S(1)}, f32[8,128]{1,0:T(8,128)S(1)}, u32[]{:S(2)}, u32[]{:S(2)}) %collective-permute-start.11) | collective-permute-done | bytes 4128 | tf_op jit(solution)/shard_map/ppermute | solution.py:609
  31.7 1.2 %collective-permute-done.12.refs_3_ = f32[8,128]{1,0:T(8,128)S(1)} collective-permute-done((f32[8,128]{1,0:T(8,128)S(1)}, f32[8,128]{1,0:T(8,128)S(1)}, u32[]{:S(2)}, u32[]{:S(2)}) %collective-permute-start.12) | collective-permute-done | bytes 4128 | tf_op jit(solution)/shard_map/ppermute | solution.py:609
  32.9 0.8 %compose.1 = f32[1,1,1,2,128]{4,3,2,1,0:T(2,128)} custom-call(f32[8,128]{1,0:T(8,128)S(1)} %get-tuple-element.34.refs_0_, f32[8,128]{1,0:T(8,128)S(1)} %collective-permute-done.10.refs_1_, f32[8,128]{1,0:T(8,128)S(1)} %collective-permute-done.11.refs_2_, f32[8,128]{1,0:T(8,128)S(1)} %collective-permute-done.12.refs_3_), custom_call_target="tpu_custom_call" | custom-call | tf_op jit(solution)/shard_map/compose/pallas_call | solution.py:526
  (37 shorter events, 0.3 us)
Async XLA Ops:
  0.6 3.2 %collective-permute-start.1 = (bf16[512,512]{1,0:T(8,128)(2,1)}, bf16[512,512]{1,0:T(8,128)(2,1)S(1)}, u32[]{:S(2)}, u32[]{:S(2)}) collective-permute-start(bf16[512,512]{1,0:T(8,128)(2,1)} %bitcast.4), channel_id=1, source_target_pairs={{0,8},{4,12},{8,0},{12,4},{16,24},{20,28},{24,16},{28,20},{1,9},{5... | collective-permute-start | bytes 1572872 | tf_op jit(solution)/shard_map/ppermute | solution.py:550
  1.1 10.7 %collective-permute-start = (bf16[512,512]{1,0:T(8,128)(2,1)}, bf16[512,512]{1,0:T(8,128)(2,1)S(1)}, u32[]{:S(2)}, u32[]{:S(2)}) collective-permute-start(bf16[512,512]{1,0:T(8,128)(2,1)} %bitcast.5), channel_id=1, source_target_pairs={{0,4},{4,0},{8,16},{12,20},{16,8},{20,12},{24,28},{28,24},{1,5},{5... | collective-permute-start | bytes 1572872 | tf_op jit(solution)/shard_map/ppermute | solution.py:550
  3.7 2.1 %copy-start.1 = (bf16[1,512,512]{2,1,0:T(8,128)(2,1)S(1)}, bf16[1,512,512]{2,1,0:T(8,128)(2,1)}, u32[]{:S(2)}) copy-start(bf16[1,512,512]{2,1,0:T(8,128)(2,1)} %param.10) | copy-start | bytes 1572868
  3.7 11.0 %collective-permute-start.2 = (f32[128,128]{1,0:T(8,128)}, f32[128,128]{1,0:T(8,128)S(1)}, u32[]{:S(2)}, u32[]{:S(2)}) collective-permute-start(f32[128,128]{1,0:T(8,128)} %bitcast.2), channel_id=1, source_target_pairs={{0,4},{8,12},{16,20},{24,28},{4,0},{12,8},{20,16},{28,24},{1,5},{9... | collective-permute-start | bytes 196616 | tf_op jit(solution)/shard_map/ppermute | solution.py:550
  3.8 1.0 %copy-start.4 = (bf16[8,128,128]{2,1,0:T(8,128)(2,1)S(1)}, bf16[8,128,128]{2,1,0:T(8,128)(2,1)}, u32[]{:S(2)}) copy-start(bf16[8,128,128]{2,1,0:T(8,128)(2,1)} %constant.25.clone.tables_ref) | copy-start | bytes 786436
  4.8 1.0 %copy-start.5 = (bf16[8,128,128]{2,1,0:T(8,128)(2,1)S(1)}, bf16[8,128,128]{2,1,0:T(8,128)(2,1)}, u32[]{:S(2)}) copy-start(bf16[8,128,128]{2,1,0:T(8,128)(2,1)} %constant.25.clone.tables_ref) | copy-start | bytes 786436
  5.8 6.0 %copy-start.2 = (bf16[512,512]{1,0:T(8,128)(2,1)S(1)}, bf16[512,512]{1,0:T(8,128)(2,1)}, u32[]{:S(2)}) copy-start(bf16[512,512]{1,0:T(8,128)(2,1)} %edge_ref.1) | copy-start | bytes 1572868
  11.8 5.6 %copy-start = (f32[1,128,128]{2,1,0:T(8,128)S(1)}, f32[1,128,128]{2,1,0:T(8,128)}, u32[]{:S(2)}) copy-start(f32[1,128,128]{2,1,0:T(8,128)} %param.12) | copy-start | bytes 196612
  14.8 7.7 %copy-start.3 = (bf16[384,384]{1,0:T(8,128)(2,1)S(1)}, bf16[384,384]{1,0:T(8,128)(2,1)}, u32[]{:S(2)}) copy-start(bf16[384,384]{1,0:T(8,128)(2,1)} %constant.26.clone.into_ref) | copy-start | bytes 884740
  14.8 4.3 %collective-permute-start.5 = (f32[8,128]{1,0:T(8,128)S(1)}, f32[8,128]{1,0:T(8,128)S(1)}, u32[]{:S(2)}, u32[]{:S(2)}) collective-permute-start(f32[8,128]{1,0:T(8,128)S(1)} %flows.1), channel_id=1, source_target_pairs={{0,8},{8,16},{16,24},{24,0},{1,9},{9,17},{17,25},{25,1},{2,10},{10... | collective-permute-start | bytes 12296 | tf_op jit(solution)/shard_map/ppermute | solution.py:567
  14.9 4.5 %collective-permute-start.4 = (f32[8,128]{1,0:T(8,128)S(1)}, f32[8,128]{1,0:T(8,128)S(1)}, u32[]{:S(2)}, u32[]{:S(2)}) collective-permute-start(f32[8,128]{1,0:T(8,128)S(1)} %flows.1), channel_id=1, source_target_pairs={{0,12},{4,8},{8,20},{12,16},{16,28},{20,24},{24,4},{28,0},{1,13},{... | collective-permute-start | bytes 12296 | tf_op jit(solution)/shard_map/ppermute | solution.py:569
  16.9 3.6 %collective-permute-start.3 = (f32[8,128]{1,0:T(8,128)S(1)}, f32[8,128]{1,0:T(8,128)S(1)}, u32[]{:S(2)}, u32[]{:S(2)}) collective-permute-start(f32[8,128]{1,0:T(8,128)S(1)} %flows.1), channel_id=1, source_target_pairs={{0,4},{8,12},{16,20},{24,28},{4,0},{12,8},{20,16},{28,24},{1,5},{9... | collective-permute-start | bytes 12296 | tf_op jit(solution)/shard_map/ppermute | solution.py:550
  17.4 5.0 %collective-permute-start.8 = (f32[192,128]{1,0:T(8,128)S(1)}, f32[192,128]{1,0:T(8,128)S(1)}, u32[]{:S(2)}, u32[]{:S(2)}) collective-permute-start(f32[192,128]{1,0:T(8,128)S(1)} %anchor_rows.1.own_ref), channel_id=1, source_target_pairs={{0,1},{8,9},{16,17},{24,25},{1,0},{9,8},{17,16},{25,24},{2,3},{10,... | collective-permute-start | bytes 294920 | tf_op jit(solution)/shard_map/ppermute | solution.py:550
  19.1 3.4 %collective-permute-start.9 = (f32[192,128]{1,0:T(8,128)S(1)}, f32[192,128]{1,0:T(8,128)S(1)}, u32[]{:S(2)}, u32[]{:S(2)}) collective-permute-start(f32[192,128]{1,0:T(8,128)S(1)} %anchor_rows.1.own_ref), channel_id=1, source_target_pairs={{0,8},{8,0},{16,24},{24,16},{1,2},{9,10},{17,18},{25,26},{2,1},{10... | collective-permute-start | bytes 294920 | tf_op jit(solution)/shard_map/ppermute | solution.py:550
  20.6 3.7 %copy-start.7 = (bf16[144,384]{1,0:T(8,128)(2,1)S(1)}, bf16[144,384]{1,0:T(8,128)(2,1)}, u32[]{:S(2)}) copy-start(bf16[144,384]{1,0:T(8,128)(2,1)} %constant.28.clone.right_ref) | copy-start | bytes 331780
  20.6 3.7 %copy-start.8 = (bf16[192,144]{1,0:T(8,128)(2,1)S(1)}, bf16[192,144]{1,0:T(8,128)(2,1)}, u32[]{:S(2)}) copy-start(bf16[192,144]{1,0:T(8,128)(2,1)} %constant.27.clone.left_ref) | copy-start | bytes 165892
  20.6 3.7 %copy-start.9 = (bf16[384,128]{1,0:T(8,128)(2,1)S(1)}, bf16[384,128]{1,0:T(8,128)(2,1)}, u32[]{:S(2)}) copy-start(bf16[384,128]{1,0:T(8,128)(2,1)} %constant.29.clone.cols_table_ref) | copy-start | bytes 294916
  20.6 3.7 %copy-start.10 = (bf16[192,128]{1,0:T(8,128)(2,1)S(1)}, bf16[192,128]{1,0:T(8,128)(2,1)}, u32[]{:S(2)}) copy-start(bf16[192,128]{1,0:T(8,128)(2,1)} %constant.30.clone.rows_table_ref) | copy-start | bytes 147460
  20.6 3.7 %collective-permute-start.6 = (f32[8,128]{1,0:T(8,128)S(1)}, f32[8,128]{1,0:T(8,128)S(1)}, u32[]{:S(2)}, u32[]{:S(2)}) collective-permute-start(f32[8,128]{1,0:T(8,128)S(1)} %maximum_maximum_fusion.own_ref), channel_id=1, source_target_pairs={{0,1},{8,9},{16,17},{24,25},{1,0},{9,8},{17,16},{25,24},{2,3},{10,... | collective-permute-start | bytes 12296 | tf_op jit(solution)/shard_map/ppermute | solution.py:550
  22.4 1.9 %collective-permute-start.7 = (f32[8,128]{1,0:T(8,128)S(1)}, f32[8,128]{1,0:T(8,128)S(1)}, u32[]{:S(2)}, u32[]{:S(2)}) collective-permute-start(f32[8,128]{1,0:T(8,128)S(1)} %maximum_maximum_fusion.own_ref), channel_id=1, source_target_pairs={{0,8},{8,0},{16,24},{24,16},{1,2},{9,10},{17,18},{25,26},{2,1},{10... | collective-permute-start | bytes 12296 | tf_op jit(solution)/shard_map/ppermute | solution.py:550
  24.3 5.7 %copy-start.6 = (bf16[384,256]{1,0:T(8,128)(2,1)S(1)}, bf16[384,256]{1,0:T(8,128)(2,1)}, u32[]{:S(2)}) copy-start(bf16[384,256]{1,0:T(8,128)(2,1)} %constant.31.clone.table_ref) | copy-start | bytes 589828
  28.0 3.0 %collective-permute-start.10 = (f32[8,128]{1,0:T(8,128)S(1)}, f32[8,128]{1,0:T(8,128)S(1)}, u32[]{:S(2)}, u32[]{:S(2)}) collective-permute-start(f32[8,128]{1,0:T(8,128)S(1)} %get-tuple-element.34.refs_0_), channel_id=1, source_target_pairs={{0,8},{8,0},{16,24},{24,16},{1,9},{9,1},{17,25},{25,17},{2,10},{10... | collective-permute-start | bytes 12296 | tf_op jit(solution)/shard_map/ppermute | solution.py:609
  28.0 3.7 %collective-permute-start.11 = (f32[8,128]{1,0:T(8,128)S(1)}, f32[8,128]{1,0:T(8,128)S(1)}, u32[]{:S(2)}, u32[]{:S(2)}) collective-permute-start(f32[8,128]{1,0:T(8,128)S(1)} %get-tuple-element.34.refs_0_), channel_id=1, source_target_pairs={{0,16},{8,24},{16,0},{24,8},{1,17},{9,25},{17,1},{25,9},{2,18},{10... | collective-permute-start | bytes 12296 | tf_op jit(solution)/shard_map/ppermute | solution.py:609
  29.9 3.0 %collective-permute-start.12 = (f32[8,128]{1,0:T(8,128)S(1)}, f32[8,128]{1,0:T(8,128)S(1)}, u32[]{:S(2)}, u32[]{:S(2)}) collective-permute-start(f32[8,128]{1,0:T(8,128)S(1)} %get-tuple-element.34.refs_0_), channel_id=1, source_target_pairs={{0,24},{8,16},{16,8},{24,0},{1,25},{9,17},{17,9},{25,1},{2,26},{10... | collective-permute-start | bytes 12296 | tf_op jit(solution)/shard_map/ppermute | solution.py:609

commit v7 on v6

--- a/solution.py
+++ b/solution.py
@@ -388,14 +388,17 @@
 
 
 def relax_kernel(
-    own_ref, even_ref, odd_ref, gain_ref, pull_ref, left_ref, right_ref, cols_table_ref, rows_table_ref,
+    up_ref, own_ref, down_ref, up_earlier_ref, earlier_ref, down_earlier_ref, gain_ref, pull_ref, left_ref, right_ref, cols_table_ref, rows_table_ref,
     work_ref, landing_ref, base_ref,
 ):
     strips, _, lanes = work_ref.shape
     nodes = landing_ref.shape[1]
     patches = left_ref.shape[1] // 9
-    before, after = tiles_beside(even_ref, odd_ref)
-    rows = [before[:3], own_ref[:3], after[:3]]
+    first = lax.axis_index("gz") <= 1
+    lines = []
+    for near, past in ((up_ref, up_earlier_ref), (own_ref, earlier_ref), (down_ref, down_earlier_ref)):
+        lines.append(jnp.where(first, near[:3], 0.5 * (near[:3] + past[3:6])))
+    rows = [line[tile : tile + 1] for tile in range(3) for line in lines]
     rows.append(jnp.zeros((PATCH - 9, PATCH), F32))
     columns = jnp.transpose(jnp.concatenate(rows, axis=0))
 
@@ -466,7 +469,7 @@
     return pl.pallas_call(
         relax_kernel,
         out_shape=(jax.ShapeDtypeStruct(shape, F32), jax.ShapeDtypeStruct((8, nodes), F32)),
-        in_specs=[VMEM] * 9,
+        in_specs=[VMEM] * 12,
         out_specs=(VMEM, VMEM),
         scratch_shapes=[pltpu.VMEM(shape, F32)],
         compiler_params=PARAMS,
@@ -569,20 +572,19 @@
     return lax.ppermute(value, ("gz", "ty"), moves)
 
 
-def patch_targets(flow):
-    first = lax.axis_index("gz") <= 1
-    before = to_next(flow, 0)
-
-    def target(near, earlier):
-        return jnp.where(first, near[0:1], 0.5 * (near[0:1] + earlier[1:2]))
-
+def flow_lines(flow):
+    even, odd = swap_pairs(flow, "tx", 0, "gz"), swap_pairs(flow, "tx", 1, "gz")
+    at_even = lax.axis_index("tx") % 2 == 0
+    before, after = jnp.where(at_even, odd, even), jnp.where(at_even, even, odd)
+    tiles = (before, flow, after)
+    lines = [tile[row : row + 1] for row in range(2) for tile in tiles]
+    lines = jnp.concatenate(lines + [flow[:2]], axis=0)
+    earlier = to_next(lines, 0)
     if lax.axis_size("ty") == 2:
-        beside = target(rows_beside(flow)[0], to_next(flow, 1))
-        lines = [beside, target(flow, before), beside]
-    else:
-        (up, down), (up_before, down_before) = rows_beside(flow), rows_beside(before)
-        lines = [target(up, up_before), target(flow, before), target(down, down_before)]
-    return jnp.concatenate(lines + [jnp.zeros((5, flow.shape[1]), F32)], axis=0)
+        beside, beside_earlier = rows_beside(lines)[0], to_next(lines, 1)
+        return (beside, lines, beside, beside_earlier, earlier, beside_earlier)
+    (up, down), (up_earlier, down_earlier) = rows_beside(lines), rows_beside(earlier)
+    return (up, lines, down, up_earlier, earlier, down_earlier)
 
 
 def local(images, boundary, anchor):
@@ -601,8 +603,7 @@
     flow, up, down = lax.optimization_barrier((flow, up, down))
     rows = anchor_rows(up, anchor[0], down)
     weights = gains(rows, swap_pairs(rows, "tx", 0, "gz"), swap_pairs(rows, "tx", 1, "gz"), nodes)
-    line = patch_targets(flow)
-    targets = (line, swap_pairs(line, "tx", 0, "gz"), swap_pairs(line, "tx", 1, "gz"))
+    targets = flow_lines(flow)
     ring, landing = relax(targets, weights, nodes, patches)
     landings = [landing]
     for code in range(1, sections):

time: 34.3 us -> 34.3 us (level); the launches traced: 33.7 us -> 34.1 us
  starting transfers between devices: 11.2 us -> 12.4 us
  waiting for transfers between devices: 9.7 us -> 8.91 us
    ppermute x8, starting transfers between devices: 7.2 us -> 10.1 us  [swap_pairs(): return lax.ppermute(value, (spare, axis) if flip else (axis, spare), moves)]
    ppermute x1, starting transfers between devices: 1.93 us -> 0.33 us  [to_next(): return lax.ppermute(value, ('gz', 'ty'), moves)]
    ppermute x1, waiting for transfers between devices: 0.33 us -> 1.84 us  [to_next(): return lax.ppermute(value, ('gz', 'ty'), moves)]
    ppermute x8, waiting for transfers between devices: 7.39 us -> 6.24 us  [swap_pairs(): return lax.ppermute(value, (spare, axis) if flip else (axis, spare), moves)]
    ppermute x3, waiting for transfers between devices: 1.98 us -> 0.83 us  [local(): lax.ppermute(landing, 'gz', [(i, i ^ code) for i in range(sections)])]
    unnamed x22 -> x20, local copies, waits for them, and re-layouts: 1.05 us -> 1.06 us
  transfers between devices with their start and end apart: 13 -> 13, of which waited for: 6 -> 5; matrix products, arithmetic and copies ran while one was open for 0% -> 0% of each run, Pallas kernels for 19% -> 19%
where the time goes in v7:
time: 34.3 us; the launch traced here: 34.1 us
  starting transfers between devices  12.4 us (36%)
  Pallas kernels  10.9 us (32%)
  waiting for transfers between devices  8.91 us (26%)
  local copies, waits for them, and re-layouts  1.1 us (3%)
  between operations  0.81 us (2%)
    ppermute x8, starting transfers between devices, swap_pairs(): return lax.ppermute(value, (spare, axis) if flip else (axis, spare), moves)  10.1 us
    ppermute x8, waiting for transfers between devices, swap_pairs(): return lax.ppermute(value, (spare, axis) if flip else (axis, spare), moves)  6.24 us
    pallas_call x1, Pallas kernels, relax(): pl.pallas_call(relax_kernel, out_shape=(jax.ShapeDtypeStruct(shape, F32),...  3.59 us
    pallas_call x1, Pallas kernels, flows(): pl.pallas_call(flows_kernel, out_shape=jax.ShapeDtypeStruct((8, PATCH), F...  3.09 us
    ppermute x3, starting transfers between devices, local(): lax.ppermute(landing, 'gz', [(i, i ^ code) for i in range(sections)])  1.93 us
    ppermute x1, waiting for transfers between devices, to_next(): return lax.ppermute(value, ('gz', 'ty'), moves)  1.84 us
    unnamed x20, local copies, waits for them, and re-layouts  1.06 us
    pallas_call x1, Pallas kernels, natural_mesh(): pl.pallas_call(mesh_kernel, out_shape=jax.ShapeDtypeStruct((1, 2, nodes,...  0.98 us
  transfers between devices with their start and end apart: 13, of which 5 were waited for; matrix products, arithmetic and copies ran while one was open for 0% of the time, Pallas kernels for 19%

profile of v7, /device:TPU:0, one launch (start us, length us, event | category | flops | bytes accessed | tf_op | source)
XLA Modules:
  0.0 34.1 jit_solution(3603521808536618713)
XLA Ops:
  0.6 0.5 %collective-permute-start.1 = (bf16[512,512]{1,0:T(8,128)(2,1)}, bf16[512,512]{1,0:T(8,128)(2,1)S(1)}, u32[]{:S(2)}, u32[]{:S(2)}) collective-permute-start(bf16[512,512]{1,0:T(8,128)(2,1)} %bitcast.4), channel_id=1, source_target_pairs={{0,8},{4,12},{8,0},{12,4},{16,24},{20,28},{24,16},{28,20},{1,9},{5... | collective-permute-start | bytes 1572872 | tf_op jit(solution)/shard_map/ppermute | solution.py:553
  1.1 2.6 %collective-permute-start = (bf16[512,512]{1,0:T(8,128)(2,1)}, bf16[512,512]{1,0:T(8,128)(2,1)S(1)}, u32[]{:S(2)}, u32[]{:S(2)}) collective-permute-start(bf16[512,512]{1,0:T(8,128)(2,1)} %bitcast.5), channel_id=1, source_target_pairs={{0,4},{4,0},{8,16},{12,20},{16,8},{20,12},{24,28},{28,24},{1,5},{5... | collective-permute-start | bytes 1572872 | tf_op jit(solution)/shard_map/ppermute | solution.py:553
  3.7 0.1 collective-permute-start.2
  3.8 1.0 %copy-done.4 = bf16[8,128,128]{2,1,0:T(8,128)(2,1)S(1)} copy-done((bf16[8,128,128]{2,1,0:T(8,128)(2,1)S(1)}, bf16[8,128,128]{2,1,0:T(8,128)(2,1)}, u32[]{:S(2)}) %copy-start.4) | copy-done | bytes 262168
  4.8 0.9 %near_spectra.1 = (f32[128,2048]{1,0:T(8,128)S(1)}, bf16[128,256]{1,0:T(8,128)(2,1)S(1)}, bf16[256,256]{1,0:T(8,128)(2,1)S(1)}) custom-call(bf16[512,512]{1,0:T(8,128)(2,1)S(1)} %collective-permute-done.1.image_ref, bf16[8,128,128]{2,1,0:T(8,128)(2,1)S(1)} %copy-done.4), custom_call_target="tpu_custom_call" | custom-call | flops 2000000000 | bytes 2097152 | tf_op jit(solution)/shard_map/near_spectra/pallas_call | solution.py:234
  5.8 0.9 %own_spectra.1.own_spec = f32[128,2048]{1,0:T(8,128)S(1)} custom-call(bf16[512,512]{1,0:T(8,128)(2,1)S(1)} %bitcast.6, bf16[128,256]{1,0:T(8,128)(2,1)S(1)} %get-tuple-element.20.forward_ref, bf16[8,128,128]{2,1,0:T(8,128)(2,1)S(1)} %copy-done.4), custom_call_target="tpu_custom_call" | custom-call | flops 1000000000 | bytes 2097152 | tf_op jit(solution)/shard_map/own_spectra/pallas_call | solution.py:246
  6.8 5.1 %collective-permute-done.far_ref = bf16[512,512]{1,0:T(8,128)(2,1)S(1)} collective-permute-done((bf16[512,512]{1,0:T(8,128)(2,1)}, bf16[512,512]{1,0:T(8,128)(2,1)S(1)}, u32[]{:S(2)}, u32[]{:S(2)}) %collective-permute-start) | collective-permute-done | bytes 524320 | tf_op jit(solution)/shard_map/ppermute | solution.py:553
  11.8 3.1 %flows.1 = f32[8,128]{1,0:T(8,128)S(1)} custom-call(bf16[512,512]{1,0:T(8,128)(2,1)S(1)} %collective-permute-done.far_ref, bf16[512,512]{1,0:T(8,128)(2,1)S(1)} %copy-done.2, f32[128,2048]{1,0:T(8,128)S(1)} %own_spectra.1.own_spec, f32[128,2048]{1,0:T(8,128)S(1)} %get-tuple-element.24.near_spec, bf16[128,256]{1,0:T(8,128)(2,1)S(1)} %get-tuple-element.20.forward_ref, ...), custom_call_target="tpu_custom_call" | custom-call | flops 4000000000 | bytes 3145728 | tf_op jit(solution)/shard_map/flows/pallas_call | solution.py:272
  14.9 0.0 copy-start.3
  14.9 2.1 %collective-permute-start.4 = (f32[8,128]{1,0:T(8,128)S(1)}, f32[8,128]{1,0:T(8,128)S(1)}, u32[]{:S(2)}, u32[]{:S(2)}) collective-permute-start(f32[8,128]{1,0:T(8,128)S(1)} %flows.1), channel_id=1, source_target_pairs={{0,1},{8,9},{16,17},{24,25},{1,0},{9,8},{17,16},{25,24},{2,3},{10,... | collective-permute-start | bytes 12296 | tf_op jit(solution)/shard_map/ppermute | solution.py:553
  17.1 3.2 %collective-permute-start.8 = (f32[192,128]{1,0:T(8,128)S(1)}, f32[192,128]{1,0:T(8,128)S(1)}, u32[]{:S(2)}, u32[]{:S(2)}) collective-permute-start(f32[192,128]{1,0:T(8,128)S(1)} %anchor_rows.1.own_ref), channel_id=1, source_target_pairs={{0,1},{8,9},{16,17},{24,25},{1,0},{9,8},{17,16},{25,24},{2,3},{10,... | collective-permute-start | bytes 294920 | tf_op jit(solution)/shard_map/ppermute | solution.py:553
  20.4 1.6 %collective-permute-start.5 = (f32[8,128]{1,0:T(8,128)S(1)}, f32[8,128]{1,0:T(8,128)S(1)}, u32[]{:S(2)}, u32[]{:S(2)}) collective-permute-start(f32[8,128]{1,0:T(8,128)S(1)} %concatenate.3.own_ref), channel_id=1, source_target_pairs={{0,4},{8,12},{16,20},{24,28},{4,0},{12,8},{20,16},{28,24},{1,5},{9... | collective-permute-start | bytes 12296 | tf_op jit(solution)/shard_map/ppermute | solution.py:553
  22.0 0.3 collective-permute-start.6
  22.4 0.6 %collective-permute-done.8.even_ref = f32[192,128]{1,0:T(8,128)S(1)} collective-permute-done((f32[192,128]{1,0:T(8,128)S(1)}, f32[192,128]{1,0:T(8,128)S(1)}, u32[]{:S(2)}, u32[]{:S(2)}) %collective-permute-start.8) | collective-permute-done | bytes 98336 | tf_op jit(solution)/shard_map/ppermute | solution.py:553
  22.9 0.6 %gains.1 = (f32[24,8,384]{2,1,0:T(8,128)S(1)}, f32[24,8,384]{2,1,0:T(8,128)S(1)}) custom-call(f32[192,128]{1,0:T(8,128)S(1)} %anchor_rows.1.own_ref, f32[192,128]{1,0:T(8,128)S(1)} %collective-permute-done.8.even_ref, f32[192,128]{1,0:T(8,128)S(1)} %collective-permute-done.9.odd_ref, bf16[384,384]{1,0:T(8,128)(2,1)S(1)} %copy-done.3), custom_call_target="tpu_custom_call" | custom-call | flops 1000000000 | bytes 1048576 | tf_op jit(solution)/shard_map/gains/pallas_call | solution.py:378
  23.5 0.6 %collective-permute-done.5.up_ref.down_ref = f32[8,128]{1,0:T(8,128)S(1)} collective-permute-done((f32[8,128]{1,0:T(8,128)S(1)}, f32[8,128]{1,0:T(8,128)S(1)}, u32[]{:S(2)}, u32[]{:S(2)}) %collective-permute-start.5) | collective-permute-done | bytes 4128 | tf_op jit(solution)/shard_map/ppermute | solution.py:553
  24.1 1.8 %collective-permute-done.6.up_earlier_ref.down_earlier_ref = f32[8,128]{1,0:T(8,128)S(1)} collective-permute-done((f32[8,128]{1,0:T(8,128)S(1)}, f32[8,128]{1,0:T(8,128)S(1)}, u32[]{:S(2)}, u32[]{:S(2)}) %collective-permute-start.6) | collective-permute-done | bytes 4128 | tf_op jit(solution)/shard_map/ppermute | solution.py:572
  26.0 3.6 %relax.1 = (f32[24,8,384]{2,1,0:T(8,128)S(1)}, f32[8,128]{1,0:T(8,128)S(1)}) custom-call(f32[8,128]{1,0:T(8,128)S(1)} %collective-permute-done.5.up_ref.down_ref, f32[8,128]{1,0:T(8,128)S(1)} %concatenate.3.own_ref, f32[8,128]{1,0:T(8,128)S(1)} %collective-permute-done.5.up_ref.down_ref, f32[8,128]{1,0:T(8,128)S(1)} %collective-permute-done.6.up_earlier_ref.down_earlier_ref, ...), custom_call_target="tpu_custom_call" | custom-call | flops 4000000000 | bytes 3145728 | tf_op jit(solution)/shard_map/relax/pallas_call | solution.py:469
  29.6 0.1 collective-permute-start.10
  29.7 0.3 collective-permute-start.11
  30.0 1.6 %collective-permute-start.12 = (f32[8,128]{1,0:T(8,128)S(1)}, f32[8,128]{1,0:T(8,128)S(1)}, u32[]{:S(2)}, u32[]{:S(2)}) collective-permute-start(f32[8,128]{1,0:T(8,128)S(1)} %get-tuple-element.34.refs_0_), channel_id=1, source_target_pairs={{0,24},{8,16},{16,8},{24,0},{1,25},{9,17},{17,9},{25,1},{2,26},{10... | collective-permute-start | bytes 12296 | tf_op jit(solution)/shard_map/ppermute | solution.py:610
  31.5 1.0 %natural_mesh.1 = f32[1,2,128,128]{3,2,1,0:T(8,128)} custom-call(f32[24,8,384]{2,1,0:T(8,128)S(1)} %get-tuple-element.31.ring_ref, bf16[384,256]{1,0:T(8,128)(2,1)S(1)} %copy-done.5), custom_call_target="tpu_custom_call" | custom-call | flops 1000000000 | bytes 1048576 | tf_op jit(solution)/shard_map/natural_mesh/pallas_call | solution.py:494
  32.5 0.8 %collective-permute-done.11.refs_2_ = f32[8,128]{1,0:T(8,128)S(1)} collective-permute-done((f32[8,128]{1,0:T(8,128)S(1)}, f32[8,128]{1,0:T(8,128)S(1)}, u32[]{:S(2)}, u32[]{:S(2)}) %collective-permute-start.11) | collective-permute-done | bytes 4128 | tf_op jit(solution)/shard_map/ppermute | solution.py:610
  33.4 0.8 %compose.1 = f32[1,1,1,2,128]{4,3,2,1,0:T(2,128)} custom-call(f32[8,128]{1,0:T(8,128)S(1)} %get-tuple-element.34.refs_0_, f32[8,128]{1,0:T(8,128)S(1)} %collective-permute-done.10.refs_1_, f32[8,128]{1,0:T(8,128)S(1)} %collective-permute-done.11.refs_2_, f32[8,128]{1,0:T(8,128)S(1)} %collective-permute-done.12.refs_3_), custom_call_target="tpu_custom_call" | custom-call | tf_op jit(solution)/shard_map/compose/pallas_call | solution.py:529
  (35 shorter events, 0.1 us)
Async XLA Ops:
  0.6 3.2 %collective-permute-start.1 = (bf16[512,512]{1,0:T(8,128)(2,1)}, bf16[512,512]{1,0:T(8,128)(2,1)S(1)}, u32[]{:S(2)}, u32[]{:S(2)}) collective-permute-start(bf16[512,512]{1,0:T(8,128)(2,1)} %bitcast.4), channel_id=1, source_target_pairs={{0,8},{4,12},{8,0},{12,4},{16,24},{20,28},{24,16},{28,20},{1,9},{5... | collective-permute-start | bytes 1572872 | tf_op jit(solution)/shard_map/ppermute | solution.py:553
  1.1 10.7 %collective-permute-start = (bf16[512,512]{1,0:T(8,128)(2,1)}, bf16[512,512]{1,0:T(8,128)(2,1)S(1)}, u32[]{:S(2)}, u32[]{:S(2)}) collective-permute-start(bf16[512,512]{1,0:T(8,128)(2,1)} %bitcast.5), channel_id=1, source_target_pairs={{0,4},{4,0},{8,16},{12,20},{16,8},{20,12},{24,28},{28,24},{1,5},{5... | collective-permute-start | bytes 1572872 | tf_op jit(solution)/shard_map/ppermute | solution.py:553
  3.7 11.2 %collective-permute-start.2 = (f32[128,128]{1,0:T(8,128)}, f32[128,128]{1,0:T(8,128)S(1)}, u32[]{:S(2)}, u32[]{:S(2)}) collective-permute-start(f32[128,128]{1,0:T(8,128)} %bitcast.2), channel_id=1, source_target_pairs={{0,4},{8,12},{16,20},{24,28},{4,0},{12,8},{20,16},{28,24},{1,5},{9... | collective-permute-start | bytes 196616 | tf_op jit(solution)/shard_map/ppermute | solution.py:553
  3.8 2.0 %copy-start.1 = (bf16[1,512,512]{2,1,0:T(8,128)(2,1)S(1)}, bf16[1,512,512]{2,1,0:T(8,128)(2,1)}, u32[]{:S(2)}) copy-start(bf16[1,512,512]{2,1,0:T(8,128)(2,1)} %param.10) | copy-start | bytes 1572868
  3.8 1.0 %copy-start.4 = (bf16[8,128,128]{2,1,0:T(8,128)(2,1)S(1)}, bf16[8,128,128]{2,1,0:T(8,128)(2,1)}, u32[]{:S(2)}) copy-start(bf16[8,128,128]{2,1,0:T(8,128)(2,1)} %constant.32.clone.tables_ref) | copy-start | bytes 786436
  5.8 6.0 %copy-start.2 = (bf16[512,512]{1,0:T(8,128)(2,1)S(1)}, bf16[512,512]{1,0:T(8,128)(2,1)}, u32[]{:S(2)}) copy-start(bf16[512,512]{1,0:T(8,128)(2,1)} %edge_ref.1) | copy-start | bytes 1572868
  11.8 5.3 %copy-start = (f32[1,128,128]{2,1,0:T(8,128)S(1)}, f32[1,128,128]{2,1,0:T(8,128)}, u32[]{:S(2)}) copy-start(f32[1,128,128]{2,1,0:T(8,128)} %param.12) | copy-start | bytes 196612
  14.9 8.0 %copy-start.3 = (bf16[384,384]{1,0:T(8,128)(2,1)S(1)}, bf16[384,384]{1,0:T(8,128)(2,1)}, u32[]{:S(2)}) copy-start(bf16[384,384]{1,0:T(8,128)(2,1)} %constant.33.clone.into_ref) | copy-start | bytes 884740
  14.9 5.4 %collective-permute-start.4 = (f32[8,128]{1,0:T(8,128)S(1)}, f32[8,128]{1,0:T(8,128)S(1)}, u32[]{:S(2)}, u32[]{:S(2)}) collective-permute-start(f32[8,128]{1,0:T(8,128)S(1)} %flows.1), channel_id=1, source_target_pairs={{0,1},{8,9},{16,17},{24,25},{1,0},{9,8},{17,16},{25,24},{2,3},{10,... | collective-permute-start | bytes 12296 | tf_op jit(solution)/shard_map/ppermute | solution.py:553
  17.1 3.3 %collective-permute-start.3 = (f32[8,128]{1,0:T(8,128)S(1)}, f32[8,128]{1,0:T(8,128)S(1)}, u32[]{:S(2)}, u32[]{:S(2)}) collective-permute-start(f32[8,128]{1,0:T(8,128)S(1)} %flows.1), channel_id=1, source_target_pairs={{0,8},{8,0},{16,24},{24,16},{1,2},{9,10},{17,18},{25,26},{2,1},{10... | collective-permute-start | bytes 12296 | tf_op jit(solution)/shard_map/ppermute | solution.py:553
  17.1 5.8 %collective-permute-start.8 = (f32[192,128]{1,0:T(8,128)S(1)}, f32[192,128]{1,0:T(8,128)S(1)}, u32[]{:S(2)}, u32[]{:S(2)}) collective-permute-start(f32[192,128]{1,0:T(8,128)S(1)} %anchor_rows.1.own_ref), channel_id=1, source_target_pairs={{0,1},{8,9},{16,17},{24,25},{1,0},{9,8},{17,16},{25,24},{2,3},{10,... | collective-permute-start | bytes 294920 | tf_op jit(solution)/shard_map/ppermute | solution.py:553
  20.3 2.6 %collective-permute-start.9 = (f32[192,128]{1,0:T(8,128)S(1)}, f32[192,128]{1,0:T(8,128)S(1)}, u32[]{:S(2)}, u32[]{:S(2)}) collective-permute-start(f32[192,128]{1,0:T(8,128)S(1)} %anchor_rows.1.own_ref), channel_id=1, source_target_pairs={{0,8},{8,0},{16,24},{24,16},{1,2},{9,10},{17,18},{25,26},{2,1},{10... | collective-permute-start | bytes 294920 | tf_op jit(solution)/shard_map/ppermute | solution.py:553
  20.4 5.6 %copy-start.6 = (bf16[144,384]{1,0:T(8,128)(2,1)S(1)}, bf16[144,384]{1,0:T(8,128)(2,1)}, u32[]{:S(2)}) copy-start(bf16[144,384]{1,0:T(8,128)(2,1)} %constant.35.clone.right_ref) | copy-start | bytes 331780
  20.4 5.6 %copy-start.7 = (bf16[192,144]{1,0:T(8,128)(2,1)S(1)}, bf16[192,144]{1,0:T(8,128)(2,1)}, u32[]{:S(2)}) copy-start(bf16[192,144]{1,0:T(8,128)(2,1)} %constant.34.clone.left_ref) | copy-start | bytes 165892
  20.4 5.6 %copy-start.8 = (bf16[384,128]{1,0:T(8,128)(2,1)S(1)}, bf16[384,128]{1,0:T(8,128)(2,1)}, u32[]{:S(2)}) copy-start(bf16[384,128]{1,0:T(8,128)(2,1)} %constant.36.clone.cols_table_ref) | copy-start | bytes 294916
  20.4 5.6 %copy-start.9 = (bf16[192,128]{1,0:T(8,128)(2,1)S(1)}, bf16[192,128]{1,0:T(8,128)(2,1)}, u32[]{:S(2)}) copy-start(bf16[192,128]{1,0:T(8,128)(2,1)} %constant.37.clone.rows_table_ref) | copy-start | bytes 147460
  20.4 3.7 %collective-permute-start.5 = (f32[8,128]{1,0:T(8,128)S(1)}, f32[8,128]{1,0:T(8,128)S(1)}, u32[]{:S(2)}, u32[]{:S(2)}) collective-permute-start(f32[8,128]{1,0:T(8,128)S(1)} %concatenate.3.own_ref), channel_id=1, source_target_pairs={{0,4},{8,12},{16,20},{24,28},{4,0},{12,8},{20,16},{28,24},{1,5},{9... | collective-permute-start | bytes 12296 | tf_op jit(solution)/shard_map/ppermute | solution.py:553
  22.0 3.9 %collective-permute-start.6 = (f32[8,128]{1,0:T(8,128)S(1)}, f32[8,128]{1,0:T(8,128)S(1)}, u32[]{:S(2)}, u32[]{:S(2)}) collective-permute-start(f32[8,128]{1,0:T(8,128)S(1)} %concatenate.3.own_ref), channel_id=1, source_target_pairs={{0,12},{4,8},{8,20},{12,16},{16,28},{20,24},{24,4},{28,0},{1,13},{... | collective-permute-start | bytes 12296 | tf_op jit(solution)/shard_map/ppermute | solution.py:572
  22.4 3.6 %collective-permute-start.7 = (f32[8,128]{1,0:T(8,128)S(1)}, f32[8,128]{1,0:T(8,128)S(1)}, u32[]{:S(2)}, u32[]{:S(2)}) collective-permute-start(f32[8,128]{1,0:T(8,128)S(1)} %concatenate.3.own_ref), channel_id=1, source_target_pairs={{0,8},{8,16},{16,24},{24,0},{1,9},{9,17},{17,25},{25,1},{2,10},{10... | collective-permute-start | bytes 12296 | tf_op jit(solution)/shard_map/ppermute | solution.py:570
  26.0 5.6 %copy-start.5 = (bf16[384,256]{1,0:T(8,128)(2,1)S(1)}, bf16[384,256]{1,0:T(8,128)(2,1)}, u32[]{:S(2)}) copy-start(bf16[384,256]{1,0:T(8,128)(2,1)} %constant.38.clone.table_ref) | copy-start | bytes 589828
  29.6 2.9 %collective-permute-start.10 = (f32[8,128]{1,0:T(8,128)S(1)}, f32[8,128]{1,0:T(8,128)S(1)}, u32[]{:S(2)}, u32[]{:S(2)}) collective-permute-start(f32[8,128]{1,0:T(8,128)S(1)} %get-tuple-element.34.refs_0_), channel_id=1, source_target_pairs={{0,8},{8,0},{16,24},{24,16},{1,9},{9,1},{17,25},{25,17},{2,10},{10... | collective-permute-start | bytes 12296 | tf_op jit(solution)/shard_map/ppermute | solution.py:610
  29.7 3.7 %collective-permute-start.11 = (f32[8,128]{1,0:T(8,128)S(1)}, f32[8,128]{1,0:T(8,128)S(1)}, u32[]{:S(2)}, u32[]{:S(2)}) collective-permute-start(f32[8,128]{1,0:T(8,128)S(1)} %get-tuple-element.34.refs_0_), channel_id=1, source_target_pairs={{0,16},{8,24},{16,0},{24,8},{1,17},{9,25},{17,1},{25,9},{2,18},{10... | collective-permute-start | bytes 12296 | tf_op jit(solution)/shard_map/ppermute | solution.py:610
  30.0 3.4 %collective-permute-start.12 = (f32[8,128]{1,0:T(8,128)S(1)}, f32[8,128]{1,0:T(8,128)S(1)}, u32[]{:S(2)}, u32[]{:S(2)}) collective-permute-start(f32[8,128]{1,0:T(8,128)S(1)} %get-tuple-element.34.refs_0_), channel_id=1, source_target_pairs={{0,24},{8,16},{16,8},{24,0},{1,25},{9,17},{17,9},{25,1},{2,26},{10... | collective-permute-start | bytes 12296 | tf_op jit(solution)/shard_map/ppermute | solution.py:610

commit v8 on v6

--- a/solution.py
+++ b/solution.py
@@ -178,11 +178,13 @@
     peak = jnp.max(groups, axis=0)
     total = jnp.zeros_like(peak)
     moment = jnp.zeros_like(peak)
-    for group in range(PATCH // 8):
-        weight = jnp.exp(groups[group] - peak)
-        shift = 8 * group - (PATCH if group >= PATCH // 16 else 0)
-        total = total + weight
-        moment = moment + float(shift) * weight
+    for group in reversed(range(PATCH // 8)):
+        total = total + jnp.exp(groups[group] - peak)
+        if group:
+            moment = moment + total
+        if group == PATCH // 16:
+            wrapped = total
+    moment = 8.0 * moment - float(PATCH) * wrapped
     for block in range(blocks):
         for pair in range(2):
             for side in range(2):

time: 34.3 us -> 34.3 us (level)
  no operation moved by 1% of the time
where the time goes in v8:
time: 34.3 us; the launch traced here: 33.7 us
  starting transfers between devices  11.2 us (33%)
  Pallas kernels  10.8 us (31%)
  waiting for transfers between devices  9.7 us (28%)
  local copies, waits for them, and re-layouts  1.12 us (3%)
  between operations  0.79 us (2%)
    ppermute x8, waiting for transfers between devices, swap_pairs(): return lax.ppermute(value, (spare, axis) if flip else (axis, spare), moves)  7.38 us
    ppermute x8, starting transfers between devices, swap_pairs(): return lax.ppermute(value, (spare, axis) if flip else (axis, spare), moves)  7.2 us
    pallas_call x1, Pallas kernels, relax(): pl.pallas_call(relax_kernel, out_shape=(jax.ShapeDtypeStruct(shape, F32),...  3.66 us
    pallas_call x1, Pallas kernels, flows(): pl.pallas_call(flows_kernel, out_shape=jax.ShapeDtypeStruct((8, PATCH), F...  2.88 us
    ppermute x3, starting transfers between devices, local(): lax.ppermute(landing, 'gz', [(i, i ^ code) for i in range(sections)])  2 us
    ppermute x3, waiting for transfers between devices, local(): lax.ppermute(landing, 'gz', [(i, i ^ code) for i in range(sections)])  1.98 us
    ppermute x1, starting transfers between devices, to_next(): return lax.ppermute(value, ('gz', 'ty'), moves)  1.93 us
    unnamed x22, local copies, waits for them, and re-layouts  1.05 us
  transfers between devices with their start and end apart: 13, of which 6 were waited for; matrix products, arithmetic and copies ran while one was open for 0% of the time, Pallas kernels for 19%

profile of v8, /device:TPU:0, one launch (start us, length us, event | category | flops | bytes accessed | tf_op | source)
XLA Modules:
  0.0 33.7 jit_solution(6443051102241948622)
XLA Ops:
  0.6 0.5 %collective-permute-start.1 = (bf16[512,512]{1,0:T(8,128)(2,1)}, bf16[512,512]{1,0:T(8,128)(2,1)S(1)}, u32[]{:S(2)}, u32[]{:S(2)}) collective-permute-start(bf16[512,512]{1,0:T(8,128)(2,1)} %bitcast.4), channel_id=1, source_target_pairs={{0,8},{4,12},{8,0},{12,4},{16,24},{20,28},{24,16},{28,20},{1,9},{5... | collective-permute-start | bytes 1572872 | tf_op jit(solution)/shard_map/ppermute | solution.py:552
  1.1 2.6 %collective-permute-start = (bf16[512,512]{1,0:T(8,128)(2,1)}, bf16[512,512]{1,0:T(8,128)(2,1)S(1)}, u32[]{:S(2)}, u32[]{:S(2)}) collective-permute-start(bf16[512,512]{1,0:T(8,128)(2,1)} %bitcast.5), channel_id=1, source_target_pairs={{0,4},{4,0},{8,16},{12,20},{16,8},{20,12},{24,28},{28,24},{1,5},{5... | collective-permute-start | bytes 1572872 | tf_op jit(solution)/shard_map/ppermute | solution.py:552
  3.7 0.1 collective-permute-start.2
  3.8 1.0 %copy-done.4 = bf16[8,128,128]{2,1,0:T(8,128)(2,1)S(1)} copy-done((bf16[8,128,128]{2,1,0:T(8,128)(2,1)S(1)}, bf16[8,128,128]{2,1,0:T(8,128)(2,1)}, u32[]{:S(2)}) %copy-start.4) | copy-done | bytes 262168
  4.8 0.9 %near_spectra.1 = (f32[128,2048]{1,0:T(8,128)S(1)}, bf16[128,256]{1,0:T(8,128)(2,1)S(1)}, bf16[256,256]{1,0:T(8,128)(2,1)S(1)}) custom-call(bf16[512,512]{1,0:T(8,128)(2,1)S(1)} %collective-permute-done.1.image_ref, bf16[8,128,128]{2,1,0:T(8,128)(2,1)S(1)} %copy-done.4), custom_call_target="tpu_custom_call" | custom-call | flops 2000000000 | bytes 2097152 | tf_op jit(solution)/shard_map/near_spectra/pallas_call | solution.py:236
  5.8 0.9 %own_spectra.1.own_spec = f32[128,2048]{1,0:T(8,128)S(1)} custom-call(bf16[512,512]{1,0:T(8,128)(2,1)S(1)} %bitcast.6, bf16[128,256]{1,0:T(8,128)(2,1)S(1)} %get-tuple-element.20.forward_ref, bf16[8,128,128]{2,1,0:T(8,128)(2,1)S(1)} %copy-done.5), custom_call_target="tpu_custom_call" | custom-call | flops 1000000000 | bytes 2097152 | tf_op jit(solution)/shard_map/own_spectra/pallas_call | solution.py:248
  6.8 5.0 %collective-permute-done.far_ref = bf16[512,512]{1,0:T(8,128)(2,1)S(1)} collective-permute-done((bf16[512,512]{1,0:T(8,128)(2,1)}, bf16[512,512]{1,0:T(8,128)(2,1)S(1)}, u32[]{:S(2)}, u32[]{:S(2)}) %collective-permute-start) | collective-permute-done | bytes 524320 | tf_op jit(solution)/shard_map/ppermute | solution.py:552
  11.8 2.9 %flows.1 = f32[8,128]{1,0:T(8,128)S(1)} custom-call(bf16[512,512]{1,0:T(8,128)(2,1)S(1)} %collective-permute-done.far_ref, bf16[512,512]{1,0:T(8,128)(2,1)S(1)} %copy-done.2, f32[128,2048]{1,0:T(8,128)S(1)} %own_spectra.1.own_spec, f32[128,2048]{1,0:T(8,128)S(1)} %get-tuple-element.24.near_spec, bf16[128,256]{1,0:T(8,128)(2,1)S(1)} %get-tuple-element.20.forward_ref, ...), custom_call_target="tpu_custom_call" | custom-call | flops 4000000000 | bytes 3145728 | tf_op jit(solution)/shard_map/flows/pallas_call | solution.py:274
  14.8 0.1 pad.3.clone
  14.9 1.9 %collective-permute-start.4 = (f32[8,128]{1,0:T(8,128)S(1)}, f32[8,128]{1,0:T(8,128)S(1)}, u32[]{:S(2)}, u32[]{:S(2)}) collective-permute-start(f32[8,128]{1,0:T(8,128)S(1)} %flows.1), channel_id=1, source_target_pairs={{0,12},{4,8},{8,20},{12,16},{16,28},{20,24},{24,4},{28,0},{1,13},{... | collective-permute-start | bytes 12296 | tf_op jit(solution)/shard_map/ppermute | solution.py:571
  16.8 0.5 %collective-permute-start.3 = (f32[8,128]{1,0:T(8,128)S(1)}, f32[8,128]{1,0:T(8,128)S(1)}, u32[]{:S(2)}, u32[]{:S(2)}) collective-permute-start(f32[8,128]{1,0:T(8,128)S(1)} %flows.1), channel_id=1, source_target_pairs={{0,4},{8,12},{16,20},{24,28},{4,0},{12,8},{20,16},{28,24},{1,5},{9... | collective-permute-start | bytes 12296 | tf_op jit(solution)/shard_map/ppermute | solution.py:552
  17.3 1.7 %collective-permute-start.8 = (f32[192,128]{1,0:T(8,128)S(1)}, f32[192,128]{1,0:T(8,128)S(1)}, u32[]{:S(2)}, u32[]{:S(2)}) collective-permute-start(f32[192,128]{1,0:T(8,128)S(1)} %anchor_rows.1.own_ref), channel_id=1, source_target_pairs={{0,1},{8,9},{16,17},{24,25},{1,0},{9,8},{17,16},{25,24},{2,3},{10,... | collective-permute-start | bytes 294920 | tf_op jit(solution)/shard_map/ppermute | solution.py:552
  19.0 0.3 collective-permute-done.4
  19.4 1.1 %collective-permute-done.3 = f32[8,128]{1,0:T(8,128)S(1)} collective-permute-done((f32[8,128]{1,0:T(8,128)S(1)}, f32[8,128]{1,0:T(8,128)S(1)}, u32[]{:S(2)}, u32[]{:S(2)}) %collective-permute-start.3) | collective-permute-done | bytes 4128 | tf_op jit(solution)/shard_map/ppermute | solution.py:552
  20.5 0.1 maximum_maximum_fusion.own_ref
  20.5 1.8 %collective-permute-start.6 = (f32[8,128]{1,0:T(8,128)S(1)}, f32[8,128]{1,0:T(8,128)S(1)}, u32[]{:S(2)}, u32[]{:S(2)}) collective-permute-start(f32[8,128]{1,0:T(8,128)S(1)} %maximum_maximum_fusion.own_ref), channel_id=1, source_target_pairs={{0,1},{8,9},{16,17},{24,25},{1,0},{9,8},{17,16},{25,24},{2,3},{10,... | collective-permute-start | bytes 12296 | tf_op jit(solution)/shard_map/ppermute | solution.py:552
  22.4 0.6 %gains.1 = (f32[24,8,384]{2,1,0:T(8,128)S(1)}, f32[24,8,384]{2,1,0:T(8,128)S(1)}) custom-call(f32[192,128]{1,0:T(8,128)S(1)} %anchor_rows.1.own_ref, f32[192,128]{1,0:T(8,128)S(1)} %collective-permute-done.8.even_ref, f32[192,128]{1,0:T(8,128)S(1)} %collective-permute-done.9.odd_ref, bf16[384,384]{1,0:T(8,128)(2,1)S(1)} %copy-done.3), custom_call_target="tpu_custom_call" | custom-call | flops 1000000000 | bytes 1048576 | tf_op jit(solution)/shard_map/gains/pallas_call | solution.py:380
  23.0 1.2 %collective-permute-done.6.even_ref = f32[8,128]{1,0:T(8,128)S(1)} collective-permute-done((f32[8,128]{1,0:T(8,128)S(1)}, f32[8,128]{1,0:T(8,128)S(1)}, u32[]{:S(2)}, u32[]{:S(2)}) %collective-permute-start.6) | collective-permute-done | bytes 4128 | tf_op jit(solution)/shard_map/ppermute | solution.py:552
  24.3 3.7 %relax.1 = (f32[24,8,384]{2,1,0:T(8,128)S(1)}, f32[8,128]{1,0:T(8,128)S(1)}) custom-call(f32[8,128]{1,0:T(8,128)S(1)} %maximum_maximum_fusion.own_ref, f32[8,128]{1,0:T(8,128)S(1)} %collective-permute-done.6.even_ref, f32[8,128]{1,0:T(8,128)S(1)} %collective-permute-done.7.odd_ref, f32[24,8,384]{2,1,0:T(8,128)S(1)} %get-tuple-element.29.gain_ref, ...), custom_call_target="tpu_custom_call" | custom-call | flops 4000000000 | bytes 3145728 | tf_op jit(solution)/shard_map/relax/pallas_call | solution.py:468
  28.0 1.9 %collective-permute-start.11 = (f32[8,128]{1,0:T(8,128)S(1)}, f32[8,128]{1,0:T(8,128)S(1)}, u32[]{:S(2)}, u32[]{:S(2)}) collective-permute-start(f32[8,128]{1,0:T(8,128)S(1)} %get-tuple-element.34.refs_0_), channel_id=1, source_target_pairs={{0,16},{8,24},{16,0},{24,8},{1,17},{9,25},{17,1},{25,9},{2,18},{10... | collective-permute-start | bytes 12296 | tf_op jit(solution)/shard_map/ppermute | solution.py:611
  29.9 1.0 %natural_mesh.1 = f32[1,2,128,128]{3,2,1,0:T(8,128)} custom-call(f32[24,8,384]{2,1,0:T(8,128)S(1)} %get-tuple-element.31.ring_ref, bf16[384,256]{1,0:T(8,128)(2,1)S(1)} %copy-done.6), custom_call_target="tpu_custom_call" | custom-call | flops 1000000000 | bytes 1048576 | tf_op jit(solution)/shard_map/natural_mesh/pallas_call | solution.py:493
  30.9 0.8 %collective-permute-done.11.refs_2_ = f32[8,128]{1,0:T(8,128)S(1)} collective-permute-done((f32[8,128]{1,0:T(8,128)S(1)}, f32[8,128]{1,0:T(8,128)S(1)}, u32[]{:S(2)}, u32[]{:S(2)}) %collective-permute-start.11) | collective-permute-done | bytes 4128 | tf_op jit(solution)/shard_map/ppermute | solution.py:611
  31.7 1.2 %collective-permute-done.12.refs_3_ = f32[8,128]{1,0:T(8,128)S(1)} collective-permute-done((f32[8,128]{1,0:T(8,128)S(1)}, f32[8,128]{1,0:T(8,128)S(1)}, u32[]{:S(2)}, u32[]{:S(2)}) %collective-permute-start.12) | collective-permute-done | bytes 4128 | tf_op jit(solution)/shard_map/ppermute | solution.py:611
  32.9 0.8 %compose.1 = f32[1,1,1,2,128]{4,3,2,1,0:T(2,128)} custom-call(f32[8,128]{1,0:T(8,128)S(1)} %get-tuple-element.34.refs_0_, f32[8,128]{1,0:T(8,128)S(1)} %collective-permute-done.10.refs_1_, f32[8,128]{1,0:T(8,128)S(1)} %collective-permute-done.11.refs_2_, f32[8,128]{1,0:T(8,128)S(1)} %collective-permute-done.12.refs_3_), custom_call_target="tpu_custom_call" | custom-call | tf_op jit(solution)/shard_map/compose/pallas_call | solution.py:528
  (37 shorter events, 0.3 us)
Async XLA Ops:
  0.6 3.2 %collective-permute-start.1 = (bf16[512,512]{1,0:T(8,128)(2,1)}, bf16[512,512]{1,0:T(8,128)(2,1)S(1)}, u32[]{:S(2)}, u32[]{:S(2)}) collective-permute-start(bf16[512,512]{1,0:T(8,128)(2,1)} %bitcast.4), channel_id=1, source_target_pairs={{0,8},{4,12},{8,0},{12,4},{16,24},{20,28},{24,16},{28,20},{1,9},{5... | collective-permute-start | bytes 1572872 | tf_op jit(solution)/shard_map/ppermute | solution.py:552
  1.1 10.7 %collective-permute-start = (bf16[512,512]{1,0:T(8,128)(2,1)}, bf16[512,512]{1,0:T(8,128)(2,1)S(1)}, u32[]{:S(2)}, u32[]{:S(2)}) collective-permute-start(bf16[512,512]{1,0:T(8,128)(2,1)} %bitcast.5), channel_id=1, source_target_pairs={{0,4},{4,0},{8,16},{12,20},{16,8},{20,12},{24,28},{28,24},{1,5},{5... | collective-permute-start | bytes 1572872 | tf_op jit(solution)/shard_map/ppermute | solution.py:552
  3.7 2.1 %copy-start.1 = (bf16[1,512,512]{2,1,0:T(8,128)(2,1)S(1)}, bf16[1,512,512]{2,1,0:T(8,128)(2,1)}, u32[]{:S(2)}) copy-start(bf16[1,512,512]{2,1,0:T(8,128)(2,1)} %param.10) | copy-start | bytes 1572868
  3.7 11.0 %collective-permute-start.2 = (f32[128,128]{1,0:T(8,128)}, f32[128,128]{1,0:T(8,128)S(1)}, u32[]{:S(2)}, u32[]{:S(2)}) collective-permute-start(f32[128,128]{1,0:T(8,128)} %bitcast.2), channel_id=1, source_target_pairs={{0,4},{8,12},{16,20},{24,28},{4,0},{12,8},{20,16},{28,24},{1,5},{9... | collective-permute-start | bytes 196616 | tf_op jit(solution)/shard_map/ppermute | solution.py:552
  3.8 1.0 %copy-start.4 = (bf16[8,128,128]{2,1,0:T(8,128)(2,1)S(1)}, bf16[8,128,128]{2,1,0:T(8,128)(2,1)}, u32[]{:S(2)}) copy-start(bf16[8,128,128]{2,1,0:T(8,128)(2,1)} %constant.25.clone.tables_ref) | copy-start | bytes 786436
  4.8 1.0 %copy-start.5 = (bf16[8,128,128]{2,1,0:T(8,128)(2,1)S(1)}, bf16[8,128,128]{2,1,0:T(8,128)(2,1)}, u32[]{:S(2)}) copy-start(bf16[8,128,128]{2,1,0:T(8,128)(2,1)} %constant.25.clone.tables_ref) | copy-start | bytes 786436
  5.8 6.0 %copy-start.2 = (bf16[512,512]{1,0:T(8,128)(2,1)S(1)}, bf16[512,512]{1,0:T(8,128)(2,1)}, u32[]{:S(2)}) copy-start(bf16[512,512]{1,0:T(8,128)(2,1)} %edge_ref.1) | copy-start | bytes 1572868
  11.8 5.5 %copy-start = (f32[1,128,128]{2,1,0:T(8,128)S(1)}, f32[1,128,128]{2,1,0:T(8,128)}, u32[]{:S(2)}) copy-start(f32[1,128,128]{2,1,0:T(8,128)} %param.12) | copy-start | bytes 196612
  14.7 7.7 %copy-start.3 = (bf16[384,384]{1,0:T(8,128)(2,1)S(1)}, bf16[384,384]{1,0:T(8,128)(2,1)}, u32[]{:S(2)}) copy-start(bf16[384,384]{1,0:T(8,128)(2,1)} %constant.26.clone.into_ref) | copy-start | bytes 884740
  14.7 4.3 %collective-permute-start.5 = (f32[8,128]{1,0:T(8,128)S(1)}, f32[8,128]{1,0:T(8,128)S(1)}, u32[]{:S(2)}, u32[]{:S(2)}) collective-permute-start(f32[8,128]{1,0:T(8,128)S(1)} %flows.1), channel_id=1, source_target_pairs={{0,8},{8,16},{16,24},{24,0},{1,9},{9,17},{17,25},{25,1},{2,10},{10... | collective-permute-start | bytes 12296 | tf_op jit(solution)/shard_map/ppermute | solution.py:569
  14.9 4.5 %collective-permute-start.4 = (f32[8,128]{1,0:T(8,128)S(1)}, f32[8,128]{1,0:T(8,128)S(1)}, u32[]{:S(2)}, u32[]{:S(2)}) collective-permute-start(f32[8,128]{1,0:T(8,128)S(1)} %flows.1), channel_id=1, source_target_pairs={{0,12},{4,8},{8,20},{12,16},{16,28},{20,24},{24,4},{28,0},{1,13},{... | collective-permute-start | bytes 12296 | tf_op jit(solution)/shard_map/ppermute | solution.py:571
  16.8 3.6 %collective-permute-start.3 = (f32[8,128]{1,0:T(8,128)S(1)}, f32[8,128]{1,0:T(8,128)S(1)}, u32[]{:S(2)}, u32[]{:S(2)}) collective-permute-start(f32[8,128]{1,0:T(8,128)S(1)} %flows.1), channel_id=1, source_target_pairs={{0,4},{8,12},{16,20},{24,28},{4,0},{12,8},{20,16},{28,24},{1,5},{9... | collective-permute-start | bytes 12296 | tf_op jit(solution)/shard_map/ppermute | solution.py:552
  17.3 5.0 %collective-permute-start.8 = (f32[192,128]{1,0:T(8,128)S(1)}, f32[192,128]{1,0:T(8,128)S(1)}, u32[]{:S(2)}, u32[]{:S(2)}) collective-permute-start(f32[192,128]{1,0:T(8,128)S(1)} %anchor_rows.1.own_ref), channel_id=1, source_target_pairs={{0,1},{8,9},{16,17},{24,25},{1,0},{9,8},{17,16},{25,24},{2,3},{10,... | collective-permute-start | bytes 294920 | tf_op jit(solution)/shard_map/ppermute | solution.py:552
  19.0 3.4 %collective-permute-start.9 = (f32[192,128]{1,0:T(8,128)S(1)}, f32[192,128]{1,0:T(8,128)S(1)}, u32[]{:S(2)}, u32[]{:S(2)}) collective-permute-start(f32[192,128]{1,0:T(8,128)S(1)} %anchor_rows.1.own_ref), channel_id=1, source_target_pairs={{0,8},{8,0},{16,24},{24,16},{1,2},{9,10},{17,18},{25,26},{2,1},{10... | collective-permute-start | bytes 294920 | tf_op jit(solution)/shard_map/ppermute | solution.py:552
  20.5 3.7 %copy-start.7 = (bf16[144,384]{1,0:T(8,128)(2,1)S(1)}, bf16[144,384]{1,0:T(8,128)(2,1)}, u32[]{:S(2)}) copy-start(bf16[144,384]{1,0:T(8,128)(2,1)} %constant.28.clone.right_ref) | copy-start | bytes 331780
  20.5 3.7 %copy-start.8 = (bf16[192,144]{1,0:T(8,128)(2,1)S(1)}, bf16[192,144]{1,0:T(8,128)(2,1)}, u32[]{:S(2)}) copy-start(bf16[192,144]{1,0:T(8,128)(2,1)} %constant.27.clone.left_ref) | copy-start | bytes 165892
  20.5 3.7 %copy-start.9 = (bf16[384,128]{1,0:T(8,128)(2,1)S(1)}, bf16[384,128]{1,0:T(8,128)(2,1)}, u32[]{:S(2)}) copy-start(bf16[384,128]{1,0:T(8,128)(2,1)} %constant.29.clone.cols_table_ref) | copy-start | bytes 294916
  20.5 3.7 %copy-start.10 = (bf16[192,128]{1,0:T(8,128)(2,1)S(1)}, bf16[192,128]{1,0:T(8,128)(2,1)}, u32[]{:S(2)}) copy-start(bf16[192,128]{1,0:T(8,128)(2,1)} %constant.30.clone.rows_table_ref) | copy-start | bytes 147460
  20.5 3.7 %collective-permute-start.6 = (f32[8,128]{1,0:T(8,128)S(1)}, f32[8,128]{1,0:T(8,128)S(1)}, u32[]{:S(2)}, u32[]{:S(2)}) collective-permute-start(f32[8,128]{1,0:T(8,128)S(1)} %maximum_maximum_fusion.own_ref), channel_id=1, source_target_pairs={{0,1},{8,9},{16,17},{24,25},{1,0},{9,8},{17,16},{25,24},{2,3},{10,... | collective-permute-start | bytes 12296 | tf_op jit(solution)/shard_map/ppermute | solution.py:552
  22.4 1.9 %collective-permute-start.7 = (f32[8,128]{1,0:T(8,128)S(1)}, f32[8,128]{1,0:T(8,128)S(1)}, u32[]{:S(2)}, u32[]{:S(2)}) collective-permute-start(f32[8,128]{1,0:T(8,128)S(1)} %maximum_maximum_fusion.own_ref), channel_id=1, source_target_pairs={{0,8},{8,0},{16,24},{24,16},{1,2},{9,10},{17,18},{25,26},{2,1},{10... | collective-permute-start | bytes 12296 | tf_op jit(solution)/shard_map/ppermute | solution.py:552
  24.2 5.7 %copy-start.6 = (bf16[384,256]{1,0:T(8,128)(2,1)S(1)}, bf16[384,256]{1,0:T(8,128)(2,1)}, u32[]{:S(2)}) copy-start(bf16[384,256]{1,0:T(8,128)(2,1)} %constant.31.clone.table_ref) | copy-start | bytes 589828
  27.9 3.0 %collective-permute-start.10 = (f32[8,128]{1,0:T(8,128)S(1)}, f32[8,128]{1,0:T(8,128)S(1)}, u32[]{:S(2)}, u32[]{:S(2)}) collective-permute-start(f32[8,128]{1,0:T(8,128)S(1)} %get-tuple-element.34.refs_0_), channel_id=1, source_target_pairs={{0,8},{8,0},{16,24},{24,16},{1,9},{9,1},{17,25},{25,17},{2,10},{10... | collective-permute-start | bytes 12296 | tf_op jit(solution)/shard_map/ppermute | solution.py:611
  28.0 3.7 %collective-permute-start.11 = (f32[8,128]{1,0:T(8,128)S(1)}, f32[8,128]{1,0:T(8,128)S(1)}, u32[]{:S(2)}, u32[]{:S(2)}) collective-permute-start(f32[8,128]{1,0:T(8,128)S(1)} %get-tuple-element.34.refs_0_), channel_id=1, source_target_pairs={{0,16},{8,24},{16,0},{24,8},{1,17},{9,25},{17,1},{25,9},{2,18},{10... | collective-permute-start | bytes 12296 | tf_op jit(solution)/shard_map/ppermute | solution.py:611
  29.9 3.0 %collective-permute-start.12 = (f32[8,128]{1,0:T(8,128)S(1)}, f32[8,128]{1,0:T(8,128)S(1)}, u32[]{:S(2)}, u32[]{:S(2)}) collective-permute-start(f32[8,128]{1,0:T(8,128)S(1)} %get-tuple-element.34.refs_0_), channel_id=1, source_target_pairs={{0,24},{8,16},{16,8},{24,0},{1,25},{9,17},{17,9},{25,1},{2,26},{10... | collective-permute-start | bytes 12296 | tf_op jit(solution)/shard_map/ppermute | solution.py:611
